TPU v7x, 32 devices: a whole 2x2x4 slice. The times are simulated.
32 devices in a mesh: ctx: 8 (over z, y), head: 4 (over x, core).
Axes of the slice: x: 2, y: 2, z: 4, core: 2. Of those that a mesh axis runs over, the one named last changes fastest.
Arguments:
- entries: bfloat16 [16384, 2048], P('ctx', 'head'), may hold values from -6 to 6
- gating: bfloat16 [16384, 2048], P('ctx', 'head'), may hold values from -6 to 6
- state_in: bfloat16 [16384, 128], P('ctx'), may hold values from -2 to 2
- state_out: bfloat16 [16384, 128], P('ctx'), may hold values from -2 to 2
- step_size: float32 [32, 16384], P('head', 'ctx'), may hold values from 0.2 to 1.5
- decay_rate: float32 [32], P('head'), may hold values from 6.1035157e-06 to 0.1
- skip_gain: float32 [32], P('head'), may hold values from 0.5 to 1.5
- level_gate: float32 [32, 5, 16384], P('head', None, 'ctx'), may hold values from 0.2 to 1.5
- norm_gain: float32 [2048], P('head'), may hold values from 0.5 to 1.5
- cotangent: bfloat16 [16384, 2048], P('ctx'), may hold values from -0.119628906 to 0.119628906
- master_weight: float32 [2048, 2048], P('ctx', 'head'), may hold values from -0.125 to 0.125
- first_moment: float32 [2048, 2048], P('ctx', 'head'), may hold values from -3 to 3
- second_moment: float32 [2048, 2048], P('ctx', 'head'), may hold values from 0.1 to 10
Outputs:
- normed: bfloat16 [16384, 2048], P('ctx', 'head')
- weights: bfloat16 [2048, 2048], P(None, 'head')
- gradient: float32 [2048, 2048], P('ctx', 'head')
All inputs are finite; a program needn't handle non-finite values.
Results may differ from a plain program's by a relative error of at most 0.0059.
Values may be sent and summed in bfloat16 or wider, within the bound.
No kernel may reach another device: no remote copies, remote signals or barrier semaphores. Data moves between devices by JAX's collectives and lax.ppermute only.
A program may use at most 128 MiB of HBM per device.

v0:
```python
import jax
import jax.numpy as jnp
from jax import lax
from jax.sharding import PartitionSpec as P

HEAD_DIM = 64
BLOCK = 256
INNER = 2048


def swapped(block, axis, apart):
    count = lax.axis_size(axis)
    route = []
    for low in range(count):
        high = low | 1 << apart
        if high != low and high < count:
            route += [(low, high), (high, low)]
    return lax.ppermute(block, axis, route)


def block_scan(scaled, state_in, state_out, log_decay):
    length, head_count, head_width = scaled.shape
    state_width = state_in.shape[1]
    blocks = length // BLOCK
    decay_blocks = log_decay.reshape(head_count, blocks, BLOCK).transpose(1, 0, 2)
    value_blocks = scaled.reshape(blocks, BLOCK, head_count, head_width)
    in_blocks = state_in.reshape(blocks, BLOCK, state_width)
    out_blocks = state_out.reshape(blocks, BLOCK, state_width)
    causal = jnp.arange(BLOCK)[:, None] >= jnp.arange(BLOCK)[None, :]

    def advance(running, pieces):
        decays, value_block, in_block, out_block = pieces
        prefix = jnp.cumsum(decays, axis=-1)
        scores = jnp.dot(out_block, in_block.T, preferred_element_type=jnp.float32)
        gap_matrix = jnp.where(causal[None], prefix[:, :, None] - prefix[:, None, :], 0.0)
        decay_mask = jnp.where(causal[None], jnp.exp(gap_matrix), 0.0)
        mix = (scores[None] * decay_mask).astype(jnp.bfloat16)
        within = jnp.einsum("hts,shp->thp", mix, value_block, preferred_element_type=jnp.float32)
        carried = jnp.einsum(
            "tn,hpn->thp",
            out_block,
            running.astype(jnp.bfloat16),
            preferred_element_type=jnp.float32,
        )
        carried = carried * jnp.exp(prefix).T[:, :, None]
        to_end = (
            value_block.astype(jnp.float32) * jnp.exp(prefix[:, -1:] - prefix).T[:, :, None]
        ).astype(jnp.bfloat16)
        update = jnp.einsum("thp,tn->hpn", to_end, in_block, preferred_element_type=jnp.float32)
        running = jnp.exp(prefix[:, -1])[:, None, None] * running + update
        return (running, (within + carried, prefix))

    start = jnp.zeros((head_count, head_width, state_width), jnp.float32)
    end_state, (outputs, prefixes) = lax.scan(
        advance, start, (decay_blocks, value_blocks, in_blocks, out_blocks)
    )
    totals = prefixes[:, :, -1]
    offsets = jnp.cumsum(totals, axis=0) - totals
    cumulative = (prefixes + offsets[:, :, None]).transpose(1, 0, 2).reshape(head_count, length)
    return (outputs.reshape(length, head_count, head_width), end_state, cumulative)


def finish(within, cumulative, by_head, gating, state_out, gate_rows, skip_gain, levels):
    length, head_count, head_width = within.shape
    across = jnp.zeros_like(within)
    for rung, level_state in enumerate(levels):
        readout = jnp.einsum(
            "tn,hpn->thp",
            state_out,
            level_state.astype(jnp.bfloat16),
            preferred_element_type=jnp.float32,
        )
        across = across + readout * gate_rows[:, rung, :].T[:, :, None]
    mixed = (
        within
        + across * jnp.exp(cumulative).T[:, :, None]
        + skip_gain[None, :, None] * by_head.astype(jnp.float32)
    )
    return mixed.reshape(length, head_count * head_width) * jax.nn.silu(gating.astype(jnp.float32))


def adamw(gradient, master, moment_one, moment_two):
    moment_one = 0.9 * moment_one + 0.1 * gradient
    moment_two = 0.95 * moment_two + 0.05 * gradient * gradient
    ratio = moment_one / (1.0 - 0.9**10) / (jnp.sqrt(moment_two / (1.0 - 0.95**10)) + 1e-08)
    return (master - 0.1 * (ratio + 0.1 * master)).astype(jnp.bfloat16)


def on_device(
    entries,
    gating,
    state_in,
    state_out,
    step_size,
    decay_rate,
    skip_gain,
    level_gate,
    norm_gain,
    cotangent,
    master_weight,
    first_moment,
    second_moment,
):
    length = entries.shape[0]
    head_count = decay_rate.shape[0]
    by_head = entries.reshape(length, head_count, HEAD_DIM)
    log_decay = -decay_rate[:, None] * step_size
    scaled = (by_head.astype(jnp.float32) * step_size.T[:, :, None]).astype(jnp.bfloat16)
    within, end_state, cumulative = block_scan(scaled, state_in, state_out, log_decay)
    decay_sum = cumulative[:, -1]
    position = lax.axis_index("ctx")
    depth = lax.axis_size("ctx").bit_length() - 1
    levels = []
    group_state = end_state
    group_decay = decay_sum
    before = jnp.zeros_like(decay_sum)
    for bit_index in range(depth):
        other_state, other_decay = swapped((group_state, group_decay), "ctx", bit_index)
        is_upper = jnp.bitwise_and(jnp.right_shift(position, bit_index), 1) == 1
        levels.append(jnp.where(is_upper, jnp.exp(before)[:, None, None] * other_state, 0.0))
        group_state = jnp.where(
            is_upper,
            group_state + jnp.exp(group_decay)[:, None, None] * other_state,
            other_state + jnp.exp(other_decay)[:, None, None] * group_state,
        )
        before = jnp.where(is_upper, before + other_decay, before)
        group_decay = group_decay + other_decay
    gated = finish(within, cumulative, by_head, gating, state_out, level_gate, skip_gain, levels)
    square_sums = lax.psum(jnp.sum(gated * gated, axis=1), "head")
    mean_sq = square_sums / INNER
    normed = (gated * lax.rsqrt(mean_sq + 1e-05)[:, None] * norm_gain[None, :]).astype(jnp.bfloat16)
    gradient = lax.psum_scatter(
        lax.dot_general(
            cotangent, normed, (((0,), (0,)), ((), ())), preferred_element_type=jnp.float32
        ),
        "ctx",
        scatter_dimension=0,
        tiled=True,
    )
    updated = adamw(gradient, master_weight, first_moment, second_moment)
    weights = lax.all_gather(updated, "ctx", axis=0, tiled=True)
    return (normed, weights, gradient)


def solution(mesh):
    return jax.shard_map(
        on_device,
        mesh=mesh,
        in_specs=(
            P("ctx", "head"),
            P("ctx", "head"),
            P("ctx", None),
            P("ctx", None),
            P("head", "ctx"),
            P("head"),
            P("head"),
            P("head", None, "ctx"),
            P("head"),
            P("ctx", None),
            P("ctx", "head"),
            P("ctx", "head"),
            P("ctx", "head"),
        ),
        out_specs=(P("ctx", "head"), P(None, "head"), P("ctx", "head")),
        check_vma=False,
    )
```

profile of v0, /device:TPU:0, one launch (start us, length us, event | category | flops | bytes accessed | tf_op | source)
XLA Modules:
  0.0 376.6 jit_solution(9245938444446525012)
XLA Ops:
  7.2 0.7 neg.8
  7.9 4.2 %copy.44 = f32[2048,512]{0,1:T(8,128)} copy(bf16[2048,512]{1,0:T(8,128)(2,1)} %param.15) | data formatting | bytes 6291456 | tf_op jit(solution)/shard_map/convert_element_type | solution.py:108
  12.1 4.2 %copy.61 = f32[64,8,8,256]{3,2,1,0:T(8,128)S(1)} copy(f32[64,8,8,256]{3,1,2,0:T(8,128)} %bitcast.130) | data formatting | bytes 8388608
  17.4 140.9 %while.16 = (s32[]{:T(128)}, f32[8,64,128]{2,1,0:T(8,128)S(1)}, f32[8,256,8,64]{1,0,3,2:T(8,128)}, f32[8,8,256]{2,1,0:T(8,128)S(1)}, f32[8,8,256]{2,1,0:T(8,128)...) while((s32[]{:T(128)}, f32[8,64,128]{2,1,0:T(8,128)S(1)}, ...), condition=%wide.region_3.4_spmd.clone.clone, body=%wide.region_0.3_spmd.clone.clone.sunk | while | flops 154865696 | bytes 6026011 | solution.py:54
  17.4 0.6 reduce-window.16
  18.8 1.1 convolution_add_fusion.2
  19.9 1.0 fusion.82
  21.0 0.7 fusion.83
  22.2 12.7 %dynamic_update_slice.16 = f32[8,256,8,64]{1,0,3,2:T(8,128)} dynamic-update-slice(f32[8,256,8,64]{1,0,3,2:T(8,128)} %get-tuple-element.228, f32[1,256,8,64]{1,0,3,2:T(1,128)S(1)} %copy.63, s32[]{:T(128)S(6)} %copy.70, s32[]{:T(128)} %constant.20.clone.1..sunk, s32[]{:T(128)} %constant.20.clone.1..sunk, s32[]{:T(128)} %constant.20.clone.1..sunk) | dynamic-update-slice | bytes 1048580 | tf_op jit(solution)/shard_map/while/body/jit(dynamic_update_index_in_dim)/dynamic_update_slice | solution.py:54
  35.0 0.6 reduce-window.16
  36.4 1.1 convolution_add_fusion.2
  37.5 1.0 fusion.82
  38.6 0.7 fusion.83
  39.9 12.7 %dynamic_update_slice.16 = f32[8,256,8,64]{1,0,3,2:T(8,128)} dynamic-update-slice(f32[8,256,8,64]{1,0,3,2:T(8,128)} %get-tuple-element.228, f32[1,256,8,64]{1,0,3,2:T(1,128)S(1)} %copy.63, s32[]{:T(128)S(6)} %copy.70, s32[]{:T(128)} %constant.20.clone.1..sunk, s32[]{:T(128)} %constant.20.clone.1..sunk, s32[]{:T(128)} %constant.20.clone.1..sunk) | dynamic-update-slice | bytes 1048580 | tf_op jit(solution)/shard_map/while/body/jit(dynamic_update_index_in_dim)/dynamic_update_slice | solution.py:54
  52.7 0.6 reduce-window.16
  54.0 1.1 convolution_add_fusion.2
  55.1 1.0 fusion.82
  56.2 0.7 fusion.83
  57.5 12.7 %dynamic_update_slice.16 = f32[8,256,8,64]{1,0,3,2:T(8,128)} dynamic-update-slice(f32[8,256,8,64]{1,0,3,2:T(8,128)} %get-tuple-element.228, f32[1,256,8,64]{1,0,3,2:T(1,128)S(1)} %copy.63, s32[]{:T(128)S(6)} %copy.70, s32[]{:T(128)} %constant.20.clone.1..sunk, s32[]{:T(128)} %constant.20.clone.1..sunk, s32[]{:T(128)} %constant.20.clone.1..sunk) | dynamic-update-slice | bytes 1048580 | tf_op jit(solution)/shard_map/while/body/jit(dynamic_update_index_in_dim)/dynamic_update_slice | solution.py:54
  70.3 0.6 reduce-window.16
  71.6 1.1 convolution_add_fusion.2
  72.7 1.0 fusion.82
  73.8 0.7 fusion.83
  75.1 12.7 %dynamic_update_slice.16 = f32[8,256,8,64]{1,0,3,2:T(8,128)} dynamic-update-slice(f32[8,256,8,64]{1,0,3,2:T(8,128)} %get-tuple-element.228, f32[1,256,8,64]{1,0,3,2:T(1,128)S(1)} %copy.63, s32[]{:T(128)S(6)} %copy.70, s32[]{:T(128)} %constant.20.clone.1..sunk, s32[]{:T(128)} %constant.20.clone.1..sunk, s32[]{:T(128)} %constant.20.clone.1..sunk) | dynamic-update-slice | bytes 1048580 | tf_op jit(solution)/shard_map/while/body/jit(dynamic_update_index_in_dim)/dynamic_update_slice | solution.py:54
  89.3 1.1 convolution_add_fusion.2
  90.4 1.0 fusion.82
  91.4 0.7 fusion.83
  92.7 12.7 %dynamic_update_slice.16 = f32[8,256,8,64]{1,0,3,2:T(8,128)} dynamic-update-slice(f32[8,256,8,64]{1,0,3,2:T(8,128)} %get-tuple-element.228, f32[1,256,8,64]{1,0,3,2:T(1,128)S(1)} %copy.63, s32[]{:T(128)S(6)} %copy.70, s32[]{:T(128)} %constant.20.clone.1..sunk, s32[]{:T(128)} %constant.20.clone.1..sunk, s32[]{:T(128)} %constant.20.clone.1..sunk) | dynamic-update-slice | bytes 1048580 | tf_op jit(solution)/shard_map/while/body/jit(dynamic_update_index_in_dim)/dynamic_update_slice | solution.py:54
  106.9 1.1 convolution_add_fusion.2
  108.0 1.0 fusion.82
  109.0 0.7 fusion.83
  110.3 12.7 %dynamic_update_slice.16 = f32[8,256,8,64]{1,0,3,2:T(8,128)} dynamic-update-slice(f32[8,256,8,64]{1,0,3,2:T(8,128)} %get-tuple-element.228, f32[1,256,8,64]{1,0,3,2:T(1,128)S(1)} %copy.63, s32[]{:T(128)S(6)} %copy.70, s32[]{:T(128)} %constant.20.clone.1..sunk, s32[]{:T(128)} %constant.20.clone.1..sunk, s32[]{:T(128)} %constant.20.clone.1..sunk) | dynamic-update-slice | bytes 1048580 | tf_op jit(solution)/shard_map/while/body/jit(dynamic_update_index_in_dim)/dynamic_update_slice | solution.py:54
  124.5 1.1 convolution_add_fusion.2
  125.6 1.0 fusion.82
  126.7 0.7 fusion.83
  127.9 12.7 %dynamic_update_slice.16 = f32[8,256,8,64]{1,0,3,2:T(8,128)} dynamic-update-slice(f32[8,256,8,64]{1,0,3,2:T(8,128)} %get-tuple-element.228, f32[1,256,8,64]{1,0,3,2:T(1,128)S(1)} %copy.63, s32[]{:T(128)S(6)} %copy.70, s32[]{:T(128)} %constant.20.clone.1..sunk, s32[]{:T(128)} %constant.20.clone.1..sunk, s32[]{:T(128)} %constant.20.clone.1..sunk) | dynamic-update-slice | bytes 1048580 | tf_op jit(solution)/shard_map/while/body/jit(dynamic_update_index_in_dim)/dynamic_update_slice | solution.py:54
  142.1 1.1 convolution_add_fusion.2
  143.2 1.0 fusion.82
  144.3 0.7 fusion.83
  145.6 12.7 %dynamic_update_slice.16 = f32[8,256,8,64]{1,0,3,2:T(8,128)} dynamic-update-slice(f32[8,256,8,64]{1,0,3,2:T(8,128)} %get-tuple-element.228, f32[1,256,8,64]{1,0,3,2:T(1,128)S(1)} %copy.63, s32[]{:T(128)S(6)} %copy.70, s32[]{:T(128)} %constant.20.clone.1..sunk, s32[]{:T(128)} %constant.20.clone.1..sunk, s32[]{:T(128)} %constant.20.clone.1..sunk) | dynamic-update-slice | bytes 1048580 | tf_op jit(solution)/shard_map/while/body/jit(dynamic_update_index_in_dim)/dynamic_update_slice | solution.py:54
  158.4 3.0 collective-permute-start
  162.2 4.9 %reshape.125 = f32[2048,8,64]{0,2,1:T(8,128)} reshape(f32[8,256,8,64]{1,0,3,2:T(8,128)} %get-tuple-element.55) | data formatting | bytes 8388608 | tf_op jit(solution)/shard_map/reshape | solution.py:60
  167.1 0.6 collective-permute-done.1
  167.7 1.8 collective-permute-start.3
  169.5 1.7 collective-permute-done.3
  171.4 1.9 collective-permute-start.2
  173.3 0.7 fusion.50
  174.0 3.9 %collective-permute-done.2 = f32[8,64,128]{2,1,0:T(8,128)S(1)} collective-permute-done((f32[8,64,128]{2,1,0:T(8,128)S(1)}, f32[8,64,128]{2,1,0:T(8,128)S(1)}, u32[]{:S(2)}, u32[]{:S(2)}) %collective-permute-start.2) | collective-permute-done | bytes 262176 | tf_op jit(solution)/shard_map/ppermute | solution.py:18
  178.0 3.4 collective-permute-start.4
  181.4 0.7 fusion.48
  182.1 7.6 %collective-permute-done.4 = f32[8,64,128]{2,1,0:T(8,128)S(1)} collective-permute-done((f32[8,64,128]{2,1,0:T(8,128)S(1)}, f32[8,64,128]{2,1,0:T(8,128)S(1)}, u32[]{:S(2)}, u32[]{:S(2)}) %collective-permute-start.4) | collective-permute-done | bytes 262176 | tf_op jit(solution)/shard_map/ppermute | solution.py:18
  189.7 3.7 fusion.39
  193.4 5.5 %copy.50 = f32[2048,512]{1,0:T(8,128)} copy(f32[2048,512]{0,1:T(8,128)} %bitcast.132) | data formatting | bytes 8388608 | tf_op jit(solution)/shard_map/reshape | solution.py:79
  198.9 3.5 multiply_reduce_fusion
  202.4 5.9 %psum.7 = f32[2048]{0:T(1024)S(1)} all-reduce(f32[2048]{0:T(1024)S(1)} %multiply_reduce_fusion), channel_id=1, replica_groups=mesh['ctx'=8,'head'=4] {'head'}, use_global_device_ids=true, to_apply=%region_6.7 | all-reduce | flops 2048 | bytes 16384 | tf_op jit(solution)/shard_map/psum | solution.py:129
  208.4 3.1 multiply_convert_fusion.3
  211.5 1.3 copy-done.4
  212.8 9.4 %convolution_bitcast_fusion.1 = f32[2048,512]{0,1:T(8,128)} fusion(bf16[2048,512]{1,0:T(8,128)(2,1)S(1)} %multiply_convert_fusion.3, bf16[2048,2048]{1,0:T(8,128)(2,1)} %param.24), kind=kOutput, calls=%fused_computation.61 | convolution fusion | flops 4294967296 | bytes 14680064 | tf_op jit(solution)/shard_map/dot_general | solution.py:133
  222.3 1.0 copy-done.5
  223.9 88.2 %reduce-scatter.2.cloned.1.call-done = f32[256,512]{0,1:T(8,128)} async-done(((f32[2048,512]{0,1:T(8,128)}), f32[256,512]{0,1:T(8,128)}) %reduce-scatter.2.cloned.1.call-update) | async-done | bytes 524304 | tf_op jit(solution)/shard_map/reduce_scatter | solution.py:132
  312.2 2.2 subtract_convert_fusion
  314.4 2.0 copy.56
  316.4 49.4 %all-gather.2.cloned.1.call-done = bf16[2048,512]{0,1:T(8,128)(2,1)} async-done(((bf16[256,512]{0,1:T(8,128)(2,1)}), bf16[2048,512]{0,1:T(8,128)(2,1)}) %all-gather.2.cloned.1.call-update) | async-done | bytes 2097168 | tf_op jit(solution)/shard_map/all_gather | solution.py:141
  365.9 3.9 %copy.55 = bf16[2048,512]{1,0:T(8,128)(2,1)} copy(bf16[2048,512]{0,1:T(8,128)(2,1)} %all-gather.2.cloned.1.call-done) | data formatting | bytes 4194304
  (151 shorter events, 16.6 us)
Async XLA Ops:
  7.2 305.0 %reduce-scatter.2.cloned.1.call-start = ((), (), s32[]{:S(2)}) async-start(), calls=%async_computation.1 | async-start | bytes 4718592 | tf_op jit(solution)/shard_map/reduce_scatter | solution.py:132
  12.1 4.2 %copy-start.8 = (f32[8,2048]{1,0:T(8,128)S(1)}, f32[8,2048]{1,0:T(8,128)}, u32[]{:S(2)}) copy-start(f32[8,2048]{1,0:T(8,128)} %param.19) | copy-start | bytes 196612
  16.4 1.0 copy-start.2
  158.4 12.9 %collective-permute-start = (f32[8,64,128]{2,1,0:T(8,128)S(1)}, f32[8,64,128]{2,1,0:T(8,128)S(1)}, u32[]{:S(2)}, u32[]{:S(2)}) collective-permute-start(f32[8,64,128]{2,1,0:T(8,128)S(1)} %get-tuple-element.56), channel_id=1, source_target_pairs={{0,4},{4,0},{8,12},{12,8},{16,20},{20,16},{24,28},{28,24},{1,5},{5... | collective-permute-start | bytes 786440 | tf_op jit(solution)/shard_map/ppermute | solution.py:18
  162.1 5.6 %collective-permute-start.1 = (f32[8]{0:T(128)S(1)}, f32[8]{0:T(128)S(1)}, u32[]{:S(2)}, u32[]{:S(2)}) collective-permute-start(f32[8]{0:T(128)S(1)} %slice_reduce_fusion.2), channel_id=1, source_target_pairs={{0,4},{4,0},{8,12},{12,8},{16,20},{20,16},{24,28},{28,24},{1,5},{5... | collective-permute-start | bytes 104 | tf_op jit(solution)/shard_map/ppermute | solution.py:18
  162.2 4.9 %copy-start.9 = (f32[8,5,2048]{2,0,1:T(8,128)S(1)}, f32[8,5,2048]{2,0,1:T(8,128)}, u32[]{:S(2)}) copy-start(f32[8,5,2048]{2,0,1:T(8,128)} %param.22) | copy-start | bytes 983044
  167.7 3.5 collective-permute-start.3
  171.4 18.3 %copy-start = (f32[2048,512]{0,1:T(8,128)S(1)}, f32[2048,512]{0,1:T(8,128)}, u32[]{:S(2)}) copy-start(f32[2048,512]{0,1:T(8,128)} %copy.44) | copy-start | bytes 12582916
  171.4 18.3 %copy-start.1 = (f32[2048,8,64]{0,2,1:T(8,128)S(1)}, f32[2048,8,64]{0,2,1:T(8,128)}, u32[]{:S(2)}) copy-start(f32[2048,8,64]{0,2,1:T(8,128)} %reshape.125) | copy-start | bytes 12582916
  171.4 18.3 %copy-start.11 = (f32[8]{0:T(128)S(1)}, f32[8]{0:T(128)}, u32[]{:S(2)}) copy-start(f32[8]{0:T(128)} %param.21) | copy-start | bytes 100
  171.4 6.4 %collective-permute-start.2 = (f32[8,64,128]{2,1,0:T(8,128)S(1)}, f32[8,64,128]{2,1,0:T(8,128)S(1)}, u32[]{:S(2)}, u32[]{:S(2)}) collective-permute-start(f32[8,64,128]{2,1,0:T(8,128)S(1)} %add_select_fusion.1), channel_id=1, source_target_pairs={{0,8},{8,0},{4,12},{12,4},{16,24},{24,16},{20,28},{28,20},{1,9},{9... | collective-permute-start | bytes 786440 | tf_op jit(solution)/shard_map/ppermute | solution.py:18
  178.0 11.7 %collective-permute-start.4 = (f32[8,64,128]{2,1,0:T(8,128)S(1)}, f32[8,64,128]{2,1,0:T(8,128)S(1)}, u32[]{:S(2)}, u32[]{:S(2)}) collective-permute-start(f32[8,64,128]{2,1,0:T(8,128)S(1)} %add_select_fusion), channel_id=1, source_target_pairs={{0,16},{16,0},{4,20},{20,4},{8,24},{24,8},{12,28},{28,12},{1,17},{... | collective-permute-start | bytes 786440 | tf_op jit(solution)/shard_map/ppermute | solution.py:18
  193.4 5.5 %copy-start.3 = (bf16[2048,512]{1,0:T(8,128)(2,1)S(1)}, bf16[2048,512]{1,0:T(8,128)(2,1)}, u32[]{:S(2)}) copy-start(bf16[2048,512]{1,0:T(8,128)(2,1)} %param.16) | copy-start | bytes 6291460
  198.9 9.5 %copy-start.10 = (f32[512]{0:T(512)S(1)}, f32[512]{0:T(512)}, u32[]{:S(2)}) copy-start(f32[512]{0:T(512)} %param.23) | copy-start | bytes 6148
  211.5 1.3 copy-start.4
  222.3 1.0 copy-start.5
  222.3 1.2 copy-start.6
  222.3 1.5 copy-start.7
  222.3 143.6 %all-gather.2.cloned.1.call-start = ((), (), s32[]{:S(2)}) async-start(), calls=%async_computation.2 | async-start | bytes 2359296 | tf_op jit(solution)/shard_map/all_gather | solution.py:141
Sparse Core Ops, SparseCore 0:
  222.4 89.7 reduce-scatter.1
  315.0 50.8 all-gather.1
where the time goes:
time: 380 us; the launch traced here: 377 us
  waiting for transfers between devices  151 us (40%)
  local copies, waits for them, and re-layouts  138 us (36%)
  matrix products  39.3 us (10%)
  other arithmetic  17.1 us (5%)
  between operations  14.3 us (4%)
  starting transfers between devices  10.2 us (3%)
  blocking collectives  5.95 us (2%)
    dynamic_update_slice x16, local copies, waits for them, and re-layouts, block_scan(): lax.scan(advance, start, (decay_blocks, value_blocks, in_blocks, out_bloc...  106 us
    reduce_scatter x1, waiting for transfers between devices, on_device(): lax.psum_scatter(lax.dot_general(cotangent, normed, (((0,), (0,)), ((), (...  88.2 us
    all_gather x1, waiting for transfers between devices, on_device(): weights = lax.all_gather(updated, 'ctx', axis=0, tiled=True)  49.4 us
    ppermute x5, waiting for transfers between devices, swapped(): return lax.ppermute(block, axis, route)  13.7 us
    unnamed x31, local copies, waits for them, and re-layouts  13.7 us
    ppermute x5, starting transfers between devices, swapped(): return lax.ppermute(block, axis, route)  10.1 us
    dot_general x1, matrix products, on_device(): lax.dot_general(cotangent, normed, (((0,), (0,)), ((), ())), preferred_el...  9.43 us
    dot_general x8, matrix products, advance(): jnp.einsum('thp,tn->hpn', to_end, in_block, preferred_element_type=jnp.fl...  8.72 us
  transfers between devices with their start and end apart: 7, of which 6 were waited for; matrix products, arithmetic and copies ran while one was open for 3% of the time, Pallas kernels for 0%

commit v1 on v0

v1 whole, which is shorter than its diff:
```python
import functools

import jax
import jax.numpy as jnp
from jax import lax
from jax.experimental import pallas as pl
from jax.experimental.pallas import tpu as pltpu
from jax.sharding import PartitionSpec as P

HEAD_DIM = 64
BLOCK = 256
BF16 = jnp.bfloat16
F32 = jnp.float32
VMEM_LIMIT = 48 * 1024 * 1024
TRANSPOSED_LHS = (((0,), (0,)), ((), ()))
TRANSPOSED_RHS = (((1,), (1,)), ((), ()))


def mm(a, b, dims=(((1,), (0,)), ((), ()))):
    return lax.dot_general(a, b, dims, preferred_element_type=F32)


def split(values):
    high = values.astype(BF16)
    return high, (values - high.astype(F32)).astype(BF16)


def params(steps=1):
    return pltpu.CompilerParams(
        dimension_semantics=("arbitrary",) * steps, vmem_limit_bytes=VMEM_LIMIT
    )


def head_select(heads, width):
    lane = lax.broadcasted_iota(jnp.int32, (heads, width), 1)
    row = lax.broadcasted_iota(jnp.int32, (heads, width), 0)
    return lane // (width // heads) == row


def spread_tokens(values, width):
    select = jnp.where(head_select(values.shape[0], width), 1.0, 0.0).astype(BF16)
    high, low = split(values.T)
    return mm(high, select) + mm(low, select)


def spread_row(values, width):
    heads = values.shape[0]
    return jnp.sum(jnp.where(head_select(heads, width), values, 0.0), axis=0, keepdims=True)


def prefix_sum(values):
    tokens = values.shape[1]
    row = lax.broadcasted_iota(jnp.int32, (tokens, tokens), 0)
    col = lax.broadcasted_iota(jnp.int32, (tokens, tokens), 1)
    upper = jnp.where(row <= col, 1.0, 0.0).astype(BF16)
    first, rest = split(values)
    second = (values - first.astype(F32) - rest.astype(F32)).astype(BF16)
    return mm(first, upper) + mm(rest, upper) + mm(second, upper)


def states_kernel(
    x_ref, b_ref, dt_ref, rate_ref, before_ref, prefix_ref, cum_ref, end_ref, decay_ref, pay_ref,
    run_ref, off_ref
):
    step = pl.program_id(0)
    width = x_ref.shape[1]

    @pl.when(step == 0)
    def _():
        run_ref[...] = jnp.zeros_like(run_ref)
        off_ref[...] = jnp.zeros_like(off_ref)

    before_ref[0] = run_ref[...].astype(BF16)
    steps = dt_ref[...]
    prefix = prefix_sum(-rate_ref[...] * steps)
    prefix_ref[...] = prefix
    cum_ref[...] = prefix + off_ref[:, 0:1]
    last = prefix[:, BLOCK - 1:BLOCK]
    weight = spread_tokens(steps * jnp.exp(last - prefix), width)
    scaled = (x_ref[...].astype(F32) * weight).astype(BF16)
    update = mm(b_ref[...], scaled, TRANSPOSED_LHS)
    running = spread_row(jnp.exp(last), width) * run_ref[...] + update
    run_ref[...] = running
    off_ref[...] = off_ref[...] + last

    @pl.when(step == pl.num_programs(0) - 1)
    def _():
        total = spread_row(off_ref[:, 0:1], width)
        end_ref[...] = running
        decay_ref[...] = total
        pack(pay_ref, running, total)


def pack(pay_ref, state, decay):
    rows = state.shape[0]
    first, second = split(decay)
    third = (decay - first.astype(F32) - second.astype(F32)).astype(BF16)
    row = lax.broadcasted_iota(jnp.int32, (16, state.shape[1]), 0)
    tail = jnp.where(
        row == 0,
        first.astype(F32),
        jnp.where(row == 1, second.astype(F32), jnp.where(row == 2, third.astype(F32), 0.0)),
    )
    pay_ref[0:rows] = state.astype(BF16)
    pay_ref[rows:rows + 16] = tail.astype(BF16)


def segment_states(entries, state_in, step_size, rate):
    length, width = entries.shape
    heads = rate.shape[0]
    states = state_in.shape[1]
    blocks = length // BLOCK
    whole = lambda shape: pl.BlockSpec(shape, lambda i: (0,) * len(shape))
    return pl.pallas_call(
        states_kernel,
        grid=(blocks,),
        in_specs=[
            pl.BlockSpec((BLOCK, width), lambda i: (i, 0)),
            pl.BlockSpec((BLOCK, states), lambda i: (i, 0)),
            pl.BlockSpec((heads, BLOCK), lambda i: (0, i)),
            whole((heads, 1)),
        ],
        out_specs=[
            pl.BlockSpec((1, states, width), lambda i: (i, 0, 0)),
            pl.BlockSpec((heads, BLOCK), lambda i: (0, i)),
            pl.BlockSpec((heads, BLOCK), lambda i: (0, i)),
            whole((states, width)),
            whole((1, width)),
            whole((states + 16, width)),
        ],
        out_shape=[
            jax.ShapeDtypeStruct((blocks, states, width), BF16),
            jax.ShapeDtypeStruct((heads, length), F32),
            jax.ShapeDtypeStruct((heads, length), F32),
            jax.ShapeDtypeStruct((states, width), F32),
            jax.ShapeDtypeStruct((1, width), F32),
            jax.ShapeDtypeStruct((states + 16, width), BF16),
        ],
        scratch_shapes=[pltpu.VMEM((states, width), F32), pltpu.VMEM((heads, 128), F32)],
        compiler_params=params(),
        name="segment_states",
    )(entries, state_in, step_size, rate)


def join_kernel(pos_ref, bit, got_ref, group_ref, decay_ref, before_ref,
                level_ref, group_out, decay_out, before_out, pay_ref):
    rows = group_ref.shape[0]
    upper = ((pos_ref[0] >> bit) & 1) == 1
    other = got_ref[0:rows].astype(F32)
    tail = got_ref[rows:rows + 16].astype(F32)
    other_decay = tail[0:1] + tail[1:2] + tail[2:3]
    decay = decay_ref[...]
    before = before_ref[...]
    group = group_ref[...]
    level_ref[...] = jnp.where(upper, jnp.exp(before) * other, 0.0).astype(BF16)
    joined = jnp.where(
        upper, group + jnp.exp(decay) * other, other + jnp.exp(other_decay) * group
    )
    group_out[...] = joined
    total = decay + other_decay
    decay_out[...] = total
    before_out[...] = jnp.where(upper, before + other_decay, before)
    pack(pay_ref, joined, total)


def join(position, bit, got, group, decay, before):
    full = lambda a: pl.BlockSpec(memory_space=pltpu.VMEM)
    row = jax.ShapeDtypeStruct(decay.shape, F32)
    return pl.pallas_call(
        lambda pos_ref, *refs: join_kernel(pos_ref, bit, *refs),
        in_specs=[pl.BlockSpec(memory_space=pltpu.SMEM)] + [full(a) for a in (got, group, decay, before)],
        out_specs=[pl.BlockSpec(memory_space=pltpu.VMEM)] * 5,
        out_shape=[
            jax.ShapeDtypeStruct(group.shape, BF16),
            jax.ShapeDtypeStruct(group.shape, F32),
            row,
            row,
            jax.ShapeDtypeStruct(got.shape, BF16),
        ],
        compiler_params=pltpu.CompilerParams(vmem_limit_bytes=VMEM_LIMIT),
        name="join_groups",
    )(position, got, group, decay, before)


def within_kernel(x_ref, z_ref, b_ref, c_ref, dt_ref, prefix_ref, state_ref, skip_ref, out_ref):
    width = x_ref.shape[1]
    prefix = prefix_ref[...]
    x = x_ref[...].astype(F32)
    weighted = (x * spread_tokens(dt_ref[...] * jnp.exp(-prefix), width)).astype(BF16)
    scores = mm(c_ref[...], b_ref[...], TRANSPOSED_RHS)
    row = lax.broadcasted_iota(jnp.int32, scores.shape, 0)
    col = lax.broadcasted_iota(jnp.int32, scores.shape, 1)
    high, low = split(jnp.where(col <= row, scores, 0.0))
    total = mm(high, weighted) + mm(low, weighted) + mm(c_ref[...], state_ref[0])
    total = total * spread_tokens(jnp.exp(prefix), width) + spread_row(skip_ref[...], width) * x
    z = z_ref[...].astype(F32)
    out_ref[...] = total * (z / (1.0 + jnp.exp(-z)))


def within_blocks(entries, gating, state_in, state_out, step_size, prefix, states, skip):
    length, width = entries.shape
    heads = skip.shape[0]
    state = state_in.shape[1]
    by_rows = lambda cols: pl.BlockSpec((BLOCK, cols), lambda i: (i, 0))
    by_cols = pl.BlockSpec((heads, BLOCK), lambda i: (0, i))
    return pl.pallas_call(
        within_kernel,
        grid=(length // BLOCK,),
        in_specs=[
            by_rows(width),
            by_rows(width),
            by_rows(state),
            by_rows(state),
            by_cols,
            by_cols,
            pl.BlockSpec((1, state, width), lambda i: (i, 0, 0)),
            pl.BlockSpec((heads, 1), lambda i: (0, 0)),
        ],
        out_specs=by_rows(width),
        out_shape=jax.ShapeDtypeStruct((length, width), F32),
        compiler_params=params(),
        name="within_blocks",
    )(entries, gating, state_in, state_out, step_size, prefix, states, skip)


def across_kernel(depth, base_ref, z_ref, c_ref, gate_ref, cum_ref, *refs):
    level_refs, (gated_ref, sums_ref) = refs[:depth], refs[depth:]
    width = base_ref.shape[1]
    decayed = jnp.exp(cum_ref[...])
    total = jnp.zeros(base_ref.shape, F32)
    for rung, level_ref in enumerate(level_refs):
        readout = mm(c_ref[...], level_ref[...])
        total = total + readout * spread_tokens(gate_ref[:, rung, :] * decayed, width)
    z = z_ref[...].astype(F32)
    gated = base_ref[...] + total * (z / (1.0 + jnp.exp(-z)))
    gated_ref[...] = gated
    high, low = split(gated * gated)
    ones = jnp.ones((8, width), BF16)
    sums = mm(ones, high, TRANSPOSED_RHS) + mm(ones, low, TRANSPOSED_RHS)
    sums_ref[...] = sums[0:1]


def across_levels(base, gating, state_out, level_gate, cumulative, levels):
    length, width = base.shape
    heads, rungs = level_gate.shape[:2]
    state = state_out.shape[1]
    by_rows = lambda cols: pl.BlockSpec((BLOCK, cols), lambda i: (i, 0))
    return pl.pallas_call(
        functools.partial(across_kernel, len(levels)),
        grid=(length // BLOCK,),
        in_specs=[
            by_rows(width),
            by_rows(width),
            by_rows(state),
            pl.BlockSpec((heads, rungs, BLOCK), lambda i: (0, 0, i)),
            pl.BlockSpec((heads, BLOCK), lambda i: (0, i)),
        ]
        + [pl.BlockSpec((state, width), lambda i: (0, 0))] * len(levels),
        out_specs=[by_rows(width), pl.BlockSpec((1, BLOCK), lambda i: (0, i))],
        out_shape=[
            jax.ShapeDtypeStruct((length, width), F32),
            jax.ShapeDtypeStruct((1, length), F32),
        ],
        compiler_params=params(),
        name="across_levels",
    )(base, gating, state_out, level_gate, cumulative, *levels)


def gradient_kernel(channels, gated_ref, sums_ref, gain_ref, cot_ref, normed_ref, out_ref, acc_ref):
    step = pl.program_id(0)
    inverse = lax.rsqrt(sums_ref[...] / channels + 1e-05)
    column = jnp.broadcast_to(inverse, (8, inverse.shape[1])).T[:, 0:1]
    normed = (gated_ref[...] * column * gain_ref[...]).astype(BF16)
    normed_ref[...] = normed

    @pl.when(step == 0)
    def _():
        acc_ref[...] = mm(cot_ref[...], normed, TRANSPOSED_LHS)

    @pl.when(step > 0)
    def _():
        acc_ref[...] += mm(cot_ref[...], normed, TRANSPOSED_LHS)

    @pl.when(step == pl.num_programs(0) - 1)
    def _():
        out_ref[...] = acc_ref[...]


def norm_gradient(gated, sums, gain, cotangent, channels):
    length, width = gated.shape
    rows = cotangent.shape[1]
    return pl.pallas_call(
        functools.partial(gradient_kernel, channels),
        grid=(length // BLOCK,),
        in_specs=[
            pl.BlockSpec((BLOCK, width), lambda i: (i, 0)),
            pl.BlockSpec((1, BLOCK), lambda i: (0, i)),
            pl.BlockSpec((1, width), lambda i: (0, 0)),
            pl.BlockSpec((BLOCK, rows), lambda i: (i, 0)),
        ],
        out_specs=[
            pl.BlockSpec((BLOCK, width), lambda i: (i, 0)),
            pl.BlockSpec((rows, width), lambda i: (0, 0)),
        ],
        out_shape=[
            jax.ShapeDtypeStruct((length, width), BF16),
            jax.ShapeDtypeStruct((rows, width), F32),
        ],
        scratch_shapes=[pltpu.VMEM((rows, width), F32)],
        compiler_params=params(),
        name="norm_gradient",
    )(gated, sums, gain, cotangent)


def adamw(gradient, master, moment_one, moment_two):
    moment_one = 0.9 * moment_one + 0.1 * gradient
    moment_two = 0.95 * moment_two + 0.05 * gradient * gradient
    ratio = moment_one / (1.0 - 0.9**10) / (jnp.sqrt(moment_two / (1.0 - 0.95**10)) + 1e-08)
    return (master - 0.1 * (ratio + 0.1 * master)).astype(BF16)


def flipped(block, axis, bit):
    count = lax.axis_size(axis)
    return lax.ppermute(block, axis, [(i, i ^ (1 << bit)) for i in range(count)])


def scatter_sum(terms, position, order):
    depth = len(order)
    left = list(range(depth - 1, -1, -1))
    for bit in order:
        axis = left.index(bit)
        left.pop(axis)
        mine = (position >> bit) & 1
        keep = lax.dynamic_index_in_dim(terms, mine, axis, keepdims=False).astype(F32)
        send = lax.dynamic_index_in_dim(terms, 1 - mine, axis, keepdims=False).astype(BF16)
        terms = keep + flipped(send, "ctx", bit).astype(F32)
    return terms


def gather_blocks(block, position, order):
    have = []
    for bit in reversed(order):
        other = flipped(block, "ctx", bit)
        axis = sum(1 for b in have if b > bit)
        mine = (position >> bit) & 1
        low = jnp.where(mine == 0, block, other)
        high = jnp.where(mine == 0, other, block)
        block = jnp.stack([low, high], axis=axis)
        have.append(bit)
    return block


def on_device(
    entries,
    gating,
    state_in,
    state_out,
    step_size,
    decay_rate,
    skip_gain,
    level_gate,
    norm_gain,
    cotangent,
    master_weight,
    first_moment,
    second_moment,
):
    width = entries.shape[1]
    channels = width * lax.axis_size("head")
    count = lax.axis_size("ctx")
    depth = count.bit_length() - 1
    position = lax.axis_index("ctx")
    rate = decay_rate[:, None]
    before_block, prefix, cumulative, group, decay, payload = segment_states(
        entries, state_in, step_size, rate
    )
    before = jnp.zeros_like(decay)
    where = position.astype(jnp.int32).reshape(1)
    levels = []
    for bit in range(depth):
        got = flipped(payload, "ctx", bit)
        level, group, decay, before, payload = join(where, bit, got, group, decay, before)
        levels.append(level)
    base = within_blocks(
        entries, gating, state_in, state_out, step_size, prefix, before_block, skip_gain[:, None]
    )
    gated, sums = across_levels(base, gating, state_out, level_gate, cumulative, levels)
    sums = jnp.sum(lax.all_gather(sums, "head", axis=0, tiled=False), axis=0)
    normed, terms = norm_gradient(gated, sums, norm_gain[None, :], cotangent, channels)

    rows = master_weight.shape[0]
    chunk = rows // 2
    terms = terms.reshape((2,) * depth + (2, chunk, width))
    bits = list(range(depth))
    orders = [bits, [1, 0] + bits[2:]]
    gradients, updates = [], []
    for half, order in enumerate(orders):
        part = slice(half * chunk, (half + 1) * chunk)
        summed = scatter_sum(terms[..., half, :, :], position, order)
        gradients.append(summed)
        updated = adamw(summed, master_weight[part], first_moment[part], second_moment[part])
        updates.append(gather_blocks(updated, position, order).reshape(count, chunk, width))
    gradient = jnp.concatenate(gradients, axis=0)
    weights = jnp.stack(updates, axis=1).reshape(count * rows, width)
    return (normed, weights, gradient)


def solution(mesh):
    return jax.shard_map(
        on_device,
        mesh=mesh,
        in_specs=(
            P("ctx", "head"),
            P("ctx", "head"),
            P("ctx", None),
            P("ctx", None),
            P("head", "ctx"),
            P("head"),
            P("head"),
            P("head", None, "ctx"),
            P("head"),
            P("ctx", None),
            P("ctx", "head"),
            P("ctx", "head"),
            P("ctx", "head"),
        ),
        out_specs=(P("ctx", "head"), P(None, "head"), P("ctx", "head")),
        check_vma=False,
    )
```

time: 380 us -> 154 us (0.41)
  local copies, waits for them, and re-layouts: 138 us -> 15.1 us
  waiting for transfers between devices: 151 us -> 60.1 us
  Pallas kernels: 0 us -> 45 us
  matrix products: 39.3 us -> 0 us
  between operations: 14.3 us -> 0.97 us
  other arithmetic: 17.1 us -> 5.99 us
  starting transfers between devices: 10.2 us -> 20.4 us
    dynamic_update_slice x16 -> x0, local copies, waits for them, and re-layouts: 106 us -> none  [block_scan(): lax.scan(advance, start, (decay_blocks, value_blocks, in_blocks, out_bloc...]
    reduce_scatter x1 -> x0, waiting for transfers between devices: 88.2 us -> none  [on_device(): lax.psum_scatter(lax.dot_general(cotangent, normed, (((0,), (0,)), ((), (...]
    all_gather x1 -> x0, waiting for transfers between devices: 49.4 us -> none  [on_device(): weights = lax.all_gather(updated, 'ctx', axis=0, tiled=True)]
    ppermute x5 -> x15, waiting for transfers between devices: 13.7 us -> 60.1 us  [flipped(): return lax.ppermute(block, axis, [(i, i ^ 1 << bit) for i in range(count)])]
    pallas_call x0 -> x7, Pallas kernels: none -> 45 us  [the longest x1 12.2 us: norm_gradient(): pl.pallas_call(functools.partial(gradient_kernel, channels), grid=(length...]
    dot_general x36 -> x0, matrix products: 39.3 us -> none  [the longest x1 9.43 us: on_device(): lax.dot_general(cotangent, normed, (((0,), (0,)), ((), ())), preferred_el...]
    reshape x10 -> x0, local copies, waits for them, and re-layouts: 10.4 us -> none  [the longest x1 5.5 us: finish(): mixed.reshape(length, head_count * head_width)]
    ppermute x5 -> x15, starting transfers between devices: 10.1 us -> 20.4 us  [flipped(): return lax.ppermute(block, axis, [(i, i ^ 1 << bit) for i in range(count)])]
  transfers between devices with their start and end apart: 7 -> 15, of which waited for: 6 -> 13; matrix products, arithmetic and copies ran while one was open for 3% -> 4% of each run, Pallas kernels for 0% -> 7%
where the time goes in v1:
time: 154 us; the launch traced here: 153 us
  waiting for transfers between devices  60.1 us (39%)
  Pallas kernels  45 us (29%)
  starting transfers between devices  20.4 us (13%)
  local copies, waits for them, and re-layouts  15.1 us (10%)
  other arithmetic  5.99 us (4%)
  blocking collectives  5.18 us (3%)
    ppermute x15, waiting for transfers between devices, flipped(): return lax.ppermute(block, axis, [(i, i ^ 1 << bit) for i in range(count)])  60.1 us
    ppermute x15, starting transfers between devices, flipped(): return lax.ppermute(block, axis, [(i, i ^ 1 << bit) for i in range(count)])  20.4 us
    pallas_call x1, Pallas kernels, norm_gradient(): pl.pallas_call(functools.partial(gradient_kernel, channels), grid=(length...  12.2 us
    unnamed x47, local copies, waits for them, and re-layouts  11.8 us
    pallas_call x1, Pallas kernels, across_levels(): pl.pallas_call(functools.partial(across_kernel, len(levels)), grid=(lengt...  11 us
    pallas_call x1, Pallas kernels, within_blocks(): pl.pallas_call(within_kernel, grid=(length // BLOCK,), in_specs=[by_rows(...  10.1 us
    pallas_call x1, Pallas kernels, segment_states(): pl.pallas_call(states_kernel, grid=(blocks,), in_specs=[pl.BlockSpec((BLO...  8.25 us
    all_gather x1, blocking collectives, on_device(): sums = jnp.sum(lax.all_gather(sums, 'head', axis=0, tiled=False), axis=0)  5.18 us
  transfers between devices with their start and end apart: 15, of which 13 were waited for; matrix products, arithmetic and copies ran while one was open for 4% of the time, Pallas kernels for 7%

profile of v1, /device:TPU:0, one launch (start us, length us, event | category | flops | bytes accessed | tf_op | source)
XLA Modules:
  0.0 152.8 jit_solution(16484547807874740542)
XLA Ops:
  0.6 0.7 copy.38.rate_ref
  1.4 1.6 %copy-done = bf16[2048,512]{1,0:T(8,128)(2,1)S(1)} copy-done((bf16[2048,512]{1,0:T(8,128)(2,1)S(1)}, bf16[2048,512]{1,0:T(8,128)(2,1)}, u32[]{:S(2)}) %copy-start) | copy-done | bytes 2097176
  3.0 1.0 copy-done.3
  4.0 0.8 copy-done.9
  4.9 8.2 %segment_states.1 = (bf16[8,128,512]{2,1,0:T(8,128)(2,1)S(1)}, f32[8,2048]{1,0:T(8,128)S(1)}, f32[8,2048]{1,0:T(8,128)S(1)}, f32[128,512]{1,0:T(8,128)S(1)}, f32...) custom-call(bf16[2048,512]{1,0:T(8,128)(2,1)S(1)} %copy-done, bf16[2048,128]{1,0:T(8,128)(2,1)S(1)} %copy-done.3, ...), custom_call_target="tpu_custom_call" | custom-call | tf_op jit(solution)/shard_map/segment_states/pallas_call | solution.py:114
  13.1 1.0 copy-done.7
  14.1 0.6 copy-done.15
  14.7 3.0 %collective-permute-start = (bf16[144,512]{1,0:T(8,128)(2,1)}, bf16[144,512]{1,0:T(8,128)(2,1)}, u32[]{:S(2)}, u32[]{:S(2)}) collective-permute-start(bf16[144,512]{1,0:T(8,128)(2,1)} %get-tuple-element.27), channel_id=1, source_target_pairs={{0,4},{4,0},{8,12},{12,8},{16,20},{20,16},{24,28},{28,24},{1,5},{5... | collective-permute-start | bytes 442376 | tf_op jit(solution)/shard_map/ppermute | solution.py:324
  17.7 4.2 %collective-permute-done.refs_0_ = bf16[144,512]{1,0:T(8,128)(2,1)} collective-permute-done((bf16[144,512]{1,0:T(8,128)(2,1)}, bf16[144,512]{1,0:T(8,128)(2,1)}, u32[]{:S(2)}, u32[]{:S(2)}) %collective-permute-start) | collective-permute-done | bytes 147488 | tf_op jit(solution)/shard_map/ppermute | solution.py:324
  21.8 1.0 join_groups.3
  22.9 0.6 copy-done.11
  23.5 1.8 %collective-permute-start.1 = (bf16[144,512]{1,0:T(8,128)(2,1)S(1)}, bf16[144,512]{1,0:T(8,128)(2,1)S(1)}, u32[]{:S(2)}, u32[]{:S(2)}) collective-permute-start(bf16[144,512]{1,0:T(8,128)(2,1)S(1)} %get-tuple-element.31), channel_id=1, source_target_pairs={{0,8},{4,12},{8,0},{12,4},{16,24},{20,28},{24,16},{28,20},{1,9},{5... | collective-permute-start | bytes 442376 | tf_op jit(solution)/shard_map/ppermute | solution.py:324
  25.3 3.3 %collective-permute-done.1.refs_0_ = bf16[144,512]{1,0:T(8,128)(2,1)S(1)} collective-permute-done((bf16[144,512]{1,0:T(8,128)(2,1)S(1)}, bf16[144,512]{1,0:T(8,128)(2,1)S(1)}, u32[]{:S(2)}, u32[]{:S(2)}) %collective-permute-start.1) | collective-permute-done | bytes 147488 | tf_op jit(solution)/shard_map/ppermute | solution.py:324
  28.7 0.8 join_groups.4
  29.4 0.6 copy-done.13
  30.1 2.8 %collective-permute-start.2 = (bf16[144,512]{1,0:T(8,128)(2,1)}, bf16[144,512]{1,0:T(8,128)(2,1)}, u32[]{:S(2)}, u32[]{:S(2)}) collective-permute-start(bf16[144,512]{1,0:T(8,128)(2,1)} %get-tuple-element.36), channel_id=1, source_target_pairs={{0,16},{4,20},{8,24},{12,28},{16,0},{20,4},{24,8},{28,12},{1,17},{... | collective-permute-start | bytes 442376 | tf_op jit(solution)/shard_map/ppermute | solution.py:324
  32.9 0.1 copy.39.skip_ref
  33.0 2.0 %copy.40.gate_ref = f32[8,5,2048]{2,1,0:T(8,128)} copy(f32[8,5,2048]{2,0,1:T(8,128)} %param.20) | data formatting | bytes 655360 | tf_op args[7]
  35.0 1.2 copy-done.8
  36.2 0.8 copy-done.16
  37.1 10.1 %within_blocks.1.base_ref = f32[2048,512]{1,0:T(8,128)} custom-call(bf16[2048,512]{1,0:T(8,128)(2,1)S(1)} %copy-done.1, bf16[2048,512]{1,0:T(8,128)(2,1)} %z_ref.3, bf16[2048,128]{1,0:T(8,128)(2,1)S(1)} %copy-done.4, bf16[2048,128]{1,0:T(8,128)(2,1)S(1)} %copy-done.5, f32[8,2048]{1,0:T(8,128)S(1)} %copy-done.10, f32[8,2048]{1,0:T(8,128)S(1)} %copy-done.16, ...), custom_call_target="tpu_custom_call" | custom-call | tf_op jit(solution)/shard_map/within_blocks/pallas_call | solution.py:206
  47.1 1.7 %join_groups.5 = (bf16[128,512]{1,0:T(8,128)(2,1)S(1)}, f32[128,512]{1,0:T(8,128)}, f32[1,512]{1,0:T(1,128)}, f32[1,512]{1,0:T(1,128)}, bf16[144,512]{1,0:T(8,128)(2,1)}) custom-call(s32[1]{0:T(128)} %bitcast.2.pos_ref, bf16[144,512]{1,0:T(8,128)(2,1)} %collective-permute-done.2.refs_0_, f32[128,512]{1,0:T(8,128)S(1)} %get-tuple-element.37.refs_1_, ...), custom_call_target="tpu_custom_call" | custom-call | tf_op jit(solution)/shard_map/join_groups/pallas_call | solution.py:169
  48.9 11.0 %across_levels.1 = (f32[2048,512]{1,0:T(8,128)}, f32[1,2048]{1,0:T(1,128)S(1)}) custom-call(f32[2048,512]{1,0:T(8,128)} %within_blocks.1.base_ref, bf16[2048,512]{1,0:T(8,128)(2,1)S(1)} %copy-done.2, bf16[2048,128]{1,0:T(8,128)(2,1)S(1)} %copy-done.5, f32[8,5,2048]{2,1,0:T(8,128)S(1)} %copy-done.6, f32[8,2048]{1,0:T(8,128)S(1)} %get-tuple-element.26.cum_ref, ...), custom_call_target="tpu_custom_call" | custom-call | tf_op jit(solution)/shard_map/across_levels/pallas_call | solution.py:248
  59.9 5.2 %all-gather.1 = f32[4,1,2048]{2,1,0:T(1,128)S(1)} all-gather(f32[1,1,2048]{2,1,0:T(1,128)S(1)} %bitcast.70), channel_id=2, replica_groups=mesh['ctx'=8,'head'=4] {'head'}, dimensions={0}, use_global_device_ids=true | all-gather | bytes 40960 | tf_op jit(solution)/shard_map/all_gather | solution.py:388
  65.1 12.2 %norm_gradient.1 = (bf16[2048,512]{1,0:T(8,128)(2,1)}, f32[2048,512]{1,0:T(8,128)S(1)}) custom-call(f32[2048,512]{1,0:T(8,128)} %get-tuple-element.41.gated_ref, f32[1,2048]{1,0:T(1,128)S(1)} %bitcast.69, f32[1,512]{1,0:T(1,128)S(1)} %bitcast.71, bf16[2048,2048]{1,0:T(8,128)(2,1)} %cot_ref.1), custom_call_target="tpu_custom_call" | custom-call | tf_op jit(solution)/shard_map/norm_gradient/pallas_call | solution.py:292
  77.3 0.6 fusion.20
  77.9 1.3 copy-done.18
  79.2 0.1 fusion.3
  79.3 1.6 %collective-permute-start.9 = (bf16[2,2,128,512]{3,2,0,1:T(8,128)(2,1)S(1)}, bf16[2,2,128,512]{3,2,0,1:T(8,128)(2,1)}, u32[]{:S(2)}, u32[]{:S(2)}) collective-permute-start(bf16[2,2,128,512]{3,2,0,1:T(8,128)(2,1)S(1)} %fusion.3), channel_id=1, source_target_pairs={{0,8},{4,12},{8,0},{12,4},{16,24},{20,28},{24,16},{28,20},{1,9},{5... | collective-permute-start | bytes 1572872 | tf_op jit(solution)/shard_map/ppermute | solution.py:324
  81.0 1.6 %collective-permute-start.3 = (bf16[2,2,128,512]{3,2,0,1:T(8,128)(2,1)S(1)}, bf16[2,2,128,512]{3,2,0,1:T(8,128)(2,1)}, u32[]{:S(2)}, u32[]{:S(2)}) collective-permute-start(bf16[2,2,128,512]{3,2,0,1:T(8,128)(2,1)S(1)} %fusion.2), channel_id=1, source_target_pairs={{0,4},{4,0},{8,12},{12,8},{16,20},{20,16},{24,28},{28,24},{1,5},{5... | collective-permute-start | bytes 1572872 | tf_op jit(solution)/shard_map/ppermute | solution.py:324
  82.6 11.0 %collective-permute-done.9 = bf16[2,2,128,512]{3,2,0,1:T(8,128)(2,1)} collective-permute-done((bf16[2,2,128,512]{3,2,0,1:T(8,128)(2,1)S(1)}, bf16[2,2,128,512]{3,2,0,1:T(8,128)(2,1)}, u32[]{:S(2)}, u32[]{:S(2)}) %collective-permute-start.9) | collective-permute-done | bytes 524320 | tf_op jit(solution)/shard_map/ppermute | solution.py:324
  93.6 1.6 %fusion = f32[2,2,128,512]{3,2,0,1:T(8,128)S(1)} fusion(bf16[2,2,128,512]{3,2,0,1:T(8,128)(2,1)} %collective-permute-done.9, f32[2,2,2,1,128,512]{5,4,3,2,1,0:T(8,128)} %copy-done.18, s32[]{:T(128)S(6)} %select_n.97), kind=kLoop, calls=%fused_computation.5 | loop fusion | flops 524288 | bytes 2621444 | tf_op jit(solution)/shard_map/add | solution.py:336
  95.3 1.6 %collective-permute-start.10 = (bf16[2,128,512]{2,1,0:T(8,128)(2,1)S(1)}, bf16[2,128,512]{2,1,0:T(8,128)(2,1)S(1)}, u32[]{:S(2)}, u32[]{:S(2)}) collective-permute-start(bf16[2,128,512]{2,1,0:T(8,128)(2,1)S(1)} %fusion.17), channel_id=1, source_target_pairs={{0,4},{4,0},{8,12},{12,8},{16,20},{20,16},{24,28},{28,24},{1,5},{5... | collective-permute-start | bytes 786440 | tf_op jit(solution)/shard_map/ppermute | solution.py:324
  96.8 1.2 fusion.1
  98.2 1.6 %collective-permute-start.4 = (bf16[2,128,512]{2,1,0:T(8,128)(2,1)S(1)}, bf16[2,128,512]{2,1,0:T(8,128)(2,1)S(1)}, u32[]{:S(2)}, u32[]{:S(2)}) collective-permute-start(bf16[2,128,512]{2,1,0:T(8,128)(2,1)S(1)} %fusion.16), channel_id=1, source_target_pairs={{0,8},{4,12},{8,0},{12,4},{16,24},{20,28},{24,16},{28,20},{1,9},{5... | collective-permute-start | bytes 786440 | tf_op jit(solution)/shard_map/ppermute | solution.py:324
  99.8 3.2 %collective-permute-done.10 = bf16[2,128,512]{2,1,0:T(8,128)(2,1)S(1)} collective-permute-done((bf16[2,128,512]{2,1,0:T(8,128)(2,1)S(1)}, bf16[2,128,512]{2,1,0:T(8,128)(2,1)S(1)}, u32[]{:S(2)}, u32[]{:S(2)}) %collective-permute-start.10) | collective-permute-done | bytes 262176 | tf_op jit(solution)/shard_map/ppermute | solution.py:324
  103.0 0.1 bitcast_add_fusion
  103.2 0.3 collective-permute-start.11
  103.5 3.3 %collective-permute-done.4 = bf16[2,128,512]{2,1,0:T(8,128)(2,1)S(1)} collective-permute-done((bf16[2,128,512]{2,1,0:T(8,128)(2,1)S(1)}, bf16[2,128,512]{2,1,0:T(8,128)(2,1)S(1)}, u32[]{:S(2)}, u32[]{:S(2)}) %collective-permute-start.4) | collective-permute-done | bytes 262176 | tf_op jit(solution)/shard_map/ppermute | solution.py:324
  106.7 0.1 bitcast_add_fusion.1
  106.8 0.1 collective-permute-start.5
  106.9 8.0 %collective-permute-done.11 = bf16[128,512]{1,0:T(8,128)(2,1)S(1)} collective-permute-done((bf16[128,512]{1,0:T(8,128)(2,1)S(1)}, bf16[128,512]{1,0:T(8,128)(2,1)S(1)}, u32[]{:S(2)}, u32[]{:S(2)}) %collective-permute-start.11) | collective-permute-done | bytes 131104 | tf_op jit(solution)/shard_map/ppermute | solution.py:324
  114.9 1.8 %collective-permute-done.5 = bf16[128,512]{1,0:T(8,128)(2,1)} collective-permute-done((bf16[128,512]{1,0:T(8,128)(2,1)S(1)}, bf16[128,512]{1,0:T(8,128)(2,1)}, u32[]{:S(2)}, u32[]{:S(2)}) %collective-permute-start.5) | collective-permute-done | bytes 131104 | tf_op jit(solution)/shard_map/ppermute | solution.py:324
  116.7 1.4 subtract_convert_fusion.1
  118.1 0.1 collective-permute-start.12
  118.2 2.9 %collective-permute-start.6 = (bf16[128,512]{1,0:T(8,128)(2,1)S(1)}, bf16[128,512]{1,0:T(8,128)(2,1)S(1)}, u32[]{:S(2)}, u32[]{:S(2)}) collective-permute-start(bf16[128,512]{1,0:T(8,128)(2,1)S(1)} %get-tuple-element.45), channel_id=1, source_target_pairs={{0,16},{4,20},{8,24},{12,28},{16,0},{20,4},{24,8},{28,12},{1,17},{... | collective-permute-start | bytes 393224 | tf_op jit(solution)/shard_map/ppermute | solution.py:324
  121.1 7.2 %collective-permute-done.12 = bf16[128,512]{1,0:T(8,128)(2,1)S(1)} collective-permute-done((bf16[128,512]{1,0:T(8,128)(2,1)S(1)}, bf16[128,512]{1,0:T(8,128)(2,1)S(1)}, u32[]{:S(2)}, u32[]{:S(2)}) %collective-permute-start.12) | collective-permute-done | bytes 131104 | tf_op jit(solution)/shard_map/ppermute | solution.py:324
  128.3 1.4 collective-permute-start.13
  129.7 0.8 collective-permute-done.6
  130.5 0.1 collective-permute-start.7
  130.6 4.9 %collective-permute-done.13 = bf16[2,128,512]{2,1,0:T(8,128)(2,1)S(1)} collective-permute-done((bf16[2,128,512]{2,1,0:T(8,128)(2,1)S(1)}, bf16[2,128,512]{2,1,0:T(8,128)(2,1)S(1)}, u32[]{:S(2)}, u32[]{:S(2)}) %collective-permute-start.13) | collective-permute-done | bytes 262176 | tf_op jit(solution)/shard_map/ppermute | solution.py:324
  135.6 0.1 collective-permute-start.14
  135.7 4.1 %collective-permute-done.7 = bf16[2,128,512]{2,1,0:T(8,128)(2,1)S(1)} collective-permute-done((bf16[2,128,512]{2,1,0:T(8,128)(2,1)S(1)}, bf16[2,128,512]{2,1,0:T(8,128)(2,1)S(1)}, u32[]{:S(2)}, u32[]{:S(2)}) %collective-permute-start.7) | collective-permute-done | bytes 262176 | tf_op jit(solution)/shard_map/ppermute | solution.py:324
  139.9 1.5 collective-permute-start.8
  141.4 0.8 pad_maximum_fusion.5
  142.2 7.3 %collective-permute-done.14 = bf16[2,2,128,512]{3,2,0,1:T(8,128)(2,1)S(1)} collective-permute-done((bf16[2,2,128,512]{3,2,0,1:T(8,128)(2,1)S(1)}, bf16[2,2,128,512]{3,2,0,1:T(8,128)(2,1)S(1)}, u32[]{:S(2)}, u32[]{:S(2)}) %collective-permute-start.14) | collective-permute-done | bytes 524320 | tf_op jit(solution)/shard_map/ppermute | solution.py:324
  149.5 0.1 select_bitcast_fusion.1
  149.6 0.1 pad_maximum_fusion.2
  149.7 0.1 copy.45
  149.8 1.1 collective-permute-done.8
  150.9 0.1 select_bitcast_fusion.3
  151.0 0.1 pad_maximum_fusion.1
  151.1 0.2 pad_maximum_fusion
  151.3 1.5 %copy.46 = bf16[8,2,128,512]{3,2,1,0:T(8,128)(2,1)} copy(bf16[8,2,128,512]{3,2,0,1:T(8,128)(2,1)S(1)} %pad_maximum_fusion) | data formatting | bytes 4194304 | tf_op jit(solution)/shard_map/stack | solution.py:404
  (53 shorter events, 0.6 us)
Async XLA Ops:
  0.6 32.3 %copy-start.22 = (f32[8]{0:T(128)S(1)}, f32[8]{0:T(128)}, u32[]{:S(2)}) copy-start(f32[8]{0:T(128)} %param.19) | copy-start | bytes 100
  1.4 1.6 %copy-start = (bf16[2048,512]{1,0:T(8,128)(2,1)S(1)}, bf16[2048,512]{1,0:T(8,128)(2,1)}, u32[]{:S(2)}) copy-start(bf16[2048,512]{1,0:T(8,128)(2,1)} %x_ref.3) | copy-start | bytes 6291460
  3.0 1.0 copy-start.3
  4.0 0.8 copy-start.9
  4.8 30.1 %copy-start.1 = (bf16[2048,512]{1,0:T(8,128)(2,1)S(1)}, bf16[2048,512]{1,0:T(8,128)(2,1)}, u32[]{:S(2)}) copy-start(bf16[2048,512]{1,0:T(8,128)(2,1)} %x_ref.3) | copy-start | bytes 6291460
  4.9 30.1 %copy-start.4 = (bf16[2048,128]{1,0:T(8,128)(2,1)S(1)}, bf16[2048,128]{1,0:T(8,128)(2,1)}, u32[]{:S(2)}) copy-start(bf16[2048,128]{1,0:T(8,128)(2,1)} %b_ref.3) | copy-start | bytes 1572868
  4.9 30.1 %copy-start.5 = (bf16[2048,128]{1,0:T(8,128)(2,1)S(1)}, bf16[2048,128]{1,0:T(8,128)(2,1)}, u32[]{:S(2)}) copy-start(bf16[2048,128]{1,0:T(8,128)(2,1)} %c_ref.3) | copy-start | bytes 1572868
  4.9 30.1 %copy-start.10 = (f32[8,2048]{1,0:T(8,128)S(1)}, f32[8,2048]{1,0:T(8,128)}, u32[]{:S(2)}) copy-start(f32[8,2048]{1,0:T(8,128)} %dt_ref.3) | copy-start | bytes 196612
  13.1 1.0 copy-start.7
  14.1 0.6 copy-start.15
  14.7 7.1 %collective-permute-start = (bf16[144,512]{1,0:T(8,128)(2,1)}, bf16[144,512]{1,0:T(8,128)(2,1)}, u32[]{:S(2)}, u32[]{:S(2)}) collective-permute-start(bf16[144,512]{1,0:T(8,128)(2,1)} %get-tuple-element.27), channel_id=1, source_target_pairs={{0,4},{4,0},{8,12},{12,8},{16,20},{20,16},{24,28},{28,24},{1,5},{5... | collective-permute-start | bytes 442376 | tf_op jit(solution)/shard_map/ppermute | solution.py:324
  22.9 0.7 copy-start.11
  23.5 5.1 %collective-permute-start.1 = (bf16[144,512]{1,0:T(8,128)(2,1)S(1)}, bf16[144,512]{1,0:T(8,128)(2,1)S(1)}, u32[]{:S(2)}, u32[]{:S(2)}) collective-permute-start(bf16[144,512]{1,0:T(8,128)(2,1)S(1)} %get-tuple-element.31), channel_id=1, source_target_pairs={{0,8},{4,12},{8,0},{12,4},{16,24},{20,28},{24,16},{28,20},{1,9},{5... | collective-permute-start | bytes 442376 | tf_op jit(solution)/shard_map/ppermute | solution.py:324
  29.4 0.6 copy-start.13
  30.1 17.0 %collective-permute-start.2 = (bf16[144,512]{1,0:T(8,128)(2,1)}, bf16[144,512]{1,0:T(8,128)(2,1)}, u32[]{:S(2)}, u32[]{:S(2)}) collective-permute-start(bf16[144,512]{1,0:T(8,128)(2,1)} %get-tuple-element.36), channel_id=1, source_target_pairs={{0,16},{4,20},{8,24},{12,28},{16,0},{20,4},{24,8},{28,12},{1,17},{... | collective-permute-start | bytes 442376 | tf_op jit(solution)/shard_map/ppermute | solution.py:324
  35.0 1.2 copy-start.8
  36.2 0.8 copy-start.16
  37.0 11.8 %copy-start.2 = (bf16[2048,512]{1,0:T(8,128)(2,1)S(1)}, bf16[2048,512]{1,0:T(8,128)(2,1)}, u32[]{:S(2)}) copy-start(bf16[2048,512]{1,0:T(8,128)(2,1)} %z_ref.3) | copy-start | bytes 6291460
  37.0 11.8 %copy-start.6 = (f32[8,5,2048]{2,1,0:T(8,128)S(1)}, f32[8,5,2048]{2,1,0:T(8,128)}, u32[]{:S(2)}) copy-start(f32[8,5,2048]{2,1,0:T(8,128)} %copy.40.gate_ref) | copy-start | bytes 983044
  37.0 11.8 %copy-start.12 = (bf16[128,512]{1,0:T(8,128)(2,1)S(1)}, bf16[128,512]{1,0:T(8,128)(2,1)}, u32[]{:S(2)}) copy-start(bf16[128,512]{1,0:T(8,128)(2,1)} %copy-done.11) | copy-start | bytes 393220
  37.0 11.8 %copy-start.14 = (bf16[128,512]{1,0:T(8,128)(2,1)S(1)}, bf16[128,512]{1,0:T(8,128)(2,1)}, u32[]{:S(2)}) copy-start(bf16[128,512]{1,0:T(8,128)(2,1)} %copy-done.13) | copy-start | bytes 393220
  48.9 16.2 %copy-start.17 = (f32[512]{0:T(512)S(1)}, f32[512]{0:T(512)}, u32[]{:S(2)}) copy-start(f32[512]{0:T(512)} %param.21) | copy-start | bytes 6148
  77.9 1.3 copy-start.18
  79.3 14.3 %collective-permute-start.9 = (bf16[2,2,128,512]{3,2,0,1:T(8,128)(2,1)S(1)}, bf16[2,2,128,512]{3,2,0,1:T(8,128)(2,1)}, u32[]{:S(2)}, u32[]{:S(2)}) collective-permute-start(bf16[2,2,128,512]{3,2,0,1:T(8,128)(2,1)S(1)} %fusion.3), channel_id=1, source_target_pairs={{0,8},{4,12},{8,0},{12,4},{16,24},{20,28},{24,16},{28,20},{1,9},{5... | collective-permute-start | bytes 1572872 | tf_op jit(solution)/shard_map/ppermute | solution.py:324
  81.0 15.8 %collective-permute-start.3 = (bf16[2,2,128,512]{3,2,0,1:T(8,128)(2,1)S(1)}, bf16[2,2,128,512]{3,2,0,1:T(8,128)(2,1)}, u32[]{:S(2)}, u32[]{:S(2)}) collective-permute-start(bf16[2,2,128,512]{3,2,0,1:T(8,128)(2,1)S(1)} %fusion.2), channel_id=1, source_target_pairs={{0,4},{4,0},{8,12},{12,8},{16,20},{20,16},{24,28},{28,24},{1,5},{5... | collective-permute-start | bytes 1572872 | tf_op jit(solution)/shard_map/ppermute | solution.py:324
  95.3 7.8 %collective-permute-start.10 = (bf16[2,128,512]{2,1,0:T(8,128)(2,1)S(1)}, bf16[2,128,512]{2,1,0:T(8,128)(2,1)S(1)}, u32[]{:S(2)}, u32[]{:S(2)}) collective-permute-start(bf16[2,128,512]{2,1,0:T(8,128)(2,1)S(1)} %fusion.17), channel_id=1, source_target_pairs={{0,4},{4,0},{8,12},{12,8},{16,20},{20,16},{24,28},{28,24},{1,5},{5... | collective-permute-start | bytes 786440 | tf_op jit(solution)/shard_map/ppermute | solution.py:324
  98.1 18.6 %copy-start.19 = (f32[256,512]{1,0:T(8,128)S(1)}, f32[256,512]{1,0:T(8,128)}, u32[]{:S(2)}) copy-start(f32[256,512]{1,0:T(8,128)} %param.25) | copy-start | bytes 1572868
  98.1 18.6 %copy-start.20 = (f32[256,512]{1,0:T(8,128)S(1)}, f32[256,512]{1,0:T(8,128)}, u32[]{:S(2)}) copy-start(f32[256,512]{1,0:T(8,128)} %param.24) | copy-start | bytes 1572868
  98.1 18.6 %copy-start.21 = (f32[256,512]{1,0:T(8,128)S(1)}, f32[256,512]{1,0:T(8,128)}, u32[]{:S(2)}) copy-start(f32[256,512]{1,0:T(8,128)} %param.23) | copy-start | bytes 1572868
  98.2 8.6 %collective-permute-start.4 = (bf16[2,128,512]{2,1,0:T(8,128)(2,1)S(1)}, bf16[2,128,512]{2,1,0:T(8,128)(2,1)S(1)}, u32[]{:S(2)}, u32[]{:S(2)}) collective-permute-start(bf16[2,128,512]{2,1,0:T(8,128)(2,1)S(1)} %fusion.16), channel_id=1, source_target_pairs={{0,8},{4,12},{8,0},{12,4},{16,24},{20,28},{24,16},{28,20},{1,9},{5... | collective-permute-start | bytes 786440 | tf_op jit(solution)/shard_map/ppermute | solution.py:324
  103.2 11.7 %collective-permute-start.11 = (bf16[128,512]{1,0:T(8,128)(2,1)S(1)}, bf16[128,512]{1,0:T(8,128)(2,1)S(1)}, u32[]{:S(2)}, u32[]{:S(2)}) collective-permute-start(bf16[128,512]{1,0:T(8,128)(2,1)S(1)} %fusion.19), channel_id=1, source_target_pairs={{0,16},{4,20},{8,24},{12,28},{16,0},{20,4},{24,8},{28,12},{1,17},{... | collective-permute-start | bytes 393224 | tf_op jit(solution)/shard_map/ppermute | solution.py:324
  106.8 9.9 %collective-permute-start.5 = (bf16[128,512]{1,0:T(8,128)(2,1)S(1)}, bf16[128,512]{1,0:T(8,128)(2,1)}, u32[]{:S(2)}, u32[]{:S(2)}) collective-permute-start(bf16[128,512]{1,0:T(8,128)(2,1)S(1)} %fusion.18), channel_id=1, source_target_pairs={{0,16},{4,20},{8,24},{12,28},{16,0},{20,4},{24,8},{28,12},{1,17},{... | collective-permute-start | bytes 393224 | tf_op jit(solution)/shard_map/ppermute | solution.py:324
  118.1 10.2 %collective-permute-start.12 = (bf16[128,512]{1,0:T(8,128)(2,1)S(1)}, bf16[128,512]{1,0:T(8,128)(2,1)S(1)}, u32[]{:S(2)}, u32[]{:S(2)}) collective-permute-start(bf16[128,512]{1,0:T(8,128)(2,1)S(1)} %get-tuple-element.51), channel_id=1, source_target_pairs={{0,16},{4,20},{8,24},{12,28},{16,0},{20,4},{24,8},{28,12},{1,17},{... | collective-permute-start | bytes 393224 | tf_op jit(solution)/shard_map/ppermute | solution.py:324
  118.2 12.3 %collective-permute-start.6 = (bf16[128,512]{1,0:T(8,128)(2,1)S(1)}, bf16[128,512]{1,0:T(8,128)(2,1)S(1)}, u32[]{:S(2)}, u32[]{:S(2)}) collective-permute-start(bf16[128,512]{1,0:T(8,128)(2,1)S(1)} %get-tuple-element.45), channel_id=1, source_target_pairs={{0,16},{4,20},{8,24},{12,28},{16,0},{20,4},{24,8},{28,12},{1,17},{... | collective-permute-start | bytes 393224 | tf_op jit(solution)/shard_map/ppermute | solution.py:324
  128.3 7.2 %collective-permute-start.13 = (bf16[2,128,512]{2,1,0:T(8,128)(2,1)S(1)}, bf16[2,128,512]{2,1,0:T(8,128)(2,1)S(1)}, u32[]{:S(2)}, u32[]{:S(2)}) collective-permute-start(bf16[2,128,512]{2,1,0:T(8,128)(2,1)S(1)} %pad_maximum_fusion.7), channel_id=1, source_target_pairs={{0,4},{4,0},{8,12},{12,8},{16,20},{20,16},{24,28},{28,24},{1,5},{5... | collective-permute-start | bytes 786440 | tf_op jit(solution)/shard_map/ppermute | solution.py:324
  130.5 9.3 %collective-permute-start.7 = (bf16[2,128,512]{2,1,0:T(8,128)(2,1)S(1)}, bf16[2,128,512]{2,1,0:T(8,128)(2,1)S(1)}, u32[]{:S(2)}, u32[]{:S(2)}) collective-permute-start(bf16[2,128,512]{2,1,0:T(8,128)(2,1)S(1)} %pad_maximum_fusion.6), channel_id=1, source_target_pairs={{0,8},{4,12},{8,0},{12,4},{16,24},{20,28},{24,16},{28,20},{1,9},{5... | collective-permute-start | bytes 786440 | tf_op jit(solution)/shard_map/ppermute | solution.py:324
  135.6 13.9 %collective-permute-start.14 = (bf16[2,2,128,512]{3,2,0,1:T(8,128)(2,1)S(1)}, bf16[2,2,128,512]{3,2,0,1:T(8,128)(2,1)S(1)}, u32[]{:S(2)}, u32[]{:S(2)}) collective-permute-start(bf16[2,2,128,512]{3,2,0,1:T(8,128)(2,1)S(1)} %pad_maximum_fusion.4), channel_id=1, source_target_pairs={{0,8},{4,12},{8,0},{12,4},{16,24},{20,28},{24,16},{28,20},{1,9},{5... | collective-permute-start | bytes 1572872 | tf_op jit(solution)/shard_map/ppermute | solution.py:324
  139.9 11.0 %collective-permute-start.8 = (bf16[2,2,128,512]{3,2,1,0:T(8,128)(2,1)S(1)}, bf16[2,2,128,512]{3,2,1,0:T(8,128)(2,1)S(1)}, u32[]{:S(2)}, u32[]{:S(2)}) collective-permute-start(bf16[2,2,128,512]{3,2,1,0:T(8,128)(2,1)S(1)} %pad_maximum_fusion.3), channel_id=1, source_target_pairs={{0,4},{4,0},{8,12},{12,8},{16,20},{20,16},{24,28},{28,24},{1,5},{5... | collective-permute-start | bytes 1572872 | tf_op jit(solution)/shard_map/ppermute | solution.py:324

commit v2 on v0

v2 whole, which is shorter than its diff:
```python
import functools

import jax
import jax.numpy as jnp
from jax import lax
from jax.experimental import pallas as pl
from jax.experimental.pallas import tpu as pltpu
from jax.sharding import PartitionSpec as P

HEAD_DIM = 64
BLOCK = 256
BF16 = jnp.bfloat16
F32 = jnp.float32
MIB = 1024 * 1024
CUTS = (0, 4, 8)
PARTS = len(CUTS) - 1
TRANSPOSED_LHS = (((0,), (0,)), ((), ()))
TRANSPOSED_RHS = (((1,), (1,)), ((), ()))


def mm(a, b, dims=(((1,), (0,)), ((), ()))):
    return lax.dot_general(a, b, dims, preferred_element_type=F32)


def split(values):
    high = values.astype(BF16)
    return high, (values - high.astype(F32)).astype(BF16)


def params(mib, steps=1):
    return pltpu.CompilerParams(
        dimension_semantics=("arbitrary",) * steps, vmem_limit_bytes=mib * MIB
    )


def in_hbm(*arrays):
    return [pltpu.with_memory_space_constraint(array, pltpu.HBM) for array in arrays]


def in_vmem(*arrays):
    return [pltpu.with_memory_space_constraint(array, pltpu.VMEM) for array in arrays]


def turn_blocks(values):
    blocks = values.shape[1] // BLOCK
    return jnp.concatenate([values[:, i * BLOCK:(i + 1) * BLOCK] for i in range(blocks)], axis=0)


def prefix_sums(values):
    heads, tokens = values.shape
    rows = turn_blocks(values)
    row = lax.broadcasted_iota(jnp.int32, (BLOCK, BLOCK), 0)
    col = lax.broadcasted_iota(jnp.int32, (BLOCK, BLOCK), 1)
    upper = jnp.where(row <= col, 1.0, 0.0).astype(BF16)
    first, rest = split(rows)
    last = (rows - first.astype(F32) - rest.astype(F32)).astype(BF16)
    sums = mm(jnp.concatenate([first, rest, last], axis=0), upper)
    count = rows.shape[0]
    sums = sums[0:count] + sums[count:2 * count] + sums[2 * count:3 * count]
    return [sums[i * heads:(i + 1) * heads] for i in range(tokens // BLOCK)]


def as_column(row):
    heads = row.shape[1]
    diagonal = lax.broadcasted_iota(jnp.int32, (heads, heads), 0) == lax.broadcasted_iota(
        jnp.int32, (heads, heads), 1
    )
    return jnp.sum(jnp.where(diagonal, row, 0.0), axis=1, keepdims=True)


def head_rows(head):
    return slice(head * HEAD_DIM, (head + 1) * HEAD_DIM)


def states_kernel(
    x_ref, b_ref, dt_ref, rate_ref, before_ref, prefix_ref, cum_ref, end_ref, decay_ref, pay_ref,
    run_ref, off_ref
):
    step = pl.program_id(0)
    tokens, width = x_ref.shape
    states = b_ref.shape[1]
    heads = dt_ref.shape[0]

    @pl.when(step == 0)
    def _():
        run_ref[...] = jnp.zeros_like(run_ref)
        off_ref[...] = jnp.zeros_like(off_ref)

    offset = off_ref[:, 0:1]
    rate = as_column(rate_ref[...])
    for block, prefix in enumerate(prefix_sums(-rate * dt_ref[...])):
        part = slice(block * BLOCK, (block + 1) * BLOCK)
        prefix_ref[:, part] = prefix
        cum_ref[:, part] = prefix + offset
        last = prefix[:, BLOCK - 1:BLOCK]
        weight = jnp.exp(last - prefix)
        decay = jnp.broadcast_to(jnp.exp(last), (heads, states))
        steps = dt_ref[:, part]
        turned = x_ref[part].T
        pieces = []
        for head in range(heads):
            x = turned[head_rows(head)].astype(F32)
            scaled = (x * steps[head:head + 1]).astype(BF16).astype(F32)
            pieces.append((scaled * weight[head:head + 1]).astype(BF16))
        update = mm(jnp.concatenate(pieces, axis=0), b_ref[part])
        for head in range(heads):
            rows = head_rows(head)
            running = run_ref[rows]
            before_ref[block, rows] = running.astype(BF16)
            run_ref[rows] = decay[head:head + 1] * running + update[rows]
        offset = offset + last
    off_ref[...] = jnp.broadcast_to(offset, off_ref.shape)

    @pl.when(step == pl.num_programs(0) - 1)
    def _():
        total = jnp.broadcast_to(offset, (heads, states))
        end_ref[...] = run_ref[...]
        decay_ref[...] = total
        pay_ref[0:width] = run_ref[...].astype(BF16)
        first, second = split(total)
        third = (total - first.astype(F32) - second.astype(F32)).astype(BF16)
        terms = [first.astype(F32), second.astype(F32), third.astype(F32)]
        terms += [jnp.zeros_like(total)] * (tail_rows(heads) // heads - 3)
        pay_ref[width:] = jnp.concatenate(terms, axis=0).astype(BF16)


def tail_rows(heads):
    return -(-3 * heads // 16) * 16


def segment_states(entries, state_in, step_size, rate, tile=1024):
    length, width = entries.shape
    heads = rate.shape[1]
    states = state_in.shape[1]
    tile = min(tile, length)
    whole = lambda shape: pl.BlockSpec(shape, lambda i: (0,) * len(shape))
    return pl.pallas_call(
        states_kernel,
        grid=(length // tile,),
        in_specs=[
            pl.BlockSpec((tile, width), lambda i: (i, 0)),
            pl.BlockSpec((tile, states), lambda i: (i, 0)),
            pl.BlockSpec((heads, tile), lambda i: (0, i)),
            whole((1, heads)),
        ],
        out_specs=[
            pl.BlockSpec((tile // BLOCK, width, states), lambda i: (i, 0, 0)),
            pl.BlockSpec((heads, tile), lambda i: (0, i)),
            pl.BlockSpec((heads, tile), lambda i: (0, i)),
            whole((width, states)),
            whole((heads, states)),
            whole((width + tail_rows(heads), states)),
        ],
        out_shape=[
            pltpu.VMEM((length // BLOCK, width, states), BF16),
            pltpu.VMEM((heads, length), F32),
            pltpu.VMEM((heads, length), F32),
            jax.ShapeDtypeStruct((width, states), F32),
            jax.ShapeDtypeStruct((heads, states), F32),
            jax.ShapeDtypeStruct((width + tail_rows(heads), states), BF16),
        ],
        scratch_shapes=[pltpu.VMEM((width, states), F32), pltpu.VMEM((heads, 128), F32)],
        compiler_params=params(24),
        name="segment_states",
    )(*in_hbm(entries, state_in, step_size, rate))


def packed(state, decay):
    heads = decay.shape[0]
    first, second = split(decay)
    third = (decay - first.astype(F32) - second.astype(F32)).astype(BF16)
    spare = jnp.zeros((tail_rows(heads) - 3 * heads, decay.shape[1]), BF16)
    return jnp.concatenate([state.astype(BF16), first, second, third, spare], axis=0)


def unpacked(got, heads):
    width = got.shape[0] - tail_rows(heads)
    terms = got[width:width + 3 * heads].astype(F32).reshape(3, heads, got.shape[1])
    return got[0:width].astype(F32), terms[0] + terms[1] + terms[2]


def decayed(decay, state):
    heads, states = decay.shape
    return (jnp.exp(decay)[:, None, :] * state.reshape(heads, -1, states)).reshape(state.shape)


def joined(upper, state, decay, other, other_decay):
    both = jnp.where(
        upper, state + decayed(decay, other), other + decayed(other_decay, state)
    )
    return both, decay + other_decay


def level_of(upper, before, other, other_decay):
    level = jnp.where(upper, decayed(before, other), 0.0).astype(BF16)
    return level, jnp.where(upper, before + other_decay, before)


def level_states(payload, state, decay, position, depth, beside):
    heads = decay.shape[0]
    uppers = [((position >> bit) & 1) == 1 for bit in range(depth)]
    before = jnp.zeros_like(decay)
    levels = []
    near = min(depth, 2)
    got = [flipped(payload, "ctx", mask) for mask in range(1, 1 << near)]
    *got, beside = lax.optimization_barrier((*got, beside))
    got = [unpacked(each, heads) for each in got]
    for bit in range(depth):
        if bit == 0:
            other, other_decay = got[0]
        elif bit == 1:
            other, other_decay = joined(uppers[0], *got[1], *got[2])
        else:
            other, other_decay = unpacked(flipped(packed(state, decay), "ctx", 1 << bit), heads)
        level, before_next = level_of(uppers[bit], before, other, other_decay)
        levels.append(level)
        state, decay = joined(uppers[bit], state, decay, other, other_decay)
        before = before_next
    return levels, beside


def silu(z):
    return z * (0.5 + 0.5 * jnp.tanh(0.5 * z))


def within_kernel(
    x_ref, z_ref, b_ref, c_ref, dt_ref, prefix_ref, state_ref, skip_ref, base_ref, gating_ref
):
    tokens, width = x_ref.shape
    heads = dt_ref.shape[0]
    skip = jnp.broadcast_to(as_column(skip_ref[...]), (heads, BLOCK))
    row = lax.broadcasted_iota(jnp.int32, (BLOCK, BLOCK), 0)
    col = lax.broadcasted_iota(jnp.int32, (BLOCK, BLOCK), 1)
    for block in range(tokens // BLOCK):
        part = slice(block * BLOCK, (block + 1) * BLOCK)
        prefix = prefix_ref[:, part]
        grow, shrink = jnp.exp(-prefix), jnp.exp(prefix)
        steps = dt_ref[:, part]
        readout = c_ref[part]
        scores = mm(b_ref[part], readout, TRANSPOSED_RHS)
        high, low = split(jnp.where(row <= col, scores, 0.0))
        turned = x_ref[part].T
        highs, lows = [], []
        for head in range(heads):
            x = turned[head_rows(head)].astype(F32)
            scaled = (x * steps[head:head + 1]).astype(BF16).astype(F32)
            weighted, rest = split(scaled * grow[head:head + 1])
            highs.append(weighted)
            lows.append(rest)
        weighted, rest = jnp.concatenate(highs, axis=0), jnp.concatenate(lows, axis=0)
        total = mm(
            jnp.concatenate([weighted, weighted, rest], axis=1),
            jnp.concatenate([high, low, high], axis=0),
        ) + mm(state_ref[block], readout, TRANSPOSED_RHS)
        z_turned = z_ref[part].T
        gating_ref[:, part] = z_turned
        for head in range(heads):
            rows = head_rows(head)
            x = turned[rows].astype(F32)
            mixed = total[rows] * shrink[head:head + 1] + skip[head:head + 1] * x
            base_ref[rows, part] = (mixed * silu(z_turned[rows].astype(F32))).astype(BF16)


def within_blocks(entries, gating, state_in, state_out, step_size, prefix, states, skip, tile=512):
    length, width = entries.shape
    heads = skip.shape[1]
    state = state_in.shape[1]
    tile = min(tile, length)
    by_rows = lambda cols: pl.BlockSpec((tile, cols), lambda i: (i, 0))
    by_cols = lambda rows: pl.BlockSpec((rows, tile), lambda i: (0, i))
    return pl.pallas_call(
        within_kernel,
        grid=(length // tile,),
        in_specs=[
            by_rows(width),
            by_rows(width),
            by_rows(state),
            by_rows(state),
            by_cols(heads),
            by_cols(heads),
            pl.BlockSpec((tile // BLOCK, width, state), lambda i: (i, 0, 0)),
            pl.BlockSpec((1, heads), lambda i: (0, 0)),
        ],
        out_specs=[by_cols(width), by_cols(width)],
        out_shape=[
            pltpu.VMEM((width, length), BF16),
            pltpu.HBM((width, length), BF16),
        ],
        compiler_params=params(24),
        name="within_blocks",
    )(
        *in_hbm(entries, gating, state_in, state_out, step_size),
        *in_vmem(prefix, states),
        *in_hbm(skip),
    )


def across_kernel(depth, base_ref, z_ref, c_ref, gate_ref, cum_ref, *refs):
    level_refs, (gated_ref, sums_ref) = refs[:depth], refs[depth:]
    width, tokens = base_ref.shape
    heads = cum_ref.shape[0]
    per_pair = 128 // HEAD_DIM
    for block in range(tokens // BLOCK):
        part = slice(block * BLOCK, (block + 1) * BLOCK)
        decayed = jnp.exp(cum_ref[:, part])
        gates = [gate_ref[rung, :, part] * decayed for rung in range(depth)]
        readouts = [mm(level_ref[...], c_ref[part], TRANSPOSED_RHS) for level_ref in level_refs]
        squares = jnp.zeros((HEAD_DIM, BLOCK), F32)
        for first in range(0, heads, per_pair):
            pair = []
            for head in range(first, first + per_pair):
                rows = head_rows(head)
                total = jnp.zeros((HEAD_DIM, BLOCK), F32)
                for gate, readout in zip(gates, readouts):
                    total = total + readout[rows] * gate[head:head + 1]
                gated = base_ref[rows, part].astype(F32) + total * silu(z_ref[rows, part].astype(F32))
                squares = squares + gated * gated
                pair.append(gated)
            cols = slice(first * HEAD_DIM, (first + per_pair) * HEAD_DIM)
            gated_ref[part, cols] = jnp.concatenate(pair, axis=0).T.astype(BF16)
        sums_ref[:, part] = jnp.sum(squares, axis=0, keepdims=True)


def across_levels(base, gating, state_out, level_gate, cumulative, levels, tile=512):
    width, length = base.shape
    rungs, heads = level_gate.shape[:2]
    state = state_out.shape[1]
    tile = min(tile, length)
    by_cols = lambda rows: pl.BlockSpec((rows, tile), lambda i: (0, i))
    return pl.pallas_call(
        functools.partial(across_kernel, len(levels)),
        grid=(length // tile,),
        in_specs=[
            by_cols(width),
            by_cols(width),
            pl.BlockSpec((tile, state), lambda i: (i, 0)),
            pl.BlockSpec((rungs, heads, tile), lambda i: (0, 0, i)),
            by_cols(heads),
        ]
        + [pl.BlockSpec((width, state), lambda i: (0, 0))] * len(levels),
        out_specs=[pl.BlockSpec((tile, width), lambda i: (i, 0)), by_cols(1)],
        out_shape=[
            pltpu.VMEM((length, width), BF16),
            jax.ShapeDtypeStruct((1, length), F32),
        ],
        compiler_params=params(24),
        name="across_levels",
    )(
        *in_vmem(base),
        *in_hbm(gating, state_out, level_gate),
        *in_vmem(cumulative),
        *levels,
    )


def normalize(channels, gated_ref, sums_ref, gain_ref, normed_ref):
    for block in range(gated_ref.shape[0] // BLOCK):
        part = slice(block * BLOCK, (block + 1) * BLOCK)
        inverse = lax.rsqrt(jnp.sum(sums_ref[:, part], axis=0, keepdims=True) / channels + 1e-05)
        column = jnp.broadcast_to(inverse, (8, BLOCK)).T[:, 0:1]
        normed_ref[part] = (gated_ref[part].astype(F32) * column * gain_ref[...]).astype(BF16)


def gradient_kernel(channels, gated_ref, sums_ref, gain_ref, cot_ref, normed_ref, out_ref):
    @pl.when(pl.program_id(0) == 0)
    def _():
        normalize(channels, gated_ref, sums_ref, gain_ref, normed_ref)

    out_ref[...] = mm(cot_ref[...], normed_ref[...], TRANSPOSED_LHS)


def norm_gradient(gated, sums, gain, cotangent, channels, tile=512):
    length, width = gated.shape
    rows = cotangent.shape[1]
    whole = lambda shape: pl.BlockSpec(shape, lambda i: (0,) * len(shape))
    return pl.pallas_call(
        functools.partial(gradient_kernel, channels),
        grid=(rows // tile,),
        in_specs=[
            whole((length, width)),
            whole(sums.shape),
            whole((1, width)),
            pl.BlockSpec((length, tile), lambda i: (0, i)),
        ],
        out_specs=[whole((length, width)), pl.BlockSpec((tile, width), lambda i: (i, 0))],
        out_shape=[
            jax.ShapeDtypeStruct((length, width), BF16),
            jax.ShapeDtypeStruct((rows, width), F32),
        ],
        compiler_params=params(32),
        name="norm_gradient",
    )(*in_vmem(gated), sums, gain, *in_hbm(cotangent))


def masks_of(bits):
    masks = [0]
    for bit in reversed(bits):
        masks = masks + [mask | 1 << bit for mask in masks]
    return masks


def column_specs(orders, length, count, chunk, keep):
    def spec(slot):
        def index(half, pos_ref):
            flips = [masks_of(order[1:])[slot] | (0 if keep else 1 << order[0]) for order in orders]
            flip = jnp.where(half == 0, flips[0], flips[1])
            return (0, 2 * (pos_ref[0] ^ flip) + half)

        return pl.BlockSpec((length, chunk), index)

    return [spec(slot) for slot in range(count // 2)]


def part_slices(width):
    edges = [cut * width // 8 for cut in CUTS]
    return [slice(start, stop) for start, stop in zip(edges, edges[1:])]


def store_half(product, out_refs):
    for half in range(2):

        @pl.when(pl.program_id(0) == half)
        def _():
            for part, cols in enumerate(part_slices(product.shape[1])):
                out_ref = out_refs[2 * part + half]
                out_ref[...] = product[:, cols].reshape(out_ref.shape).astype(out_ref.dtype)


def send_kernel(channels, pos_ref, gated_ref, sums_ref, gain_ref, *refs):
    cot_refs, (normed_ref, *out_refs) = refs[:-2 * PARTS - 1], refs[-2 * PARTS - 1:]

    @pl.when(pl.program_id(0) == 0)
    def _():
        normalize(channels, gated_ref, sums_ref, gain_ref, normed_ref)

    columns = jnp.concatenate([ref[...] for ref in cot_refs], axis=1)
    store_half(mm(columns, normed_ref[...], TRANSPOSED_LHS), out_refs)


def keep_kernel(pos_ref, normed_ref, *refs):
    cot_refs, out_refs = refs[:-2 * PARTS], refs[-2 * PARTS:]
    columns = jnp.concatenate([ref[...] for ref in cot_refs], axis=1)
    store_half(mm(columns, normed_ref[...], TRANSPOSED_LHS), out_refs)


def terms_call(kernel, name, position, inputs, cotangent, orders, chunk, keep, outs, dtype):
    length, width = inputs[0].shape
    count = 1 << len(orders[0])
    cots = column_specs(orders, length, count, chunk, keep)
    whole = lambda shape: pl.BlockSpec(shape, lambda i, pos_ref: (0,) * len(shape))
    shapes = [
        (count // 2, chunk, cols.stop - cols.start) for cols in part_slices(width) for _ in range(2)
    ]
    out = pl.pallas_call(
        kernel,
        grid_spec=pltpu.PrefetchScalarGridSpec(
            num_scalar_prefetch=1,
            grid=(2,),
            in_specs=[whole(each.shape) for each in inputs] + cots,
            out_specs=[whole(each.shape) for each in outs] + [whole(shape) for shape in shapes],
        ),
        out_shape=outs + [jax.ShapeDtypeStruct(shape, dtype) for shape in shapes],
        compiler_params=params(32),
        name=name,
    )(position, *inputs, *in_hbm(*[cotangent] * len(cots)))
    terms = out[len(outs):]
    return out[:len(outs)], [terms[2 * part:2 * part + 2] for part in range(PARTS)]


def terms_to_send(position, gated, sums, gain, cotangent, channels, orders, chunk):
    return terms_call(
        functools.partial(send_kernel, channels),
        "terms_to_send",
        position,
        [*in_vmem(gated), sums, gain],
        cotangent,
        orders,
        chunk,
        False,
        [pltpu.HBM(gated.shape, BF16)],
        BF16,
    )


def terms_to_keep(position, normed, cotangent, orders, chunk):
    return terms_call(
        keep_kernel,
        "terms_to_keep",
        position,
        in_hbm(normed),
        cotangent,
        orders,
        chunk,
        True,
        [],
        F32,
    )[1]


def place_kernel(slots, rows, pos_ref, *refs):
    block_refs, (out_ref, sems) = refs[:-2], refs[-2:]
    copies = []
    for block_ref, (masks, half, start) in zip(block_refs, slots):
        _, chunk, width = block_ref.shape
        for slot, mask in enumerate(masks):
            row = pl.multiple_of((pos_ref[0] ^ mask) * rows + half * chunk, chunk)
            target = out_ref.at[pl.ds(row, chunk), pl.ds(start, width)]
            copies.append(
                pltpu.make_async_copy(block_ref.at[slot], target, sems.at[len(copies)])
            )
    for copy in copies:
        copy.start()
    for copy in copies:
        copy.wait()


def placed(position, pieces, shape, rows):
    blocks = [block for block, *_ in pieces]
    slots = [tuple(place) for _, *place in pieces]
    return pl.pallas_call(
        functools.partial(place_kernel, slots, rows),
        in_specs=[pl.BlockSpec(memory_space=pltpu.SMEM)]
        + [pl.BlockSpec(memory_space=pltpu.VMEM)] * len(blocks),
        out_specs=pl.BlockSpec(memory_space=pltpu.HBM),
        out_shape=jax.ShapeDtypeStruct(shape, BF16),
        scratch_shapes=[pltpu.SemaphoreType.DMA((sum(len(masks) for masks, *_ in slots),))],
        compiler_params=pltpu.CompilerParams(vmem_limit_bytes=16 * MIB),
        name="placed_weights",
    )(position, *blocks)


def adamw(gradient, master, moment_one, moment_two):
    moment_one = 0.9 * moment_one + 0.1 * gradient
    moment_two = 0.95 * moment_two + 0.05 * gradient * gradient
    ratio = moment_one / (1.0 - 0.9**10) / (jnp.sqrt(moment_two / (1.0 - 0.95**10)) + 1e-08)
    return (master - 0.1 * (ratio + 0.1 * master)).astype(BF16)


def flipped(block, axis, mask):
    count = lax.axis_size(axis)
    return lax.ppermute(block, axis, [(i, i ^ mask) for i in range(count)])


def fold(total, bit):
    slots = total.shape[0] // 2
    got = flipped(total[slots:].astype(BF16), "ctx", 1 << bit)
    return total[:slots] + got.astype(F32)


def gathered(have, masks, orders, start):
    chunk = have.shape[1] // 2
    pieces = []
    for half, order in enumerate(orders):
        mine = have[:, half * chunk:(half + 1) * chunk]
        names = masks
        for bit in reversed(order[1:2]):
            mine = jnp.concatenate([mine, flipped(mine, "ctx", 1 << bit)], axis=0)
            names = names + [mask | 1 << bit for mask in names]
        last = flipped(mine, "ctx", 1 << order[0])
        pieces.append((mine, names, half, start))
        pieces.append((last, [mask | 1 << order[0] for mask in names], half, start))
    return pieces


def on_device(
    entries,
    gating,
    state_in,
    state_out,
    step_size,
    decay_rate,
    skip_gain,
    level_gate,
    norm_gain,
    cotangent,
    master_weight,
    first_moment,
    second_moment,
):
    width = entries.shape[1]
    channels = width * lax.axis_size("head")
    count = lax.axis_size("ctx")
    depth = count.bit_length() - 1
    position = lax.axis_index("ctx")
    before_block, prefix, cumulative, group, decay, payload = segment_states(
        entries, state_in, step_size, decay_rate[None, :]
    )
    base, turned = within_blocks(
        entries, gating, state_in, state_out, step_size, prefix, before_block, skip_gain[None, :]
    )
    levels, (base, turned) = level_states(
        payload, group, decay, position, depth, (base, turned)
    )
    gates = level_gate.transpose(1, 0, 2)
    gated, sums = across_levels(base, turned, state_out, gates, cumulative, levels)
    sums = lax.all_gather(sums[0], "head", axis=0, tiled=False)

    rows = master_weight.shape[0]
    chunk = rows // 2
    parts = part_slices(width)
    gain = norm_gain[None, :]
    bits = list(range(depth))
    orders = [bits, [1, 0] + bits[2:]]
    where = position.astype(jnp.int32).reshape(1)
    sends, keeps = [], []
    if chunk % 128 == 0:
        (normed,), sends = terms_to_send(
            where, gated, sums, gain, cotangent, channels, orders, chunk
        )
        keeps = terms_to_keep(where, normed, cotangent, orders, chunk)
    else:
        normed, terms = norm_gradient(gated, sums, gain, cotangent, channels)
        terms = terms.reshape(count, 2, chunk, width)
        for cols in parts:
            for kind, flip, dtype in ((sends, 1, BF16), (keeps, 0, F32)):
                kind.append([
                    terms[position ^ jnp.array(masks_of(order[1:])) ^ (flip << order[0])][
                        :, half, :, cols
                    ].astype(dtype)
                    for half, order in enumerate(orders)
                ])
    gots = [
        [flipped(term, "ctx", 1 << order[0]) for term, order in zip(send, orders)]
        for send in sends
    ]
    totals = []
    for keep, got in zip(keeps, gots):
        halves = []
        for mine, other, order in zip(keep, got, orders):
            total = mine + other.astype(F32)
            for bit in order[1:2]:
                total = fold(total, bit)
            halves.append(total)
        totals.append(jnp.concatenate(halves, axis=1))
    for bit in bits[2:]:
        totals = [fold(total, bit) for total in totals]
    gradients = [total[0] for total in totals]
    haves = [
        adamw(total, master_weight[:, cols], first_moment[:, cols], second_moment[:, cols])[None]
        for total, cols in zip(gradients, parts)
    ]
    masks = [0]
    for bit in reversed(bits[2:]):
        haves = [
            jnp.concatenate([have, flipped(have, "ctx", 1 << bit)], axis=0) for have in haves
        ]
        masks = masks + [mask | 1 << bit for mask in masks]
    pieces = []
    for have, cols in zip(haves, parts):
        pieces += gathered(have, masks, orders, cols.start)
    gradient = jnp.concatenate(gradients, axis=1)
    weights = placed(where, pieces, (count * rows, width), rows)
    return (normed, weights, gradient)


def solution(mesh):
    return jax.shard_map(
        on_device,
        mesh=mesh,
        in_specs=(
            P("ctx", "head"),
            P("ctx", "head"),
            P("ctx", None),
            P("ctx", None),
            P("head", "ctx"),
            P("head"),
            P("head"),
            P("head", None, "ctx"),
            P("head"),
            P("ctx", None),
            P("ctx", "head"),
            P("ctx", "head"),
            P("ctx", "head"),
        ),
        out_specs=(P("ctx", "head"), P(None, "head"), P("ctx", "head")),
        check_vma=False,
    )
```

time: 380 us -> 110 us (0.29)
  local copies, waits for them, and re-layouts: 138 us -> 0.12 us
  waiting for transfers between devices: 151 us -> 39.6 us
  matrix products: 39.3 us -> 0 us
  Pallas kernels: 0 us -> 29 us
  starting transfers between devices: 10.2 us -> 30.3 us
  between operations: 14.3 us -> 0.91 us
  other arithmetic: 17.1 us -> 4.64 us
    dynamic_update_slice x16 -> x0, local copies, waits for them, and re-layouts: 106 us -> none  [block_scan(): lax.scan(advance, start, (decay_blocks, value_blocks, in_blocks, out_bloc...]
    reduce_scatter x1 -> x0, waiting for transfers between devices: 88.2 us -> none  [on_device(): lax.psum_scatter(lax.dot_general(cotangent, normed, (((0,), (0,)), ((), (...]
    all_gather x1 -> x0, waiting for transfers between devices: 49.4 us -> none  [on_device(): weights = lax.all_gather(updated, 'ctx', axis=0, tiled=True)]
    dot_general x36 -> x0, matrix products: 39.3 us -> none  [the longest x1 9.43 us: on_device(): lax.dot_general(cotangent, normed, (((0,), (0,)), ((), ())), preferred_el...]
    pallas_call x0 -> x6, Pallas kernels: none -> 29 us  [the longest x2 11.8 us: terms_call(): pl.pallas_call(kernel, grid_spec=pltpu.PrefetchScalarGridSpec(num_scalar_...]
    ppermute x5 -> x24, waiting for transfers between devices: 13.7 us -> 39.6 us  [flipped(): return lax.ppermute(block, axis, [(i, i ^ mask) for i in range(count)])]
    ppermute x5 -> x24, starting transfers between devices: 10.1 us -> 30.3 us  [flipped(): return lax.ppermute(block, axis, [(i, i ^ mask) for i in range(count)])]
    unnamed x31 -> x10, local copies, waits for them, and re-layouts: 13.7 us -> 0.05 us
  transfers between devices with their start and end apart: 7 -> 24, of which waited for: 6 -> 16; matrix products, arithmetic and copies ran while one was open for 3% -> 1% of each run, Pallas kernels for 0% -> 11%
where the time goes in v2:
time: 110 us
  waiting for transfers between devices  39.6 us (36%)
  starting transfers between devices  30.3 us (28%)
  Pallas kernels  29 us (26%)
  blocking collectives  5.19 us (5%)
  other arithmetic  4.64 us (4%)
    ppermute x24, waiting for transfers between devices, flipped(): return lax.ppermute(block, axis, [(i, i ^ mask) for i in range(count)])  39.6 us
    ppermute x24, starting transfers between devices, flipped(): return lax.ppermute(block, axis, [(i, i ^ mask) for i in range(count)])  30.3 us
    pallas_call x2, Pallas kernels, terms_call(): pl.pallas_call(kernel, grid_spec=pltpu.PrefetchScalarGridSpec(num_scalar_...  11.8 us
    pallas_call x1, Pallas kernels, within_blocks(): pl.pallas_call(within_kernel, grid=(length // tile,), in_specs=[by_rows(w...  6.82 us
    all_gather x1, blocking collectives, on_device(): sums = lax.all_gather(sums[0], 'head', axis=0, tiled=False)  5.19 us
    pallas_call x1, Pallas kernels, across_levels(): pl.pallas_call(functools.partial(across_kernel, len(levels)), grid=(lengt...  5.19 us
    pallas_call x1, Pallas kernels, segment_states(): pl.pallas_call(states_kernel, grid=(length // tile,), in_specs=[pl.BlockS...  3.59 us
  transfers between devices with their start and end apart: 24, of which 16 were waited for; matrix products, arithmetic and copies ran while one was open for 1% of the time, Pallas kernels for 11%

profile of v2, /device:TPU:0, one launch (start us, length us, event | category | flops | bytes accessed | tf_op | source)
XLA Modules:
  0.0 109.7 jit_solution(15979054011593740025)
XLA Ops:
  0.6 3.6 %segment_states.1 = (bf16[8,512,128]{2,1,0:T(8,128)(2,1)S(1)}, f32[8,2048]{1,0:T(8,128)S(1)}, f32[8,2048]{1,0:T(8,128)S(1)}, f32[512,128]{1,0:T(8,128)S(1)}, f32...) custom-call(bf16[2048,512]{1,0:T(8,128)(2,1)} %x_ref.3, bf16[2048,128]{1,0:T(8,128)(2,1)} %b_ref.3, f32[8,2048]{1,0:T(8,128)} %dt_ref.3, ...), custom_call_target="tpu_custom_call" | custom-call | tf_op jit(solution)/shard_map/segment_states/pallas_call | solution.py:137
  4.2 4.0 %collective-permute-start.2 = (bf16[544,128]{1,0:T(8,128)(2,1)}, bf16[544,128]{1,0:T(8,128)(2,1)}, u32[]{:S(2)}, u32[]{:S(2)}) collective-permute-start(bf16[544,128]{1,0:T(8,128)(2,1)} %get-tuple-element.27), channel_id=1, source_target_pairs={{0,12},{4,8},{8,4},{12,0},{16,28},{20,24},{24,20},{28,16},{1,13},{... | collective-permute-start | bytes 417800 | tf_op jit(solution)/shard_map/ppermute | solution.py:541
  8.2 0.4 collective-permute-start.1
  8.6 0.1 collective-permute-start
  8.8 6.8 %within_blocks.1 = (bf16[512,2048]{1,0:T(8,128)(2,1)S(1)}, bf16[512,2048]{1,0:T(8,128)(2,1)}) custom-call(bf16[2048,512]{1,0:T(8,128)(2,1)} %x_ref.3, bf16[2048,512]{1,0:T(8,128)(2,1)} %z_ref.1, bf16[2048,128]{1,0:T(8,128)(2,1)} %b_ref.3, bf16[2048,128]{1,0:T(8,128)(2,1)} %c_ref.3, f32[8,2048]{1,0:T(8,128)} %dt_ref.3, ...), custom_call_target="tpu_custom_call" | custom-call | tf_op jit(solution)/shard_map/within_blocks/pallas_call | solution.py:271
  15.6 0.0 collective-permute-done.2
  15.6 0.0 collective-permute-done
  15.6 0.7 slice_convert_fusion.6
  16.3 0.7 slice_convert_fusion.4
  17.1 1.2 %fusion.26 = (bf16[512,128]{1,0:T(8,128)(2,1)S(1)}, bf16[512,128]{1,0:T(8,128)(2,1)S(1)}, bf16[512,128]{1,0:T(8,128)(2,1)S(1)}) fusion(f32[512,128]{1,0:T(8,128)S(1)} %get-tuple-element.38, f32[8,128]{1,0:T(8,128)S(1)} %get-tuple-element.74, f32[8,128]{1,0:T(8,128)S(1)} %get-tuple-element.71, f32[8,128]{1,0:T(8,128)S(1)} %get-tuple-element.72, ...), kind=kLoop, calls=%fused_computation.63 | loop fusion | flops 1572864 | bytes 1077250 | tf_op jit(solution)/shard_map/convert_element_type | solution.py:173
  18.4 3.0 %collective-permute-start.3 = (bf16[544,128]{1,0:T(8,128)(2,1)S(1)}, bf16[544,128]{1,0:T(8,128)(2,1)S(1)}, u32[]{:S(2)}, u32[]{:S(2)}) collective-permute-start(bf16[544,128]{1,0:T(8,128)(2,1)S(1)} %constant_dynamic-update-slice_fusion), channel_id=1, source_target_pairs={{0,16},{4,20},{8,24},{12,28},{16,0},{20,4},{24,8},{28,12},{1,17},{... | collective-permute-start | bytes 417800 | tf_op jit(solution)/shard_map/ppermute | solution.py:541
  21.4 5.8 %collective-permute-done.3 = bf16[544,128]{1,0:T(8,128)(2,1)S(1)} collective-permute-done((bf16[544,128]{1,0:T(8,128)(2,1)S(1)}, bf16[544,128]{1,0:T(8,128)(2,1)S(1)}, u32[]{:S(2)}, u32[]{:S(2)}) %collective-permute-start.3) | collective-permute-done | bytes 139296 | tf_op jit(solution)/shard_map/ppermute | solution.py:541
  27.3 0.0 copy-start
  27.3 5.2 %across_levels.1 = (bf16[2048,512]{1,0:T(8,128)(2,1)S(1)}, f32[1,2048]{1,0:T(1,128)S(1)}) custom-call(bf16[512,2048]{1,0:T(8,128)(2,1)S(1)} %get-tuple-element.32.base_ref, bf16[512,2048]{1,0:T(8,128)(2,1)} %get-tuple-element.33.z_ref, bf16[2048,128]{1,0:T(8,128)(2,1)} %c_ref.3, f32[5,8,2048]{2,1,0:T(8,128)} %bitcast.66, ...), custom_call_target="tpu_custom_call" | custom-call | tf_op jit(solution)/shard_map/across_levels/pallas_call | solution.py:330
  32.5 5.2 %all-gather = f32[4,1,2048]{2,1,0:T(1,128)S(1)} all-gather(f32[1,1,2048]{2,1,0:T(1,128)S(1)} %bitcast.64), channel_id=1, replica_groups=mesh['ctx'=8,'head'=4] {'head'}, dimensions={0}, use_global_device_ids=true | all-gather | bytes 40960 | tf_op jit(solution)/shard_map/all_gather | solution.py:596
  37.7 6.5 %terms_to_send.1 = (bf16[2048,512]{1,0:T(8,128)(2,1)}, bf16[4,128,256]{2,1,0:T(8,128)(2,1)S(1)}, bf16[4,128,256]{2,1,0:T(8,128)(2,1)S(1)}, bf16[4,128,256]{2,1,0:T(8,128)(2,1)S(1)}, bf16[4,128,256]{2,1,0:T(8,128)(2,1)S(1)}) custom-call(s32[1]{0:T(128)} %bitcast.pos_ref, bf16[2048,512]{1,0:T(8,128)(2,1)S(1)} %get-tuple-element.40.gated_ref, ...), custom_call_target="tpu_custom_call" | custom-call | tf_op jit(solution)/shard_map/terms_to_send/pallas_call | solution.py:454
  44.2 1.9 %collective-permute-start.4 = (bf16[4,128,256]{2,1,0:T(8,128)(2,1)S(1)}, bf16[4,128,256]{2,1,0:T(8,128)(2,1)S(1)}, u32[]{:S(2)}, u32[]{:S(2)}) collective-permute-start(bf16[4,128,256]{2,1,0:T(8,128)(2,1)S(1)} %get-tuple-element.44), channel_id=1, source_target_pairs={{0,4},{4,0},{8,12},{12,8},{16,20},{20,16},{24,28},{28,24},{1,5},{5... | collective-permute-start | bytes 786440 | tf_op jit(solution)/shard_map/ppermute | solution.py:541
  46.1 0.6 collective-permute-start.6
  46.7 0.3 collective-permute-start.14
  47.0 1.3 %collective-permute-start.16 = (bf16[4,128,256]{2,1,0:T(8,128)(2,1)S(1)}, bf16[4,128,256]{2,1,0:T(8,128)(2,1)S(1)}, u32[]{:S(2)}, u32[]{:S(2)}) collective-permute-start(bf16[4,128,256]{2,1,0:T(8,128)(2,1)S(1)} %get-tuple-element.50), channel_id=1, source_target_pairs={{0,8},{4,12},{8,0},{12,4},{16,24},{20,28},{24,16},{28,20},{1,9},{5... | collective-permute-start | bytes 786440 | tf_op jit(solution)/shard_map/ppermute | solution.py:541
  48.3 5.3 %terms_to_keep.1 = (f32[4,128,256]{2,1,0:T(8,128)S(1)}, f32[4,128,256]{2,1,0:T(8,128)S(1)}, f32[4,128,256]{2,1,0:T(8,128)S(1)}, f32[4,128,256]{2,1,0:T(8,128)S(1)}) custom-call(s32[1]{0:T(128)} %bitcast.pos_ref, bf16[2048,512]{1,0:T(8,128)(2,1)} %get-tuple-element.24.normed_ref, bf16[2048,2048]{1,0:T(8,128)(2,1)} %refs_3_.3, bf16[2048,2048]{1,0:T(8,128)(2,1)} %refs_3_.3, ...), custom_call_target="tpu_custom_call" | custom-call | tf_op jit(solution)/shard_map/terms_to_keep/pallas_call | solution.py:454
  53.6 0.0 collective-permute-done.4
  53.6 0.1 convert_add_fusion.3
  53.7 0.8 collective-permute-start.5
  54.5 0.8 collective-permute-done.6
  55.3 0.1 convert_add_fusion.2
  55.4 1.0 collective-permute-start.7
  56.4 2.6 %collective-permute-done.14 = bf16[4,128,256]{2,1,0:T(8,128)(2,1)S(1)} collective-permute-done((bf16[4,128,256]{2,1,0:T(8,128)(2,1)S(1)}, bf16[4,128,256]{2,1,0:T(8,128)(2,1)S(1)}, u32[]{:S(2)}, u32[]{:S(2)}) %collective-permute-start.14) | collective-permute-done | bytes 262176 | tf_op jit(solution)/shard_map/ppermute | solution.py:541
  59.0 0.1 convert_add_fusion.1
  59.1 0.8 collective-permute-start.15
  59.9 1.0 collective-permute-done.16
  60.9 0.1 convert_add_fusion
  61.0 0.0 copy-start.1
  61.0 0.0 copy-start.2
  61.0 0.0 copy-start.3
  61.0 0.8 collective-permute-start.17
  61.8 1.9 %collective-permute-done.5 = bf16[2,128,256]{2,1,0:T(8,128)(2,1)S(1)} collective-permute-done((bf16[2,128,256]{2,1,0:T(8,128)(2,1)S(1)}, bf16[2,128,256]{2,1,0:T(8,128)(2,1)S(1)}, u32[]{:S(2)}, u32[]{:S(2)}) %collective-permute-start.5) | collective-permute-done | bytes 131104 | tf_op jit(solution)/shard_map/ppermute | solution.py:541
  63.8 1.9 %collective-permute-start.8 = (bf16[1,256,256]{2,1,0:T(8,128)(2,1)S(1)}, bf16[1,256,256]{2,1,0:T(8,128)(2,1)S(1)}, u32[]{:S(2)}, u32[]{:S(2)}) collective-permute-start(bf16[1,256,256]{2,1,0:T(8,128)(2,1)S(1)} %fusion.23), channel_id=1, source_target_pairs={{0,16},{4,20},{8,24},{12,28},{16,0},{20,4},{24,8},{28,12},{1,17},{... | collective-permute-start | bytes 393224 | tf_op jit(solution)/shard_map/ppermute | solution.py:541
  65.8 0.3 collective-permute-done.17
  66.1 2.4 %collective-permute-start.18 = (bf16[1,256,256]{2,1,0:T(8,128)(2,1)S(1)}, bf16[1,256,256]{2,1,0:T(8,128)(2,1)S(1)}, u32[]{:S(2)}, u32[]{:S(2)}) collective-permute-start(bf16[1,256,256]{2,1,0:T(8,128)(2,1)S(1)} %fusion.22), channel_id=1, source_target_pairs={{0,16},{4,20},{8,24},{12,28},{16,0},{20,4},{24,8},{28,12},{1,17},{... | collective-permute-start | bytes 393224 | tf_op jit(solution)/shard_map/ppermute | solution.py:541
  68.6 7.1 %collective-permute-done.8 = bf16[1,256,256]{2,1,0:T(8,128)(2,1)S(1)} collective-permute-done((bf16[1,256,256]{2,1,0:T(8,128)(2,1)S(1)}, bf16[1,256,256]{2,1,0:T(8,128)(2,1)S(1)}, u32[]{:S(2)}, u32[]{:S(2)}) %collective-permute-start.8) | collective-permute-done | bytes 131104 | tf_op jit(solution)/shard_map/ppermute | solution.py:541
  75.7 1.4 %collective-permute-done.18 = bf16[1,256,256]{2,1,0:T(8,128)(2,1)S(1)} collective-permute-done((bf16[1,256,256]{2,1,0:T(8,128)(2,1)S(1)}, bf16[1,256,256]{2,1,0:T(8,128)(2,1)S(1)}, u32[]{:S(2)}, u32[]{:S(2)}) %collective-permute-start.18) | collective-permute-done | bytes 131104 | tf_op jit(solution)/shard_map/ppermute | solution.py:541
  77.1 0.5 fusion.35
  77.6 0.1 collective-permute-start.9
  77.7 2.9 %collective-permute-start.19 = (bf16[1,256,256]{2,1,0:T(8,128)(2,1)S(1)}, bf16[1,256,256]{2,1,0:T(8,128)(2,1)S(1)}, u32[]{:S(2)}, u32[]{:S(2)}) collective-permute-start(bf16[1,256,256]{2,1,0:T(8,128)(2,1)S(1)} %get-tuple-element.51), channel_id=1, source_target_pairs={{0,16},{4,20},{8,24},{12,28},{16,0},{20,4},{24,8},{28,12},{1,17},{... | collective-permute-start | bytes 393224 | tf_op jit(solution)/shard_map/ppermute | solution.py:541
  80.6 9.0 %collective-permute-done.9 = bf16[1,256,256]{2,1,0:T(8,128)(2,1)S(1)} collective-permute-done((bf16[1,256,256]{2,1,0:T(8,128)(2,1)S(1)}, bf16[1,256,256]{2,1,0:T(8,128)(2,1)S(1)}, u32[]{:S(2)}, u32[]{:S(2)}) %collective-permute-start.9) | collective-permute-done | bytes 131104 | tf_op jit(solution)/shard_map/ppermute | solution.py:541
  89.6 0.1 collective-permute-start.10
  89.7 0.6 collective-permute-start.12
  90.3 0.9 collective-permute-done.19
  91.2 0.6 collective-permute-start.22
  91.9 1.9 %collective-permute-start.20 = (bf16[2,128,256]{2,1,0:T(8,128)(2,1)S(1)}, bf16[2,128,256]{2,1,0:T(8,128)(2,1)S(1)}, u32[]{:S(2)}, u32[]{:S(2)}) collective-permute-start(bf16[2,128,256]{2,1,0:T(8,128)(2,1)S(1)} %get-tuple-element.66), channel_id=1, source_target_pairs={{0,8},{4,12},{8,0},{12,4},{16,24},{20,28},{24,16},{28,20},{1,9},{5... | collective-permute-start | bytes 393224 | tf_op jit(solution)/shard_map/ppermute | solution.py:541
  93.8 1.9 %collective-permute-done.10 = bf16[2,128,256]{2,1,0:T(8,128)(2,1)S(1)} collective-permute-done((bf16[2,128,256]{2,1,0:T(8,128)(2,1)S(1)}, bf16[2,128,256]{2,1,0:T(8,128)(2,1)S(1)}, u32[]{:S(2)}, u32[]{:S(2)}) %collective-permute-start.10) | collective-permute-done | bytes 131104 | tf_op jit(solution)/shard_map/ppermute | solution.py:541
  95.7 0.5 collective-permute-start.11
  96.2 0.0 collective-permute-done.12
  96.2 1.8 %collective-permute-start.13 = (bf16[4,128,256]{2,1,0:T(8,128)(2,1)S(1)}, bf16[4,128,256]{2,1,0:T(8,128)(2,1)S(1)}, u32[]{:S(2)}, u32[]{:S(2)}) collective-permute-start(bf16[4,128,256]{2,1,0:T(8,128)(2,1)S(1)} %pad_maximum_fusion.4.refs_2_), channel_id=1, source_target_pairs={{0,8},{4,12},{8,0},{12,4},{16,24},{20,28},{24,16},{28,20},{1,9},{5... | collective-permute-start | bytes 786440 | tf_op jit(solution)/shard_map/ppermute | solution.py:541
  98.1 0.4 collective-permute-done.20
  98.5 1.2 %collective-permute-start.21 = (bf16[4,128,256]{2,1,0:T(8,128)(2,1)S(1)}, bf16[4,128,256]{2,1,0:T(8,128)(2,1)S(1)}, u32[]{:S(2)}, u32[]{:S(2)}) collective-permute-start(bf16[4,128,256]{2,1,0:T(8,128)(2,1)S(1)} %pad_maximum_fusion.5.refs_4_), channel_id=1, source_target_pairs={{0,4},{4,0},{8,12},{12,8},{16,20},{20,16},{24,28},{28,24},{1,5},{5... | collective-permute-start | bytes 786440 | tf_op jit(solution)/shard_map/ppermute | solution.py:541
  99.8 1.1 collective-permute-start.23
  100.9 0.9 pad_maximum_fusion
  101.7 3.3 %collective-permute-done.11.refs_1_ = bf16[4,128,256]{2,1,0:T(8,128)(2,1)S(1)} collective-permute-done((bf16[4,128,256]{2,1,0:T(8,128)(2,1)S(1)}, bf16[4,128,256]{2,1,0:T(8,128)(2,1)S(1)}, u32[]{:S(2)}, u32[]{:S(2)}) %collective-permute-start.11) | collective-permute-done | bytes 262176 | tf_op jit(solution)/shard_map/ppermute | solution.py:541
  105.0 0.3 collective-permute-done.13.refs_3_
  105.3 2.7 %collective-permute-done.21.refs_5_ = bf16[4,128,256]{2,1,0:T(8,128)(2,1)S(1)} collective-permute-done((bf16[4,128,256]{2,1,0:T(8,128)(2,1)S(1)}, bf16[4,128,256]{2,1,0:T(8,128)(2,1)S(1)}, u32[]{:S(2)}, u32[]{:S(2)}) %collective-permute-start.21) | collective-permute-done | bytes 262176 | tf_op jit(solution)/shard_map/ppermute | solution.py:541
  108.0 0.1 collective-permute-done.23.refs_7_
  108.1 1.6 %placed_weights.1 = bf16[2048,512]{1,0:T(8,128)(2,1)} custom-call(s32[1]{0:T(128)} %bitcast.pos_ref, bf16[4,128,256]{2,1,0:T(8,128)(2,1)S(1)} %pad_maximum_fusion.3.refs_0_, bf16[4,128,256]{2,1,0:T(8,128)(2,1)S(1)} %collective-permute-done.11.refs_1_, bf16[4,128,256]{2,1,0:T(8,128)(2,1)S(1)} %pad_maximum_fusion.4.refs_2_, ...), custom_call_target="tpu_custom_call" | custom-call | tf_op jit(solution)/shard_map/placed_weights/pallas_call | solution.py:520
  (34 shorter events, 0.5 us)
Async XLA Ops:
  4.2 11.4 %collective-permute-start.2 = (bf16[544,128]{1,0:T(8,128)(2,1)}, bf16[544,128]{1,0:T(8,128)(2,1)}, u32[]{:S(2)}, u32[]{:S(2)}) collective-permute-start(bf16[544,128]{1,0:T(8,128)(2,1)} %get-tuple-element.27), channel_id=1, source_target_pairs={{0,12},{4,8},{8,4},{12,0},{16,28},{20,24},{24,20},{28,16},{1,13},{... | collective-permute-start | bytes 417800 | tf_op jit(solution)/shard_map/ppermute | solution.py:541
  8.2 7.4 %collective-permute-start.1 = (bf16[544,128]{1,0:T(8,128)(2,1)}, bf16[544,128]{1,0:T(8,128)(2,1)}, u32[]{:S(2)}, u32[]{:S(2)}) collective-permute-start(bf16[544,128]{1,0:T(8,128)(2,1)} %get-tuple-element.27), channel_id=1, source_target_pairs={{0,8},{4,12},{8,0},{12,4},{16,24},{20,28},{24,16},{28,20},{1,9},{5... | collective-permute-start | bytes 417800 | tf_op jit(solution)/shard_map/ppermute | solution.py:541
  8.6 6.9 %collective-permute-start = (bf16[544,128]{1,0:T(8,128)(2,1)}, bf16[544,128]{1,0:T(8,128)(2,1)}, u32[]{:S(2)}, u32[]{:S(2)}) collective-permute-start(bf16[544,128]{1,0:T(8,128)(2,1)} %get-tuple-element.27), channel_id=1, source_target_pairs={{0,4},{4,0},{8,12},{12,8},{16,20},{20,16},{24,28},{28,24},{1,5},{5... | collective-permute-start | bytes 417800 | tf_op jit(solution)/shard_map/ppermute | solution.py:541
  18.4 8.9 %collective-permute-start.3 = (bf16[544,128]{1,0:T(8,128)(2,1)S(1)}, bf16[544,128]{1,0:T(8,128)(2,1)S(1)}, u32[]{:S(2)}, u32[]{:S(2)}) collective-permute-start(bf16[544,128]{1,0:T(8,128)(2,1)S(1)} %constant_dynamic-update-slice_fusion), channel_id=1, source_target_pairs={{0,16},{4,20},{8,24},{12,28},{16,0},{20,4},{24,8},{28,12},{1,17},{... | collective-permute-start | bytes 417800 | tf_op jit(solution)/shard_map/ppermute | solution.py:541
  27.3 10.4 %copy-start = (f32[512]{0:T(512)S(1)}, f32[512]{0:T(512)}, u32[]{:S(2)}) copy-start(f32[512]{0:T(512)} %param.21) | copy-start | bytes 6148
  44.2 9.3 %collective-permute-start.4 = (bf16[4,128,256]{2,1,0:T(8,128)(2,1)S(1)}, bf16[4,128,256]{2,1,0:T(8,128)(2,1)S(1)}, u32[]{:S(2)}, u32[]{:S(2)}) collective-permute-start(bf16[4,128,256]{2,1,0:T(8,128)(2,1)S(1)} %get-tuple-element.44), channel_id=1, source_target_pairs={{0,4},{4,0},{8,12},{12,8},{16,20},{20,16},{24,28},{28,24},{1,5},{5... | collective-permute-start | bytes 786440 | tf_op jit(solution)/shard_map/ppermute | solution.py:541
  46.1 9.2 %collective-permute-start.6 = (bf16[4,128,256]{2,1,0:T(8,128)(2,1)S(1)}, bf16[4,128,256]{2,1,0:T(8,128)(2,1)S(1)}, u32[]{:S(2)}, u32[]{:S(2)}) collective-permute-start(bf16[4,128,256]{2,1,0:T(8,128)(2,1)S(1)} %get-tuple-element.46), channel_id=1, source_target_pairs={{0,8},{4,12},{8,0},{12,4},{16,24},{20,28},{24,16},{28,20},{1,9},{5... | collective-permute-start | bytes 786440 | tf_op jit(solution)/shard_map/ppermute | solution.py:541
  46.7 12.3 %collective-permute-start.14 = (bf16[4,128,256]{2,1,0:T(8,128)(2,1)S(1)}, bf16[4,128,256]{2,1,0:T(8,128)(2,1)S(1)}, u32[]{:S(2)}, u32[]{:S(2)}) collective-permute-start(bf16[4,128,256]{2,1,0:T(8,128)(2,1)S(1)} %get-tuple-element.48), channel_id=1, source_target_pairs={{0,4},{4,0},{8,12},{12,8},{16,20},{20,16},{24,28},{28,24},{1,5},{5... | collective-permute-start | bytes 786440 | tf_op jit(solution)/shard_map/ppermute | solution.py:541
  47.0 13.9 %collective-permute-start.16 = (bf16[4,128,256]{2,1,0:T(8,128)(2,1)S(1)}, bf16[4,128,256]{2,1,0:T(8,128)(2,1)S(1)}, u32[]{:S(2)}, u32[]{:S(2)}) collective-permute-start(bf16[4,128,256]{2,1,0:T(8,128)(2,1)S(1)} %get-tuple-element.50), channel_id=1, source_target_pairs={{0,8},{4,12},{8,0},{12,4},{16,24},{20,28},{24,16},{28,20},{1,9},{5... | collective-permute-start | bytes 786440 | tf_op jit(solution)/shard_map/ppermute | solution.py:541
  53.7 10.0 %collective-permute-start.5 = (bf16[2,128,256]{2,1,0:T(8,128)(2,1)S(1)}, bf16[2,128,256]{2,1,0:T(8,128)(2,1)S(1)}, u32[]{:S(2)}, u32[]{:S(2)}) collective-permute-start(bf16[2,128,256]{2,1,0:T(8,128)(2,1)S(1)} %slice.279), channel_id=1, source_target_pairs={{0,8},{4,12},{8,0},{12,4},{16,24},{20,28},{24,16},{28,20},{1,9},{5... | collective-permute-start | bytes 393224 | tf_op jit(solution)/shard_map/ppermute | solution.py:541
  55.4 8.4 %collective-permute-start.7 = (bf16[2,128,256]{2,1,0:T(8,128)(2,1)S(1)}, bf16[2,128,256]{2,1,0:T(8,128)(2,1)S(1)}, u32[]{:S(2)}, u32[]{:S(2)}) collective-permute-start(bf16[2,128,256]{2,1,0:T(8,128)(2,1)S(1)} %slice.278), channel_id=1, source_target_pairs={{0,4},{4,0},{8,12},{12,8},{16,20},{20,16},{24,28},{28,24},{1,5},{5... | collective-permute-start | bytes 393224 | tf_op jit(solution)/shard_map/ppermute | solution.py:541
  59.1 6.7 %collective-permute-start.15 = (bf16[2,128,256]{2,1,0:T(8,128)(2,1)S(1)}, bf16[2,128,256]{2,1,0:T(8,128)(2,1)S(1)}, u32[]{:S(2)}, u32[]{:S(2)}) collective-permute-start(bf16[2,128,256]{2,1,0:T(8,128)(2,1)S(1)} %slice.277), channel_id=1, source_target_pairs={{0,8},{4,12},{8,0},{12,4},{16,24},{20,28},{24,16},{28,20},{1,9},{5... | collective-permute-start | bytes 393224 | tf_op jit(solution)/shard_map/ppermute | solution.py:541
  61.0 16.1 %copy-start.1 = (f32[256,512]{1,0:T(8,128)S(1)}, f32[256,512]{1,0:T(8,128)}, u32[]{:S(2)}) copy-start(f32[256,512]{1,0:T(8,128)} %param.25) | copy-start | bytes 1572868
  61.0 16.1 %copy-start.2 = (f32[256,512]{1,0:T(8,128)S(1)}, f32[256,512]{1,0:T(8,128)}, u32[]{:S(2)}) copy-start(f32[256,512]{1,0:T(8,128)} %param.24) | copy-start | bytes 1572868
  61.0 16.1 %copy-start.3 = (f32[256,512]{1,0:T(8,128)S(1)}, f32[256,512]{1,0:T(8,128)}, u32[]{:S(2)}) copy-start(f32[256,512]{1,0:T(8,128)} %param.23) | copy-start | bytes 1572868
  61.0 5.0 %collective-permute-start.17 = (bf16[2,128,256]{2,1,0:T(8,128)(2,1)S(1)}, bf16[2,128,256]{2,1,0:T(8,128)(2,1)S(1)}, u32[]{:S(2)}, u32[]{:S(2)}) collective-permute-start(bf16[2,128,256]{2,1,0:T(8,128)(2,1)S(1)} %slice.276), channel_id=1, source_target_pairs={{0,4},{4,0},{8,12},{12,8},{16,20},{20,16},{24,28},{28,24},{1,5},{5... | collective-permute-start | bytes 393224 | tf_op jit(solution)/shard_map/ppermute | solution.py:541
  63.8 11.9 %collective-permute-start.8 = (bf16[1,256,256]{2,1,0:T(8,128)(2,1)S(1)}, bf16[1,256,256]{2,1,0:T(8,128)(2,1)S(1)}, u32[]{:S(2)}, u32[]{:S(2)}) collective-permute-start(bf16[1,256,256]{2,1,0:T(8,128)(2,1)S(1)} %fusion.23), channel_id=1, source_target_pairs={{0,16},{4,20},{8,24},{12,28},{16,0},{20,4},{24,8},{28,12},{1,17},{... | collective-permute-start | bytes 393224 | tf_op jit(solution)/shard_map/ppermute | solution.py:541
  66.1 11.0 %collective-permute-start.18 = (bf16[1,256,256]{2,1,0:T(8,128)(2,1)S(1)}, bf16[1,256,256]{2,1,0:T(8,128)(2,1)S(1)}, u32[]{:S(2)}, u32[]{:S(2)}) collective-permute-start(bf16[1,256,256]{2,1,0:T(8,128)(2,1)S(1)} %fusion.22), channel_id=1, source_target_pairs={{0,16},{4,20},{8,24},{12,28},{16,0},{20,4},{24,8},{28,12},{1,17},{... | collective-permute-start | bytes 393224 | tf_op jit(solution)/shard_map/ppermute | solution.py:541
  77.6 12.0 %collective-permute-start.9 = (bf16[1,256,256]{2,1,0:T(8,128)(2,1)S(1)}, bf16[1,256,256]{2,1,0:T(8,128)(2,1)S(1)}, u32[]{:S(2)}, u32[]{:S(2)}) collective-permute-start(bf16[1,256,256]{2,1,0:T(8,128)(2,1)S(1)} %get-tuple-element.61), channel_id=1, source_target_pairs={{0,16},{4,20},{8,24},{12,28},{16,0},{20,4},{24,8},{28,12},{1,17},{... | collective-permute-start | bytes 393224 | tf_op jit(solution)/shard_map/ppermute | solution.py:541
  77.7 13.5 %collective-permute-start.19 = (bf16[1,256,256]{2,1,0:T(8,128)(2,1)S(1)}, bf16[1,256,256]{2,1,0:T(8,128)(2,1)S(1)}, u32[]{:S(2)}, u32[]{:S(2)}) collective-permute-start(bf16[1,256,256]{2,1,0:T(8,128)(2,1)S(1)} %get-tuple-element.51), channel_id=1, source_target_pairs={{0,16},{4,20},{8,24},{12,28},{16,0},{20,4},{24,8},{28,12},{1,17},{... | collective-permute-start | bytes 393224 | tf_op jit(solution)/shard_map/ppermute | solution.py:541
  89.6 6.1 %collective-permute-start.10 = (bf16[2,128,256]{2,1,0:T(8,128)(2,1)S(1)}, bf16[2,128,256]{2,1,0:T(8,128)(2,1)S(1)}, u32[]{:S(2)}, u32[]{:S(2)}) collective-permute-start(bf16[2,128,256]{2,1,0:T(8,128)(2,1)S(1)} %get-tuple-element.68), channel_id=1, source_target_pairs={{0,8},{4,12},{8,0},{12,4},{16,24},{20,28},{24,16},{28,20},{1,9},{5... | collective-permute-start | bytes 393224 | tf_op jit(solution)/shard_map/ppermute | solution.py:541
  89.7 6.5 %collective-permute-start.12 = (bf16[2,128,256]{2,1,0:T(8,128)(2,1)S(1)}, bf16[2,128,256]{2,1,0:T(8,128)(2,1)S(1)}, u32[]{:S(2)}, u32[]{:S(2)}) collective-permute-start(bf16[2,128,256]{2,1,0:T(8,128)(2,1)S(1)} %get-tuple-element.67), channel_id=1, source_target_pairs={{0,4},{4,0},{8,12},{12,8},{16,20},{20,16},{24,28},{28,24},{1,5},{5... | collective-permute-start | bytes 393224 | tf_op jit(solution)/shard_map/ppermute | solution.py:541
  91.2 8.6 %collective-permute-start.22 = (bf16[2,128,256]{2,1,0:T(8,128)(2,1)S(1)}, bf16[2,128,256]{2,1,0:T(8,128)(2,1)S(1)}, u32[]{:S(2)}, u32[]{:S(2)}) collective-permute-start(bf16[2,128,256]{2,1,0:T(8,128)(2,1)S(1)} %get-tuple-element.65), channel_id=1, source_target_pairs={{0,4},{4,0},{8,12},{12,8},{16,20},{20,16},{24,28},{28,24},{1,5},{5... | collective-permute-start | bytes 393224 | tf_op jit(solution)/shard_map/ppermute | solution.py:541
  91.9 6.6 %collective-permute-start.20 = (bf16[2,128,256]{2,1,0:T(8,128)(2,1)S(1)}, bf16[2,128,256]{2,1,0:T(8,128)(2,1)S(1)}, u32[]{:S(2)}, u32[]{:S(2)}) collective-permute-start(bf16[2,128,256]{2,1,0:T(8,128)(2,1)S(1)} %get-tuple-element.66), channel_id=1, source_target_pairs={{0,8},{4,12},{8,0},{12,4},{16,24},{20,28},{24,16},{28,20},{1,9},{5... | collective-permute-start | bytes 393224 | tf_op jit(solution)/shard_map/ppermute | solution.py:541
  95.7 9.3 %collective-permute-start.11 = (bf16[4,128,256]{2,1,0:T(8,128)(2,1)S(1)}, bf16[4,128,256]{2,1,0:T(8,128)(2,1)S(1)}, u32[]{:S(2)}, u32[]{:S(2)}) collective-permute-start(bf16[4,128,256]{2,1,0:T(8,128)(2,1)S(1)} %pad_maximum_fusion.3.refs_0_), channel_id=1, source_target_pairs={{0,4},{4,0},{8,12},{12,8},{16,20},{20,16},{24,28},{28,24},{1,5},{5... | collective-permute-start | bytes 786440 | tf_op jit(solution)/shard_map/ppermute | solution.py:541
  96.2 9.1 %collective-permute-start.13 = (bf16[4,128,256]{2,1,0:T(8,128)(2,1)S(1)}, bf16[4,128,256]{2,1,0:T(8,128)(2,1)S(1)}, u32[]{:S(2)}, u32[]{:S(2)}) collective-permute-start(bf16[4,128,256]{2,1,0:T(8,128)(2,1)S(1)} %pad_maximum_fusion.4.refs_2_), channel_id=1, source_target_pairs={{0,8},{4,12},{8,0},{12,4},{16,24},{20,28},{24,16},{28,20},{1,9},{5... | collective-permute-start | bytes 786440 | tf_op jit(solution)/shard_map/ppermute | solution.py:541
  98.5 9.5 %collective-permute-start.21 = (bf16[4,128,256]{2,1,0:T(8,128)(2,1)S(1)}, bf16[4,128,256]{2,1,0:T(8,128)(2,1)S(1)}, u32[]{:S(2)}, u32[]{:S(2)}) collective-permute-start(bf16[4,128,256]{2,1,0:T(8,128)(2,1)S(1)} %pad_maximum_fusion.5.refs_4_), channel_id=1, source_target_pairs={{0,4},{4,0},{8,12},{12,8},{16,20},{20,16},{24,28},{28,24},{1,5},{5... | collective-permute-start | bytes 786440 | tf_op jit(solution)/shard_map/ppermute | solution.py:541
  99.8 8.3 %collective-permute-start.23 = (bf16[4,128,256]{2,1,0:T(8,128)(2,1)S(1)}, bf16[4,128,256]{2,1,0:T(8,128)(2,1)S(1)}, u32[]{:S(2)}, u32[]{:S(2)}) collective-permute-start(bf16[4,128,256]{2,1,0:T(8,128)(2,1)S(1)} %pad_maximum_fusion.6.refs_6_), channel_id=1, source_target_pairs={{0,8},{4,12},{8,0},{12,4},{16,24},{20,28},{24,16},{28,20},{1,9},{5... | collective-permute-start | bytes 786440 | tf_op jit(solution)/shard_map/ppermute | solution.py:541

commit v3 on v2

--- a/solution.py
+++ b/solution.py
@@ -12,8 +12,6 @@
 BF16 = jnp.bfloat16
 F32 = jnp.float32
 MIB = 1024 * 1024
-CUTS = (0, 4, 8)
-PARTS = len(CUTS) - 1
 TRANSPOSED_LHS = (((0,), (0,)), ((), ()))
 TRANSPOSED_RHS = (((1,), (1,)), ((), ()))
 
@@ -117,11 +115,7 @@
         end_ref[...] = run_ref[...]
         decay_ref[...] = total
         pay_ref[0:width] = run_ref[...].astype(BF16)
-        first, second = split(total)
-        third = (total - first.astype(F32) - second.astype(F32)).astype(BF16)
-        terms = [first.astype(F32), second.astype(F32), third.astype(F32)]
-        terms += [jnp.zeros_like(total)] * (tail_rows(heads) // heads - 3)
-        pay_ref[width:] = jnp.concatenate(terms, axis=0).astype(BF16)
+        pay_ref[width:] = packed_tail(total)
 
 
 def tail_rows(heads):
@@ -153,11 +147,11 @@
         ],
         out_shape=[
             pltpu.VMEM((length // BLOCK, width, states), BF16),
-            pltpu.VMEM((heads, length), F32),
-            pltpu.VMEM((heads, length), F32),
+            pltpu.HBM((heads, length), F32),
+            pltpu.HBM((heads, length), F32),
             jax.ShapeDtypeStruct((width, states), F32),
             jax.ShapeDtypeStruct((heads, states), F32),
-            jax.ShapeDtypeStruct((width + tail_rows(heads), states), BF16),
+            pltpu.VMEM((width + tail_rows(heads), states), BF16),
         ],
         scratch_shapes=[pltpu.VMEM((width, states), F32), pltpu.VMEM((heads, 128), F32)],
         compiler_params=params(24),
@@ -196,26 +190,85 @@
     return level, jnp.where(upper, before + other_decay, before)
 
 
+def near_kernel(
+    pos_ref, got_one, got_two, got_three, state_ref, decay_ref,
+    low_ref, high_ref, pay_ref, group_ref, total_ref, before_ref
+):
+    heads = decay_ref.shape[0]
+    width = state_ref.shape[0]
+    odd = (pos_ref[0] & 1) == 1
+    late = ((pos_ref[0] >> 1) & 1) == 1
+    first = decay_ref[...]
+
+    def tail(got):
+        terms = got[width:].astype(F32)
+        return terms[0:heads] + terms[heads:2 * heads] + terms[2 * heads:3 * heads]
+
+    second, third, fourth = tail(got_one), tail(got_two), tail(got_three)
+    before = jnp.where(odd, second, 0.0)
+    own, other = first + second, third + fourth
+    own_first = jnp.where(odd, 1.0, jnp.exp(second))
+    own_second = jnp.where(odd, jnp.exp(first), 1.0)
+    other_first = jnp.where(odd, 1.0, jnp.exp(fourth))
+    other_second = jnp.where(odd, jnp.exp(third), 1.0)
+    from_own = jnp.where(late, 1.0, jnp.exp(other))
+    from_other = jnp.where(late, jnp.exp(own), 1.0)
+    reach = jnp.exp(before)
+    total = own + other
+    for head in range(heads):
+        rows, row = head_rows(head), slice(head, head + 1)
+        one = got_one[rows].astype(F32)
+        pair = own_first[row] * state_ref[rows] + own_second[row] * one
+        far = other_first[row] * got_two[rows].astype(F32)
+        far = far + other_second[row] * got_three[rows].astype(F32)
+        low_ref[rows] = jnp.where(odd, one, 0.0).astype(BF16)
+        high_ref[rows] = jnp.where(late, reach[row] * far, 0.0).astype(BF16)
+        group = from_own[row] * pair + from_other[row] * far
+        group_ref[rows] = group
+        pay_ref[rows] = group.astype(BF16)
+    pay_ref[width:] = packed_tail(total)
+    total_ref[...] = total
+    before_ref[...] = jnp.where(late, before + other, before)
+
+
+def packed_tail(decay):
+    heads = decay.shape[0]
+    first, second = split(decay)
+    third = (decay - first.astype(F32) - second.astype(F32)).astype(BF16)
+    terms = [first.astype(F32), second.astype(F32), third.astype(F32)]
+    terms += [jnp.zeros_like(decay)] * (tail_rows(heads) // heads - 3)
+    return jnp.concatenate(terms, axis=0).astype(BF16)
+
+
+def near_levels(where, gots, state, decay):
+    width, states = state.shape
+    own = lambda dtype: pltpu.VMEM((width, states), dtype)
+    row = pltpu.VMEM(decay.shape, F32)
+    return pl.pallas_call(
+        near_kernel,
+        in_specs=[pl.BlockSpec(memory_space=pltpu.SMEM)]
+        + [pl.BlockSpec(memory_space=pltpu.VMEM)] * 5,
+        out_specs=[pl.BlockSpec(memory_space=pltpu.VMEM)] * 6,
+        out_shape=[own(BF16), own(BF16), pltpu.VMEM(gots[0].shape, BF16), own(F32), row, row],
+        compiler_params=pltpu.CompilerParams(vmem_limit_bytes=16 * MIB),
+        name="near_levels",
+    )(where, *in_vmem(*gots, state, decay))
+
+
 def level_states(payload, state, decay, position, depth, beside):
     heads = decay.shape[0]
-    uppers = [((position >> bit) & 1) == 1 for bit in range(depth)]
-    before = jnp.zeros_like(decay)
-    levels = []
-    near = min(depth, 2)
-    got = [flipped(payload, "ctx", mask) for mask in range(1, 1 << near)]
-    *got, beside = lax.optimization_barrier((*got, beside))
-    got = [unpacked(each, heads) for each in got]
-    for bit in range(depth):
-        if bit == 0:
-            other, other_decay = got[0]
-        elif bit == 1:
-            other, other_decay = joined(uppers[0], *got[1], *got[2])
-        else:
-            other, other_decay = unpacked(flipped(packed(state, decay), "ctx", 1 << bit), heads)
-        level, before_next = level_of(uppers[bit], before, other, other_decay)
+    gots = [flipped(payload, "ctx", mask) for mask in (1, 2, 3)]
+    *gots, beside = lax.optimization_barrier((*gots, beside))
+    where = position.astype(jnp.int32).reshape(1)
+    *levels, payload, state, decay, before = near_levels(where, gots, state, decay)
+    for bit in range(2, depth):
+        upper = ((position >> bit) & 1) == 1
+        other, other_decay = unpacked(flipped(payload, "ctx", 1 << bit), heads)
+        level, before = level_of(upper, before, other, other_decay)
         levels.append(level)
-        state, decay = joined(uppers[bit], state, decay, other, other_decay)
-        before = before_next
+        if bit < depth - 1:
+            state, decay = joined(upper, state, decay, other, other_decay)
+            payload = packed(state, decay)
     return levels, beside
 
 
@@ -289,8 +342,8 @@
         compiler_params=params(24),
         name="within_blocks",
     )(
-        *in_hbm(entries, gating, state_in, state_out, step_size),
-        *in_vmem(prefix, states),
+        *in_hbm(entries, gating, state_in, state_out, step_size, prefix),
+        *in_vmem(states),
         *in_hbm(skip),
     )
 
@@ -321,7 +374,7 @@
         sums_ref[:, part] = jnp.sum(squares, axis=0, keepdims=True)
 
 
-def across_levels(base, gating, state_out, level_gate, cumulative, levels, tile=512):
+def across_levels(base, gating, state_out, level_gate, cumulative, levels, tile=1024):
     width, length = base.shape
     rungs, heads = level_gate.shape[:2]
     state = state_out.shape[1]
@@ -347,8 +400,7 @@
         name="across_levels",
     )(
         *in_vmem(base),
-        *in_hbm(gating, state_out, level_gate),
-        *in_vmem(cumulative),
+        *in_hbm(gating, state_out, level_gate, cumulative),
         *levels,
     )
 
@@ -399,114 +451,112 @@
     return masks
 
 
-def column_specs(orders, length, count, chunk, keep):
-    def spec(slot):
-        def index(half, pos_ref):
-            flips = [masks_of(order[1:])[slot] | (0 if keep else 1 << order[0]) for order in orders]
-            flip = jnp.where(half == 0, flips[0], flips[1])
-            return (0, 2 * (pos_ref[0] ^ flip) + half)
-
-        return pl.BlockSpec((length, chunk), index)
-
-    return [spec(slot) for slot in range(count // 2)]
-
-
-def part_slices(width):
-    edges = [cut * width // 8 for cut in CUTS]
-    return [slice(start, stop) for start, stop in zip(edges, edges[1:])]
-
-
-def store_half(product, out_refs):
-    for half in range(2):
-
-        @pl.when(pl.program_id(0) == half)
-        def _():
-            for part, cols in enumerate(part_slices(product.shape[1])):
-                out_ref = out_refs[2 * part + half]
-                out_ref[...] = product[:, cols].reshape(out_ref.shape).astype(out_ref.dtype)
-
-
-def send_kernel(channels, pos_ref, gated_ref, sums_ref, gain_ref, *refs):
-    cot_refs, (normed_ref, *out_refs) = refs[:-2 * PARTS - 1], refs[-2 * PARTS - 1:]
-
-    @pl.when(pl.program_id(0) == 0)
+def slot_flips(order, kind, keep):
+    later = masks_of(order[2:])
+    later = later[:1] if kind == "near" else later[1:]
+    first = 0 if keep else 1 << order[0]
+    return [first | second | mask for second in (0, 1 << order[1]) for mask in later]
+
+
+def column_specs(orders, jobs, tile, chunk):
+    def spec(flip, half):
+        return pl.BlockSpec(
+            (tile, chunk), lambda i, pos_ref: (i, 2 * (pos_ref[0] ^ flip) + half)
+        )
+
+    return [
+        spec(flip, half)
+        for kind, keep in jobs
+        for half, order in enumerate(orders)
+        for flip in slot_flips(order, kind, keep)
+    ]
+
+
+def terms_kernel(channels, pos_ref, *refs):
+    refs, acc_ref = refs[:-1], refs[-1]
+    if channels is None:
+        normed_ref, rest = refs[0], refs[1:]
+    else:
+        gated_ref, sums_ref, gain_ref, *rest = refs
+    outs = [ref for ref in rest if len(ref.shape) == 3]
+    rest = [ref for ref in rest if len(ref.shape) == 2]
+    if channels is not None:
+        normed_ref = rest.pop()
+        normalize(channels, gated_ref, sums_ref, gain_ref, normed_ref)
+    columns = jnp.concatenate([ref[...] for ref in rest], axis=1)
+    product = mm(columns, normed_ref[...], TRANSPOSED_LHS)
+    step, steps = pl.program_id(0), pl.num_programs(0)
+
+    @pl.when(step == 0)
     def _():
-        normalize(channels, gated_ref, sums_ref, gain_ref, normed_ref)
-
-    columns = jnp.concatenate([ref[...] for ref in cot_refs], axis=1)
-    store_half(mm(columns, normed_ref[...], TRANSPOSED_LHS), out_refs)
-
-
-def keep_kernel(pos_ref, normed_ref, *refs):
-    cot_refs, out_refs = refs[:-2 * PARTS], refs[-2 * PARTS:]
-    columns = jnp.concatenate([ref[...] for ref in cot_refs], axis=1)
-    store_half(mm(columns, normed_ref[...], TRANSPOSED_LHS), out_refs)
-
-
-def terms_call(kernel, name, position, inputs, cotangent, orders, chunk, keep, outs, dtype):
-    length, width = inputs[0].shape
-    count = 1 << len(orders[0])
-    cots = column_specs(orders, length, count, chunk, keep)
+        acc_ref[...] = product
+
+    @pl.when((step > 0) & (step < steps - 1))
+    def _():
+        acc_ref[...] += product
+
+    @pl.when(step == steps - 1)
+    def _():
+        start = 0
+        for out_ref in outs:
+            slots, chunk, _ = out_ref.shape
+            rows = slice(start, start + slots * chunk)
+            total = acc_ref[rows] + product[rows]
+            out_ref[...] = total.reshape(out_ref.shape).astype(out_ref.dtype)
+            start += slots * chunk
+
+
+def terms_call(name, position, normed, cotangent, orders, jobs, chunk, norm=None, tile=1024):
+    length, width = cotangent.shape[0], normed.shape[1]
+    tile = min(tile, length // 2)
+    cots = column_specs(orders, jobs, tile, chunk)
+    shapes = [
+        (len(slot_flips(order, kind, keep)), chunk, width)
+        for kind, keep in jobs
+        for order in orders
+    ]
+    dtypes = [F32 if keep else BF16 for _, keep in jobs for _ in orders]
     whole = lambda shape: pl.BlockSpec(shape, lambda i, pos_ref: (0,) * len(shape))
-    shapes = [
-        (count // 2, chunk, cols.stop - cols.start) for cols in part_slices(width) for _ in range(2)
-    ]
-    out = pl.pallas_call(
-        kernel,
+    by_tokens = pl.BlockSpec((tile, width), lambda i, pos_ref: (i, 0))
+    in_specs, outs, out_specs, channels = [by_tokens], [], [], None
+    if norm is None:
+        inputs = in_hbm(normed)
+    else:
+        sums, gain, channels = norm
+        inputs = [*in_vmem(normed), sums, gain]
+        in_specs += [
+            pl.BlockSpec((sums.shape[0], tile), lambda i, pos_ref: (0, i)),
+            whole(gain.shape),
+        ]
+        outs, out_specs = [pltpu.HBM(normed.shape, BF16)], [by_tokens]
+    result = pl.pallas_call(
+        functools.partial(terms_kernel, channels),
         grid_spec=pltpu.PrefetchScalarGridSpec(
             num_scalar_prefetch=1,
-            grid=(2,),
-            in_specs=[whole(each.shape) for each in inputs] + cots,
-            out_specs=[whole(each.shape) for each in outs] + [whole(shape) for shape in shapes],
+            grid=(length // tile,),
+            in_specs=in_specs + cots,
+            out_specs=out_specs + [whole(shape) for shape in shapes],
+            scratch_shapes=[pltpu.VMEM((len(cots) * chunk, width), F32)],
         ),
-        out_shape=outs + [jax.ShapeDtypeStruct(shape, dtype) for shape in shapes],
+        out_shape=outs + [jax.ShapeDtypeStruct(*each) for each in zip(shapes, dtypes)],
         compiler_params=params(32),
         name=name,
     )(position, *inputs, *in_hbm(*[cotangent] * len(cots)))
-    terms = out[len(outs):]
-    return out[:len(outs)], [terms[2 * part:2 * part + 2] for part in range(PARTS)]
-
-
-def terms_to_send(position, gated, sums, gain, cotangent, channels, orders, chunk):
-    return terms_call(
-        functools.partial(send_kernel, channels),
-        "terms_to_send",
-        position,
-        [*in_vmem(gated), sums, gain],
-        cotangent,
-        orders,
-        chunk,
-        False,
-        [pltpu.HBM(gated.shape, BF16)],
-        BF16,
-    )
-
-
-def terms_to_keep(position, normed, cotangent, orders, chunk):
-    return terms_call(
-        keep_kernel,
-        "terms_to_keep",
-        position,
-        in_hbm(normed),
-        cotangent,
-        orders,
-        chunk,
-        True,
-        [],
-        F32,
-    )[1]
+    terms = result[len(outs):]
+    return result[:len(outs)], [terms[2 * job:2 * job + 2] for job in range(len(jobs))]
 
 
 def place_kernel(slots, rows, pos_ref, *refs):
-    block_refs, (out_ref, sems) = refs[:-2], refs[-2:]
+    block_refs, (out_ref, sems) = refs[:len(slots)], refs[-2:]
     copies = []
-    for block_ref, (masks, half, start) in zip(block_refs, slots):
-        _, chunk, width = block_ref.shape
+    for block_ref, (masks, half) in zip(block_refs, slots):
+        _, chunk, _ = block_ref.shape
         for slot, mask in enumerate(masks):
             row = pl.multiple_of((pos_ref[0] ^ mask) * rows + half * chunk, chunk)
-            target = out_ref.at[pl.ds(row, chunk), pl.ds(start, width)]
             copies.append(
-                pltpu.make_async_copy(block_ref.at[slot], target, sems.at[len(copies)])
+                pltpu.make_async_copy(
+                    block_ref.at[slot], out_ref.at[pl.ds(row, chunk)], sems.at[len(copies)]
+                )
             )
     for copy in copies:
         copy.start()
@@ -514,19 +564,22 @@
         copy.wait()
 
 
-def placed(position, pieces, shape, rows):
+def placed(position, pieces, shape, rows, name, already=None):
     blocks = [block for block, *_ in pieces]
     slots = [tuple(place) for _, *place in pieces]
+    before = [] if already is None else [already]
     return pl.pallas_call(
         functools.partial(place_kernel, slots, rows),
         in_specs=[pl.BlockSpec(memory_space=pltpu.SMEM)]
-        + [pl.BlockSpec(memory_space=pltpu.VMEM)] * len(blocks),
+        + [pl.BlockSpec(memory_space=pltpu.VMEM)] * len(blocks)
+        + [pl.BlockSpec(memory_space=pltpu.HBM)] * len(before),
         out_specs=pl.BlockSpec(memory_space=pltpu.HBM),
-        out_shape=jax.ShapeDtypeStruct(shape, BF16),
+        out_shape=pltpu.HBM(shape, BF16),
         scratch_shapes=[pltpu.SemaphoreType.DMA((sum(len(masks) for masks, *_ in slots),))],
+        input_output_aliases={1 + len(blocks): 0} if before else {},
         compiler_params=pltpu.CompilerParams(vmem_limit_bytes=16 * MIB),
-        name="placed_weights",
-    )(position, *blocks)
+        name=name,
+    )(position, *blocks, *before)
 
 
 def adamw(gradient, master, moment_one, moment_two):
@@ -536,29 +589,60 @@
     return (master - 0.1 * (ratio + 0.1 * master)).astype(BF16)
 
 
+def update_kernel(keep_ref, got_ref, master_ref, one_ref, two_ref, gradient_ref, updated_ref):
+    gradient = keep_ref[...] + got_ref[...].astype(F32)
+    gradient_ref[...] = gradient
+    updated_ref[...] = adamw(gradient, master_ref[...], one_ref[...], two_ref[...])
+
+
+def update(keep, got, master, one, two):
+    shape = keep.shape
+    return pl.pallas_call(
+        update_kernel,
+        out_shape=[jax.ShapeDtypeStruct(shape, F32), jax.ShapeDtypeStruct(shape, BF16)],
+        compiler_params=pltpu.CompilerParams(vmem_limit_bytes=16 * MIB),
+        name="update_rows",
+    )(keep, got, master, one, two)
+
+
 def flipped(block, axis, mask):
     count = lax.axis_size(axis)
     return lax.ppermute(block, axis, [(i, i ^ mask) for i in range(count)])
 
 
-def fold(total, bit):
-    slots = total.shape[0] // 2
-    got = flipped(total[slots:].astype(BF16), "ctx", 1 << bit)
-    return total[:slots] + got.astype(F32)
-
-
-def gathered(have, masks, orders, start):
+def first_sums(keeps, sends, orders):
+    sums = []
+    for keep, send, order in zip(keeps, sends, orders):
+        total = keep + flipped(send, "ctx", 1 << order[0]).astype(F32)
+        slots = total.shape[0] // 2
+        sums.append((total[slots:].astype(BF16), total[:slots]))
+    return sums
+
+
+def second_sums(sums, orders):
+    halves = [
+        keep + flipped(send, "ctx", 1 << order[1]).astype(F32)
+        for (send, keep), order in zip(sums, orders)
+    ]
+    return jnp.concatenate(halves, axis=1)
+
+
+def nearby(have, orders):
     chunk = have.shape[1] // 2
+    halves = []
+    for half, order in enumerate(orders):
+        mine = have[:, half * chunk:(half + 1) * chunk]
+        halves.append(jnp.concatenate([mine, flipped(mine, "ctx", 1 << order[1])], axis=0))
+    return halves
+
+
+def gathered(halves, masks, orders):
     pieces = []
     for half, order in enumerate(orders):
-        mine = have[:, half * chunk:(half + 1) * chunk]
-        names = masks
-        for bit in reversed(order[1:2]):
-            mine = jnp.concatenate([mine, flipped(mine, "ctx", 1 << bit)], axis=0)
-            names = names + [mask | 1 << bit for mask in names]
-        last = flipped(mine, "ctx", 1 << order[0])
-        pieces.append((mine, names, half, start))
-        pieces.append((last, [mask | 1 << order[0] for mask in names], half, start))
+        names = masks + [mask | 1 << order[1] for mask in masks]
+        last = flipped(halves[half], "ctx", 1 << order[0])
+        pieces.append((halves[half], names, half))
+        pieces.append((last, [mask | 1 << order[0] for mask in names], half))
     return pieces
 
 
@@ -597,59 +681,62 @@
 
     rows = master_weight.shape[0]
     chunk = rows // 2
-    parts = part_slices(width)
     gain = norm_gain[None, :]
     bits = list(range(depth))
     orders = [bits, [1, 0] + bits[2:]]
     where = position.astype(jnp.int32).reshape(1)
-    sends, keeps = [], []
     if chunk % 128 == 0:
-        (normed,), sends = terms_to_send(
-            where, gated, sums, gain, cotangent, channels, orders, chunk
+        call = lambda name, normed, jobs, **kw: terms_call(
+            name, where, normed, cotangent, orders, jobs, chunk, **kw
         )
-        keeps = terms_to_keep(where, normed, cotangent, orders, chunk)
+        (normed,), (far_sends,) = call(
+            "far_terms_to_send", gated, [("far", False)], norm=(sums, gain, channels)
+        )
+        _, (far_keeps, near_sends) = call(
+            "far_terms_to_keep", normed, [("far", True), ("near", False)]
+        )
+        firsts = first_sums(far_keeps, far_sends, orders)
+        firsts, near_sends = lax.optimization_barrier((firsts, near_sends))
+        far = second_sums(firsts, orders)
+        far, again = lax.optimization_barrier((far, normed))
+        _, (near_keeps,) = call("near_terms_to_keep", again, [("near", True)])
     else:
         normed, terms = norm_gradient(gated, sums, gain, cotangent, channels)
         terms = terms.reshape(count, 2, chunk, width)
-        for cols in parts:
-            for kind, flip, dtype in ((sends, 1, BF16), (keeps, 0, F32)):
-                kind.append([
-                    terms[position ^ jnp.array(masks_of(order[1:])) ^ (flip << order[0])][
-                        :, half, :, cols
-                    ].astype(dtype)
-                    for half, order in enumerate(orders)
-                ])
-    gots = [
-        [flipped(term, "ctx", 1 << order[0]) for term, order in zip(send, orders)]
-        for send in sends
-    ]
-    totals = []
-    for keep, got in zip(keeps, gots):
-        halves = []
-        for mine, other, order in zip(keep, got, orders):
-            total = mine + other.astype(F32)
-            for bit in order[1:2]:
-                total = fold(total, bit)
-            halves.append(total)
-        totals.append(jnp.concatenate(halves, axis=1))
+        pick = lambda kind, keep: [
+            terms[position ^ jnp.array(slot_flips(order, kind, keep)), half].astype(
+                F32 if keep else BF16
+            )
+            for half, order in enumerate(orders)
+        ]
+        far_sends, far_keeps = pick("far", False), pick("far", True)
+        near_sends, near_keeps = pick("near", False), pick("near", True)
+        far = second_sums(first_sums(far_keeps, far_sends, orders), orders)
+    near = second_sums(first_sums(near_keeps, near_sends, orders), orders)
+    totals = dict(zip(masks_of(bits[2:]), [near[0], *far]))
     for bit in bits[2:]:
-        totals = [fold(total, bit) for total in totals]
-    gradients = [total[0] for total in totals]
-    haves = [
-        adamw(total, master_weight[:, cols], first_moment[:, cols], second_moment[:, cols])[None]
-        for total, cols in zip(gradients, parts)
-    ]
-    masks = [0]
+        left = [mask for mask in totals if not mask >> bit & 1]
+        send = jnp.stack([totals[mask | 1 << bit].astype(BF16) for mask in left])
+        got = flipped(send, "ctx", 1 << bit)
+        if bit == depth - 1:
+            gradient, updated = update(
+                totals[0], got[0], master_weight, first_moment, second_moment
+            )
+        totals = {mask: totals[mask] + got[at].astype(F32) for at, mask in enumerate(left)}
+    halves = nearby(updated[None], orders)
+    have, masks = updated[None], [0]
     for bit in reversed(bits[2:]):
-        haves = [
-            jnp.concatenate([have, flipped(have, "ctx", 1 << bit)], axis=0) for have in haves
-        ]
+        got = flipped(have, "ctx", 1 << bit)
+        got = lax.optimization_barrier((got, halves[1]))[0]
+        have = jnp.concatenate([have, got], axis=0)
         masks = masks + [mask | 1 << bit for mask in masks]
-    pieces = []
-    for have, cols in zip(haves, parts):
-        pieces += gathered(have, masks, orders, cols.start)
-    gradient = jnp.concatenate(gradients, axis=1)
-    weights = placed(where, pieces, (count * rows, width), rows)
+    pieces = gathered(halves, [0], orders)
+    pieces += gathered(nearby(have[1:], orders), masks[1:], orders)
+    shape = (count * rows, width)
+    late = [pieces[5], pieces[7]]
+    early = pieces[:5] + [pieces[6]]
+    weights = placed(where, early, shape, rows, "placed_early")
+    weights = placed(where, late, shape, rows, "placed_late", weights)
     return (normed, weights, gradient)
 
 

time: 110 us -> 100 us (0.909)
  waiting for transfers between devices: 39.6 us -> 30.9 us
  other arithmetic: 4.64 us -> 0.61 us
  Pallas kernels: 29 us -> 33 us
  starting transfers between devices: 30.3 us -> 29.2 us
    ppermute x24 -> x22, waiting for transfers between devices: 39.6 us -> 30.9 us  [flipped(): return lax.ppermute(block, axis, [(i, i ^ mask) for i in range(count)])]
    pallas_call x2 -> x5, Pallas kernels: 11.8 us -> 15.8 us  [the longest x3 13 us: terms_call(): pl.pallas_call(functools.partial(terms_kernel, channels), grid_spec=pltpu...]
    convert_element_type x3 -> x0, other arithmetic: 2.65 us -> none  [the longest x2 1.41 us: unpacked(): got[width:width + 3 * heads].astype(F32).reshape(3, heads, got.shape[1])]
    ppermute x24 -> x22, starting transfers between devices: 30.3 us -> 29.2 us  [flipped(): return lax.ppermute(block, axis, [(i, i ^ mask) for i in range(count)])]
  transfers between devices with their start and end apart: 24 -> 22, of which waited for: 16 -> 16; matrix products, arithmetic and copies ran while one was open for 1% -> 1% of each run, Pallas kernels for 11% -> 16%
where the time goes in v3:
time: 100 us
  Pallas kernels  33 us (33%)
  waiting for transfers between devices  30.9 us (31%)
  starting transfers between devices  29.2 us (29%)
  blocking collectives  5.19 us (5%)
    ppermute x22, waiting for transfers between devices, flipped(): return lax.ppermute(block, axis, [(i, i ^ mask) for i in range(count)])  30.9 us
    ppermute x22, starting transfers between devices, flipped(): return lax.ppermute(block, axis, [(i, i ^ mask) for i in range(count)])  29.2 us
    pallas_call x3, Pallas kernels, terms_call(): pl.pallas_call(functools.partial(terms_kernel, channels), grid_spec=pltpu...  13 us
    pallas_call x1, Pallas kernels, within_blocks(): pl.pallas_call(within_kernel, grid=(length // tile,), in_specs=[by_rows(w...  6.85 us
    all_gather x1, blocking collectives, on_device(): sums = lax.all_gather(sums[0], 'head', axis=0, tiled=False)  5.19 us
    pallas_call x1, Pallas kernels, across_levels(): pl.pallas_call(functools.partial(across_kernel, len(levels)), grid=(lengt...  4.71 us
    pallas_call x1, Pallas kernels, segment_states(): pl.pallas_call(states_kernel, grid=(length // tile,), in_specs=[pl.BlockS...  3.63 us
    pallas_call x2, Pallas kernels, placed(): pl.pallas_call(functools.partial(place_kernel, slots, rows), in_specs=[pl...  2.05 us
  transfers between devices with their start and end apart: 22, of which 16 were waited for; matrix products, arithmetic and copies ran while one was open for 1% of the time, Pallas kernels for 16%

profile of v3, /device:TPU:0, one launch (start us, length us, event | category | flops | bytes accessed | tf_op | source)
XLA Modules:
  0.0 100.1 jit_solution(2008579735146029633)
XLA Ops:
  0.6 3.6 %segment_states.1 = (bf16[8,512,128]{2,1,0:T(8,128)(2,1)S(1)}, f32[8,2048]{1,0:T(8,128)}, f32[8,2048]{1,0:T(8,128)}, f32[512,128]{1,0:T(8,128)S(1)}, f32[8,128]{1,0:T(8,128)S(1)}, /*index=5*/bf16[544,128]{1,0:T(8,128)(2,1)}) custom-call(bf16[2048,512]{1,0:T(8,128)(2,1)} %x_ref.3, bf16[2048,128]{1,0:T(8,128)(2,1)} %b_ref.3, f32[8,2048]{1,0:T(8,128)} %dt_ref.3, ...), custom_call_target="tpu_custom_call" | custom-call | tf_op jit(solution)/shard_map/segment_states/pallas_call | solution.py:131
  4.3 4.0 %collective-permute-start.2 = (bf16[544,128]{1,0:T(8,128)(2,1)}, bf16[544,128]{1,0:T(8,128)(2,1)S(1)}, u32[]{:S(2)}, u32[]{:S(2)}) collective-permute-start(bf16[544,128]{1,0:T(8,128)(2,1)} %get-tuple-element.42), channel_id=1, source_target_pairs={{0,12},{4,8},{8,4},{12,0},{16,28},{20,24},{24,20},{28,16},{1,13},{... | collective-permute-start | bytes 417800 | tf_op jit(solution)/shard_map/ppermute | solution.py:610
  8.3 0.5 collective-permute-start.1
  8.8 0.2 collective-permute-start
  8.9 6.9 %within_blocks.1 = (bf16[512,2048]{1,0:T(8,128)(2,1)S(1)}, bf16[512,2048]{1,0:T(8,128)(2,1)}) custom-call(bf16[2048,512]{1,0:T(8,128)(2,1)} %x_ref.3, bf16[2048,512]{1,0:T(8,128)(2,1)} %z_ref.1, bf16[2048,128]{1,0:T(8,128)(2,1)} %b_ref.3, bf16[2048,128]{1,0:T(8,128)(2,1)} %c_ref.3, f32[8,2048]{1,0:T(8,128)} %dt_ref.3, ...), custom_call_target="tpu_custom_call" | custom-call | tf_op jit(solution)/shard_map/within_blocks/pallas_call | solution.py:324
  15.8 0.0 collective-permute-done.2.got_three
  15.8 0.0 collective-permute-done.1.got_two
  15.8 0.0 collective-permute-done.got_one
  15.8 1.8 %near_levels.1 = (bf16[512,128]{1,0:T(8,128)(2,1)S(1)}, bf16[512,128]{1,0:T(8,128)(2,1)S(1)}, bf16[544,128]{1,0:T(8,128)(2,1)S(1)}, f32[512,128]{1,0:T(8,128)}, f32[8,128]{1,0:T(8,128)}, /*index=5*/f32[8,128]{1,0:T(8,128)S(1)}) custom-call(s32[1]{0:T(128)} %bitcast.pos_ref, bf16[544,128]{1,0:T(8,128)(2,1)} %collective-permute-done.got_one, ...), custom_call_target="tpu_custom_call" | custom-call | tf_op jit(solution)/shard_map/near_levels/pallas_call | solution.py:247
  17.6 2.9 %collective-permute-start.3 = (bf16[544,128]{1,0:T(8,128)(2,1)S(1)}, bf16[544,128]{1,0:T(8,128)(2,1)S(1)}, u32[]{:S(2)}, u32[]{:S(2)}) collective-permute-start(bf16[544,128]{1,0:T(8,128)(2,1)S(1)} %get-tuple-element.58), channel_id=1, source_target_pairs={{0,16},{4,20},{8,24},{12,28},{16,0},{20,4},{24,8},{28,12},{1,17},{... | collective-permute-start | bytes 417800 | tf_op jit(solution)/shard_map/ppermute | solution.py:610
  20.5 5.8 %collective-permute-done.3 = bf16[544,128]{1,0:T(8,128)(2,1)S(1)} collective-permute-done((bf16[544,128]{1,0:T(8,128)(2,1)S(1)}, bf16[544,128]{1,0:T(8,128)(2,1)S(1)}, u32[]{:S(2)}, u32[]{:S(2)}) %collective-permute-start.3) | collective-permute-done | bytes 139296 | tf_op jit(solution)/shard_map/ppermute | solution.py:610
  26.4 0.0 copy-start.3
  26.4 4.7 %across_levels.1 = (bf16[2048,512]{1,0:T(8,128)(2,1)S(1)}, f32[1,2048]{1,0:T(1,128)S(1)}) custom-call(bf16[512,2048]{1,0:T(8,128)(2,1)S(1)} %get-tuple-element.47.base_ref, bf16[512,2048]{1,0:T(8,128)(2,1)} %get-tuple-element.48.z_ref, bf16[2048,128]{1,0:T(8,128)(2,1)} %c_ref.3, f32[5,8,2048]{2,1,0:T(8,128)} %bitcast.25, ...), custom_call_target="tpu_custom_call" | custom-call | tf_op jit(solution)/shard_map/across_levels/pallas_call | solution.py:383
  31.1 5.2 %all-gather = f32[4,1,2048]{2,1,0:T(1,128)S(1)} all-gather(f32[1,1,2048]{2,1,0:T(1,128)S(1)} %bitcast.23), channel_id=1, replica_groups=mesh['ctx'=8,'head'=4] {'head'}, dimensions={0}, use_global_device_ids=true | all-gather | bytes 40960 | tf_op jit(solution)/shard_map/all_gather | solution.py:680
  36.4 0.0 copy-done.3
  36.4 4.9 %far_terms_to_send.1 = (bf16[2048,512]{1,0:T(8,128)(2,1)}, bf16[2,128,512]{2,1,0:T(8,128)(2,1)S(1)}, bf16[2,128,512]{2,1,0:T(8,128)(2,1)S(1)}) custom-call(s32[1]{0:T(128)} %bitcast.pos_ref, bf16[2048,512]{1,0:T(8,128)(2,1)S(1)} %get-tuple-element.59.refs_0_, f32[4,2048]{1,0:T(4,128)S(1)} %bitcast.22, f32[1,512]{1,0:T(1,128)S(1)} %bitcast.24, ...), custom_call_target="tpu_custom_call" | custom-call | tf_op jit(solution)/shard_map/far_terms_to_send/pallas_call | solution.py:532
  41.2 1.8 %collective-permute-start.4 = (bf16[2,128,512]{2,1,0:T(8,128)(2,1)S(1)}, bf16[2,128,512]{2,1,0:T(8,128)(2,1)S(1)}, u32[]{:S(2)}, u32[]{:S(2)}) collective-permute-start(bf16[2,128,512]{2,1,0:T(8,128)(2,1)S(1)} %get-tuple-element.63), channel_id=1, source_target_pairs={{0,4},{4,0},{8,12},{12,8},{16,20},{20,16},{24,28},{28,24},{1,5},{5... | collective-permute-start | bytes 786440 | tf_op jit(solution)/shard_map/ppermute | solution.py:610
  43.1 0.6 collective-permute-start.5
  43.6 4.9 %far_terms_to_keep.1 = (f32[2,128,512]{2,1,0:T(8,128)S(1)}, f32[2,128,512]{2,1,0:T(8,128)S(1)}, bf16[2,128,512]{2,1,0:T(8,128)(2,1)S(1)}, bf16[2,128,512]{2,1,0:T(8,128)(2,1)S(1)}) custom-call(s32[1]{0:T(128)} %bitcast.pos_ref, bf16[2048,512]{1,0:T(8,128)(2,1)} %get-tuple-element.72.refs_0_, bf16[2048,2048]{1,0:T(8,128)(2,1)} %refs_4_.5, ...), custom_call_target="tpu_custom_call" | custom-call | tf_op jit(solution)/shard_map/far_terms_to_keep/pallas_call | solution.py:532
  48.6 1.3 %collective-permute-done.4 = bf16[2,128,512]{2,1,0:T(8,128)(2,1)S(1)} collective-permute-done((bf16[2,128,512]{2,1,0:T(8,128)(2,1)S(1)}, bf16[2,128,512]{2,1,0:T(8,128)(2,1)S(1)}, u32[]{:S(2)}, u32[]{:S(2)}) %collective-permute-start.4) | collective-permute-done | bytes 262176 | tf_op jit(solution)/shard_map/ppermute | solution.py:610
  49.9 0.1 convert_add_fusion.3
  50.0 1.3 %collective-permute-done.5 = bf16[2,128,512]{2,1,0:T(8,128)(2,1)S(1)} collective-permute-done((bf16[2,128,512]{2,1,0:T(8,128)(2,1)S(1)}, bf16[2,128,512]{2,1,0:T(8,128)(2,1)S(1)}, u32[]{:S(2)}, u32[]{:S(2)}) %collective-permute-start.5) | collective-permute-done | bytes 262176 | tf_op jit(solution)/shard_map/ppermute | solution.py:610
  51.3 0.1 convert_add_fusion.2
  51.5 0.6 collective-permute-start.6
  52.1 0.4 collective-permute-start.7
  52.5 1.6 %collective-permute-start.8 = (bf16[2,128,512]{2,1,0:T(8,128)(2,1)S(1)}, bf16[2,128,512]{2,1,0:T(8,128)(2,1)S(1)}, u32[]{:S(2)}, u32[]{:S(2)}) collective-permute-start(bf16[2,128,512]{2,1,0:T(8,128)(2,1)S(1)} %get-tuple-element.74), channel_id=1, source_target_pairs={{0,4},{4,0},{8,12},{12,8},{16,20},{20,16},{24,28},{28,24},{1,5},{5... | collective-permute-start | bytes 786440 | tf_op jit(solution)/shard_map/ppermute | solution.py:610
  54.1 1.5 %collective-permute-start.10 = (bf16[2,128,512]{2,1,0:T(8,128)(2,1)S(1)}, bf16[2,128,512]{2,1,0:T(8,128)(2,1)S(1)}, u32[]{:S(2)}, u32[]{:S(2)}) collective-permute-start(bf16[2,128,512]{2,1,0:T(8,128)(2,1)S(1)} %get-tuple-element.76), channel_id=1, source_target_pairs={{0,8},{4,12},{8,0},{12,4},{16,24},{20,28},{24,16},{28,20},{1,9},{5... | collective-permute-start | bytes 786440 | tf_op jit(solution)/shard_map/ppermute | solution.py:610
  55.6 2.3 %collective-permute-done.6 = bf16[1,128,512]{2,1,0:T(8,128)(2,1)S(1)} collective-permute-done((bf16[1,128,512]{2,1,0:T(8,128)(2,1)S(1)}, bf16[1,128,512]{2,1,0:T(8,128)(2,1)S(1)}, u32[]{:S(2)}, u32[]{:S(2)}) %collective-permute-start.6) | collective-permute-done | bytes 131104 | tf_op jit(solution)/shard_map/ppermute | solution.py:610
  57.9 0.6 collective-permute-done.7
  58.6 3.5 %collective-permute-start.12 = (bf16[1,256,512]{2,1,0:T(8,128)(2,1)S(1)}, bf16[1,256,512]{2,1,0:T(8,128)(2,1)S(1)}, u32[]{:S(2)}, u32[]{:S(2)}) collective-permute-start(bf16[1,256,512]{2,1,0:T(8,128)(2,1)S(1)} %pad_maximum_fusion), channel_id=1, source_target_pairs={{0,16},{4,20},{8,24},{12,28},{16,0},{20,4},{24,8},{28,12},{1,17},{... | collective-permute-start | bytes 786440 | tf_op jit(solution)/shard_map/ppermute | solution.py:610
  62.0 3.3 %near_terms_to_keep.1 = (f32[2,128,512]{2,1,0:T(8,128)S(1)}, f32[2,128,512]{2,1,0:T(8,128)S(1)}) custom-call(s32[1]{0:T(128)} %bitcast.pos_ref, bf16[2048,512]{1,0:T(8,128)(2,1)} %get-tuple-element.72.refs_0_, bf16[2048,2048]{1,0:T(8,128)(2,1)} %refs_4_.5, bf16[2048,2048]{1,0:T(8,128)(2,1)} %refs_4_.5, bf16[2048,2048]{1,0:T(8,128)(2,1)} %refs_4_.5, ...), custom_call_target="tpu_custom_call" | custom-call | tf_op jit(solution)/shard_map/near_terms_to_keep/pallas_call | solution.py:532
  65.3 0.0 collective-permute-done.8
  65.3 0.1 convert_add_fusion.1
  65.4 0.0 copy-start
  65.4 0.0 copy-start.1
  65.4 0.0 copy-start.2
  65.5 0.4 collective-permute-start.9
  65.8 1.3 %collective-permute-done.10 = bf16[2,128,512]{2,1,0:T(8,128)(2,1)S(1)} collective-permute-done((bf16[2,128,512]{2,1,0:T(8,128)(2,1)S(1)}, bf16[2,128,512]{2,1,0:T(8,128)(2,1)S(1)}, u32[]{:S(2)}, u32[]{:S(2)}) %collective-permute-start.10) | collective-permute-done | bytes 262176 | tf_op jit(solution)/shard_map/ppermute | solution.py:610
  67.1 0.1 convert_add_fusion
  67.2 0.3 collective-permute-start.11
  67.5 3.4 %collective-permute-done.9 = bf16[1,128,512]{2,1,0:T(8,128)(2,1)S(1)} collective-permute-done((bf16[1,128,512]{2,1,0:T(8,128)(2,1)S(1)}, bf16[1,128,512]{2,1,0:T(8,128)(2,1)S(1)}, u32[]{:S(2)}, u32[]{:S(2)}) %collective-permute-start.9) | collective-permute-done | bytes 131104 | tf_op jit(solution)/shard_map/ppermute | solution.py:610
  70.9 1.3 %collective-permute-done.11 = bf16[1,128,512]{2,1,0:T(8,128)(2,1)S(1)} collective-permute-done((bf16[1,128,512]{2,1,0:T(8,128)(2,1)S(1)}, bf16[1,128,512]{2,1,0:T(8,128)(2,1)S(1)}, u32[]{:S(2)}, u32[]{:S(2)}) %collective-permute-start.11) | collective-permute-done | bytes 131104 | tf_op jit(solution)/shard_map/ppermute | solution.py:610
  72.3 0.0 collective-permute-done.12
  72.3 0.9 update_rows.1
  73.3 1.9 %collective-permute-start.13 = (bf16[1,256,512]{2,1,0:T(8,128)(2,1)S(1)}, bf16[1,256,512]{2,1,0:T(8,128)(2,1)S(1)}, u32[]{:S(2)}, u32[]{:S(2)}) collective-permute-start(bf16[1,256,512]{2,1,0:T(8,128)(2,1)S(1)} %bitcast.20), channel_id=1, source_target_pairs={{0,16},{4,20},{8,24},{12,28},{16,0},{20,4},{24,8},{28,12},{1,17},{... | collective-permute-start | bytes 786440 | tf_op jit(solution)/shard_map/ppermute | solution.py:610
  75.1 0.1 collective-permute-start.14
  75.2 3.7 %collective-permute-start.19 = (bf16[1,128,512]{2,1,0:T(8,128)(2,1)S(1)}, bf16[1,128,512]{2,1,0:T(8,128)(2,1)S(1)}, u32[]{:S(2)}, u32[]{:S(2)}) collective-permute-start(bf16[1,128,512]{2,1,0:T(8,128)(2,1)S(1)} %get-tuple-element.81), channel_id=1, source_target_pairs={{0,8},{4,12},{8,0},{12,4},{16,24},{20,28},{24,16},{28,20},{1,9},{5... | collective-permute-start | bytes 393224 | tf_op jit(solution)/shard_map/ppermute | solution.py:610
  78.9 1.3 %collective-permute-done.14 = bf16[1,128,512]{2,1,0:T(8,128)(2,1)S(1)} collective-permute-done((bf16[1,128,512]{2,1,0:T(8,128)(2,1)S(1)}, bf16[1,128,512]{2,1,0:T(8,128)(2,1)S(1)}, u32[]{:S(2)}, u32[]{:S(2)}) %collective-permute-start.14) | collective-permute-done | bytes 131104 | tf_op jit(solution)/shard_map/ppermute | solution.py:610
  80.2 4.0 %collective-permute-done.13 = bf16[1,256,512]{2,1,0:T(8,128)(2,1)S(1)} collective-permute-done((bf16[1,256,512]{2,1,0:T(8,128)(2,1)S(1)}, bf16[1,256,512]{2,1,0:T(8,128)(2,1)S(1)}, u32[]{:S(2)}, u32[]{:S(2)}) %collective-permute-start.13) | collective-permute-done | bytes 262176 | tf_op jit(solution)/shard_map/ppermute | solution.py:610
  84.3 0.1 collective-permute-start.15
  84.4 2.0 %collective-permute-start.21 = (bf16[2,128,512]{2,1,0:T(8,128)(2,1)S(1)}, bf16[2,128,512]{2,1,0:T(8,128)(2,1)S(1)}, u32[]{:S(2)}, u32[]{:S(2)}) collective-permute-start(bf16[2,128,512]{2,1,0:T(8,128)(2,1)S(1)} %pad_maximum_fusion.1.refs_2_), channel_id=1, source_target_pairs={{0,8},{4,12},{8,0},{12,4},{16,24},{20,28},{24,16},{28,20},{1,9},{5... | collective-permute-start | bytes 786440 | tf_op jit(solution)/shard_map/ppermute | solution.py:610
  86.4 0.2 collective-permute-start.17
  86.6 0.0 collective-permute-done.19
  86.6 1.9 %collective-permute-start.20 = (bf16[2,128,512]{2,1,0:T(8,128)(2,1)S(1)}, bf16[2,128,512]{2,1,0:T(8,128)(2,1)S(1)}, u32[]{:S(2)}, u32[]{:S(2)}) collective-permute-start(bf16[2,128,512]{2,1,0:T(8,128)(2,1)S(1)} %pad_maximum_fusion.4.refs_0_), channel_id=1, source_target_pairs={{0,4},{4,0},{8,12},{12,8},{16,20},{20,16},{24,28},{28,24},{1,5},{5... | collective-permute-start | bytes 786440 | tf_op jit(solution)/shard_map/ppermute | solution.py:610
  88.5 1.5 %collective-permute-done.15 = bf16[1,128,512]{2,1,0:T(8,128)(2,1)S(1)} collective-permute-done((bf16[1,128,512]{2,1,0:T(8,128)(2,1)S(1)}, bf16[1,128,512]{2,1,0:T(8,128)(2,1)S(1)}, u32[]{:S(2)}, u32[]{:S(2)}) %collective-permute-start.15) | collective-permute-done | bytes 131104 | tf_op jit(solution)/shard_map/ppermute | solution.py:610
  90.0 1.1 %collective-permute-start.16 = (bf16[2,128,512]{2,1,0:T(8,128)(2,1)S(1)}, bf16[2,128,512]{2,1,0:T(8,128)(2,1)S(1)}, u32[]{:S(2)}, u32[]{:S(2)}) collective-permute-start(bf16[2,128,512]{2,1,0:T(8,128)(2,1)S(1)} %pad_maximum_fusion.2.refs_4_), channel_id=1, source_target_pairs={{0,4},{4,0},{8,12},{12,8},{16,20},{20,16},{24,28},{28,24},{1,5},{5... | collective-permute-start | bytes 786440 | tf_op jit(solution)/shard_map/ppermute | solution.py:610
  91.1 1.7 %collective-permute-done.17 = bf16[1,128,512]{2,1,0:T(8,128)(2,1)S(1)} collective-permute-done((bf16[1,128,512]{2,1,0:T(8,128)(2,1)S(1)}, bf16[1,128,512]{2,1,0:T(8,128)(2,1)S(1)}, u32[]{:S(2)}, u32[]{:S(2)}) %collective-permute-start.17) | collective-permute-done | bytes 131104 | tf_op jit(solution)/shard_map/ppermute | solution.py:610
  92.8 0.1 collective-permute-start.18
  93.0 2.4 %collective-permute-done.21.refs_3_ = bf16[2,128,512]{2,1,0:T(8,128)(2,1)S(1)} collective-permute-done((bf16[2,128,512]{2,1,0:T(8,128)(2,1)S(1)}, bf16[2,128,512]{2,1,0:T(8,128)(2,1)S(1)}, u32[]{:S(2)}, u32[]{:S(2)}) %collective-permute-start.21) | collective-permute-done | bytes 262176 | tf_op jit(solution)/shard_map/ppermute | solution.py:610
  95.4 0.8 collective-permute-done.20.refs_1_
  96.2 1.2 %placed_early.1.refs_2_ = bf16[2048,512]{1,0:T(8,128)(2,1)} custom-call(s32[1]{0:T(128)} %bitcast.pos_ref, bf16[2,128,512]{2,1,0:T(8,128)(2,1)S(1)} %pad_maximum_fusion.4.refs_0_, bf16[2,128,512]{2,1,0:T(8,128)(2,1)S(1)} %collective-permute-done.20.refs_1_, bf16[2,128,512]{2,1,0:T(8,128)(2,1)S(1)} %pad_maximum_fusion.1.refs_2_, ...), custom_call_target="tpu_custom_call" | custom-call | tf_op jit(solution)/shard_map/placed_early/pallas_call | solution.py:571
  97.5 1.6 %collective-permute-done.16.refs_0_ = bf16[2,128,512]{2,1,0:T(8,128)(2,1)S(1)} collective-permute-done((bf16[2,128,512]{2,1,0:T(8,128)(2,1)S(1)}, bf16[2,128,512]{2,1,0:T(8,128)(2,1)S(1)}, u32[]{:S(2)}, u32[]{:S(2)}) %collective-permute-start.16) | collective-permute-done | bytes 262176 | tf_op jit(solution)/shard_map/ppermute | solution.py:610
  99.0 0.2 collective-permute-done.18.refs_1_
  99.3 0.8 placed_late.1
  (24 shorter events, 0.5 us)
Async XLA Ops:
  4.3 11.5 %collective-permute-start.2 = (bf16[544,128]{1,0:T(8,128)(2,1)}, bf16[544,128]{1,0:T(8,128)(2,1)S(1)}, u32[]{:S(2)}, u32[]{:S(2)}) collective-permute-start(bf16[544,128]{1,0:T(8,128)(2,1)} %get-tuple-element.42), channel_id=1, source_target_pairs={{0,12},{4,8},{8,4},{12,0},{16,28},{20,24},{24,20},{28,16},{1,13},{... | collective-permute-start | bytes 417800 | tf_op jit(solution)/shard_map/ppermute | solution.py:610
  8.3 7.5 %collective-permute-start.1 = (bf16[544,128]{1,0:T(8,128)(2,1)}, bf16[544,128]{1,0:T(8,128)(2,1)}, u32[]{:S(2)}, u32[]{:S(2)}) collective-permute-start(bf16[544,128]{1,0:T(8,128)(2,1)} %get-tuple-element.42), channel_id=1, source_target_pairs={{0,8},{4,12},{8,0},{12,4},{16,24},{20,28},{24,16},{28,20},{1,9},{5... | collective-permute-start | bytes 417800 | tf_op jit(solution)/shard_map/ppermute | solution.py:610
  8.8 7.1 %collective-permute-start = (bf16[544,128]{1,0:T(8,128)(2,1)}, bf16[544,128]{1,0:T(8,128)(2,1)}, u32[]{:S(2)}, u32[]{:S(2)}) collective-permute-start(bf16[544,128]{1,0:T(8,128)(2,1)} %get-tuple-element.42), channel_id=1, source_target_pairs={{0,4},{4,0},{8,12},{12,8},{16,20},{20,16},{24,28},{28,24},{1,5},{5... | collective-permute-start | bytes 417800 | tf_op jit(solution)/shard_map/ppermute | solution.py:610
  17.6 8.7 %collective-permute-start.3 = (bf16[544,128]{1,0:T(8,128)(2,1)S(1)}, bf16[544,128]{1,0:T(8,128)(2,1)S(1)}, u32[]{:S(2)}, u32[]{:S(2)}) collective-permute-start(bf16[544,128]{1,0:T(8,128)(2,1)S(1)} %get-tuple-element.58), channel_id=1, source_target_pairs={{0,16},{4,20},{8,24},{12,28},{16,0},{20,4},{24,8},{28,12},{1,17},{... | collective-permute-start | bytes 417800 | tf_op jit(solution)/shard_map/ppermute | solution.py:610
  26.4 9.9 %copy-start.3 = (f32[512]{0:T(512)S(1)}, f32[512]{0:T(512)}, u32[]{:S(2)}) copy-start(f32[512]{0:T(512)} %param.21) | copy-start | bytes 6148
  41.2 8.6 %collective-permute-start.4 = (bf16[2,128,512]{2,1,0:T(8,128)(2,1)S(1)}, bf16[2,128,512]{2,1,0:T(8,128)(2,1)S(1)}, u32[]{:S(2)}, u32[]{:S(2)}) collective-permute-start(bf16[2,128,512]{2,1,0:T(8,128)(2,1)S(1)} %get-tuple-element.63), channel_id=1, source_target_pairs={{0,4},{4,0},{8,12},{12,8},{16,20},{20,16},{24,28},{28,24},{1,5},{5... | collective-permute-start | bytes 786440 | tf_op jit(solution)/shard_map/ppermute | solution.py:610
  43.1 8.2 %collective-permute-start.5 = (bf16[2,128,512]{2,1,0:T(8,128)(2,1)S(1)}, bf16[2,128,512]{2,1,0:T(8,128)(2,1)S(1)}, u32[]{:S(2)}, u32[]{:S(2)}) collective-permute-start(bf16[2,128,512]{2,1,0:T(8,128)(2,1)S(1)} %get-tuple-element.65), channel_id=1, source_target_pairs={{0,8},{4,12},{8,0},{12,4},{16,24},{20,28},{24,16},{28,20},{1,9},{5... | collective-permute-start | bytes 786440 | tf_op jit(solution)/shard_map/ppermute | solution.py:610
  51.5 6.4 %collective-permute-start.6 = (bf16[1,128,512]{2,1,0:T(8,128)(2,1)S(1)}, bf16[1,128,512]{2,1,0:T(8,128)(2,1)S(1)}, u32[]{:S(2)}, u32[]{:S(2)}) collective-permute-start(bf16[1,128,512]{2,1,0:T(8,128)(2,1)S(1)} %slice.77), channel_id=1, source_target_pairs={{0,8},{4,12},{8,0},{12,4},{16,24},{20,28},{24,16},{28,20},{1,9},{5... | collective-permute-start | bytes 393224 | tf_op jit(solution)/shard_map/ppermute | solution.py:610
  52.1 6.4 %collective-permute-start.7 = (bf16[1,128,512]{2,1,0:T(8,128)(2,1)S(1)}, bf16[1,128,512]{2,1,0:T(8,128)(2,1)S(1)}, u32[]{:S(2)}, u32[]{:S(2)}) collective-permute-start(bf16[1,128,512]{2,1,0:T(8,128)(2,1)S(1)} %slice.76), channel_id=1, source_target_pairs={{0,4},{4,0},{8,12},{12,8},{16,20},{20,16},{24,28},{28,24},{1,5},{5... | collective-permute-start | bytes 393224 | tf_op jit(solution)/shard_map/ppermute | solution.py:610
  52.5 12.8 %collective-permute-start.8 = (bf16[2,128,512]{2,1,0:T(8,128)(2,1)S(1)}, bf16[2,128,512]{2,1,0:T(8,128)(2,1)S(1)}, u32[]{:S(2)}, u32[]{:S(2)}) collective-permute-start(bf16[2,128,512]{2,1,0:T(8,128)(2,1)S(1)} %get-tuple-element.74), channel_id=1, source_target_pairs={{0,4},{4,0},{8,12},{12,8},{16,20},{20,16},{24,28},{28,24},{1,5},{5... | collective-permute-start | bytes 786440 | tf_op jit(solution)/shard_map/ppermute | solution.py:610
  54.1 13.0 %collective-permute-start.10 = (bf16[2,128,512]{2,1,0:T(8,128)(2,1)S(1)}, bf16[2,128,512]{2,1,0:T(8,128)(2,1)S(1)}, u32[]{:S(2)}, u32[]{:S(2)}) collective-permute-start(bf16[2,128,512]{2,1,0:T(8,128)(2,1)S(1)} %get-tuple-element.76), channel_id=1, source_target_pairs={{0,8},{4,12},{8,0},{12,4},{16,24},{20,28},{24,16},{28,20},{1,9},{5... | collective-permute-start | bytes 786440 | tf_op jit(solution)/shard_map/ppermute | solution.py:610
  58.6 13.7 %collective-permute-start.12 = (bf16[1,256,512]{2,1,0:T(8,128)(2,1)S(1)}, bf16[1,256,512]{2,1,0:T(8,128)(2,1)S(1)}, u32[]{:S(2)}, u32[]{:S(2)}) collective-permute-start(bf16[1,256,512]{2,1,0:T(8,128)(2,1)S(1)} %pad_maximum_fusion), channel_id=1, source_target_pairs={{0,16},{4,20},{8,24},{12,28},{16,0},{20,4},{24,8},{28,12},{1,17},{... | collective-permute-start | bytes 786440 | tf_op jit(solution)/shard_map/ppermute | solution.py:610
  65.4 6.9 %copy-start = (f32[256,512]{1,0:T(8,128)S(1)}, f32[256,512]{1,0:T(8,128)}, u32[]{:S(2)}) copy-start(f32[256,512]{1,0:T(8,128)} %master_ref.1) | copy-start | bytes 1572868
  65.4 6.9 %copy-start.1 = (f32[256,512]{1,0:T(8,128)S(1)}, f32[256,512]{1,0:T(8,128)}, u32[]{:S(2)}) copy-start(f32[256,512]{1,0:T(8,128)} %one_ref.1) | copy-start | bytes 1572868
  65.4 6.9 %copy-start.2 = (f32[256,512]{1,0:T(8,128)S(1)}, f32[256,512]{1,0:T(8,128)}, u32[]{:S(2)}) copy-start(f32[256,512]{1,0:T(8,128)} %two_ref.1) | copy-start | bytes 1572868
  65.5 5.4 %collective-permute-start.9 = (bf16[1,128,512]{2,1,0:T(8,128)(2,1)S(1)}, bf16[1,128,512]{2,1,0:T(8,128)(2,1)S(1)}, u32[]{:S(2)}, u32[]{:S(2)}) collective-permute-start(bf16[1,128,512]{2,1,0:T(8,128)(2,1)S(1)} %slice.75), channel_id=1, source_target_pairs={{0,8},{4,12},{8,0},{12,4},{16,24},{20,28},{24,16},{28,20},{1,9},{5... | collective-permute-start | bytes 393224 | tf_op jit(solution)/shard_map/ppermute | solution.py:610
  67.2 5.0 %collective-permute-start.11 = (bf16[1,128,512]{2,1,0:T(8,128)(2,1)S(1)}, bf16[1,128,512]{2,1,0:T(8,128)(2,1)S(1)}, u32[]{:S(2)}, u32[]{:S(2)}) collective-permute-start(bf16[1,128,512]{2,1,0:T(8,128)(2,1)S(1)} %slice.74), channel_id=1, source_target_pairs={{0,4},{4,0},{8,12},{12,8},{16,20},{20,16},{24,28},{28,24},{1,5},{5... | collective-permute-start | bytes 393224 | tf_op jit(solution)/shard_map/ppermute | solution.py:610
  73.3 11.0 %collective-permute-start.13 = (bf16[1,256,512]{2,1,0:T(8,128)(2,1)S(1)}, bf16[1,256,512]{2,1,0:T(8,128)(2,1)S(1)}, u32[]{:S(2)}, u32[]{:S(2)}) collective-permute-start(bf16[1,256,512]{2,1,0:T(8,128)(2,1)S(1)} %bitcast.20), channel_id=1, source_target_pairs={{0,16},{4,20},{8,24},{12,28},{16,0},{20,4},{24,8},{28,12},{1,17},{... | collective-permute-start | bytes 786440 | tf_op jit(solution)/shard_map/ppermute | solution.py:610
  75.1 5.0 %collective-permute-start.14 = (bf16[1,128,512]{2,1,0:T(8,128)(2,1)S(1)}, bf16[1,128,512]{2,1,0:T(8,128)(2,1)S(1)}, u32[]{:S(2)}, u32[]{:S(2)}) collective-permute-start(bf16[1,128,512]{2,1,0:T(8,128)(2,1)S(1)} %get-tuple-element.82), channel_id=1, source_target_pairs={{0,4},{4,0},{8,12},{12,8},{16,20},{20,16},{24,28},{28,24},{1,5},{5... | collective-permute-start | bytes 393224 | tf_op jit(solution)/shard_map/ppermute | solution.py:610
  75.2 11.4 %collective-permute-start.19 = (bf16[1,128,512]{2,1,0:T(8,128)(2,1)S(1)}, bf16[1,128,512]{2,1,0:T(8,128)(2,1)S(1)}, u32[]{:S(2)}, u32[]{:S(2)}) collective-permute-start(bf16[1,128,512]{2,1,0:T(8,128)(2,1)S(1)} %get-tuple-element.81), channel_id=1, source_target_pairs={{0,8},{4,12},{8,0},{12,4},{16,24},{20,28},{24,16},{28,20},{1,9},{5... | collective-permute-start | bytes 393224 | tf_op jit(solution)/shard_map/ppermute | solution.py:610
  84.3 5.7 %collective-permute-start.15 = (bf16[1,128,512]{2,1,0:T(8,128)(2,1)S(1)}, bf16[1,128,512]{2,1,0:T(8,128)(2,1)S(1)}, u32[]{:S(2)}, u32[]{:S(2)}) collective-permute-start(bf16[1,128,512]{2,1,0:T(8,128)(2,1)S(1)} %get-tuple-element.84), channel_id=1, source_target_pairs={{0,8},{4,12},{8,0},{12,4},{16,24},{20,28},{24,16},{28,20},{1,9},{5... | collective-permute-start | bytes 393224 | tf_op jit(solution)/shard_map/ppermute | solution.py:610
  84.4 11.0 %collective-permute-start.21 = (bf16[2,128,512]{2,1,0:T(8,128)(2,1)S(1)}, bf16[2,128,512]{2,1,0:T(8,128)(2,1)S(1)}, u32[]{:S(2)}, u32[]{:S(2)}) collective-permute-start(bf16[2,128,512]{2,1,0:T(8,128)(2,1)S(1)} %pad_maximum_fusion.1.refs_2_), channel_id=1, source_target_pairs={{0,8},{4,12},{8,0},{12,4},{16,24},{20,28},{24,16},{28,20},{1,9},{5... | collective-permute-start | bytes 786440 | tf_op jit(solution)/shard_map/ppermute | solution.py:610
  86.4 6.4 %collective-permute-start.17 = (bf16[1,128,512]{2,1,0:T(8,128)(2,1)S(1)}, bf16[1,128,512]{2,1,0:T(8,128)(2,1)S(1)}, u32[]{:S(2)}, u32[]{:S(2)}) collective-permute-start(bf16[1,128,512]{2,1,0:T(8,128)(2,1)S(1)} %get-tuple-element.83), channel_id=1, source_target_pairs={{0,4},{4,0},{8,12},{12,8},{16,20},{20,16},{24,28},{28,24},{1,5},{5... | collective-permute-start | bytes 393224 | tf_op jit(solution)/shard_map/ppermute | solution.py:610
  86.6 9.6 %collective-permute-start.20 = (bf16[2,128,512]{2,1,0:T(8,128)(2,1)S(1)}, bf16[2,128,512]{2,1,0:T(8,128)(2,1)S(1)}, u32[]{:S(2)}, u32[]{:S(2)}) collective-permute-start(bf16[2,128,512]{2,1,0:T(8,128)(2,1)S(1)} %pad_maximum_fusion.4.refs_0_), channel_id=1, source_target_pairs={{0,4},{4,0},{8,12},{12,8},{16,20},{20,16},{24,28},{28,24},{1,5},{5... | collective-permute-start | bytes 786440 | tf_op jit(solution)/shard_map/ppermute | solution.py:610
  90.0 9.0 %collective-permute-start.16 = (bf16[2,128,512]{2,1,0:T(8,128)(2,1)S(1)}, bf16[2,128,512]{2,1,0:T(8,128)(2,1)S(1)}, u32[]{:S(2)}, u32[]{:S(2)}) collective-permute-start(bf16[2,128,512]{2,1,0:T(8,128)(2,1)S(1)} %pad_maximum_fusion.2.refs_4_), channel_id=1, source_target_pairs={{0,4},{4,0},{8,12},{12,8},{16,20},{20,16},{24,28},{28,24},{1,5},{5... | collective-permute-start | bytes 786440 | tf_op jit(solution)/shard_map/ppermute | solution.py:610
  92.8 6.4 %collective-permute-start.18 = (bf16[2,128,512]{2,1,0:T(8,128)(2,1)S(1)}, bf16[2,128,512]{2,1,0:T(8,128)(2,1)S(1)}, u32[]{:S(2)}, u32[]{:S(2)}) collective-permute-start(bf16[2,128,512]{2,1,0:T(8,128)(2,1)S(1)} %pad_maximum_fusion.3.refs_5_), channel_id=1, source_target_pairs={{0,8},{4,12},{8,0},{12,4},{16,24},{20,28},{24,16},{28,20},{1,9},{5... | collective-permute-start | bytes 786440 | tf_op jit(solution)/shard_map/ppermute | solution.py:610

commit v4 on v3

--- a/solution.py
+++ b/solution.py
@@ -192,7 +192,7 @@
 
 def near_kernel(
     pos_ref, got_one, got_two, got_three, state_ref, decay_ref,
-    low_ref, high_ref, pay_ref, group_ref, total_ref, before_ref
+    low_ref, high_ref, pay_ref, before_ref, *group_refs
 ):
     heads = decay_ref.shape[0]
     width = state_ref.shape[0]
@@ -224,11 +224,13 @@
         low_ref[rows] = jnp.where(odd, one, 0.0).astype(BF16)
         high_ref[rows] = jnp.where(late, reach[row] * far, 0.0).astype(BF16)
         group = from_own[row] * pair + from_other[row] * far
-        group_ref[rows] = group
         pay_ref[rows] = group.astype(BF16)
+        if group_refs:
+            group_refs[0][rows] = group
     pay_ref[width:] = packed_tail(total)
-    total_ref[...] = total
     before_ref[...] = jnp.where(late, before + other, before)
+    if group_refs:
+        group_refs[1][...] = total
 
 
 def packed_tail(decay):
@@ -240,16 +242,19 @@
     return jnp.concatenate(terms, axis=0).astype(BF16)
 
 
-def near_levels(where, gots, state, decay):
+def near_levels(where, gots, state, decay, with_group):
     width, states = state.shape
     own = lambda dtype: pltpu.VMEM((width, states), dtype)
     row = pltpu.VMEM(decay.shape, F32)
+    shapes = [own(BF16), own(BF16), pltpu.VMEM(gots[0].shape, BF16), row]
+    if with_group:
+        shapes += [own(F32), row]
     return pl.pallas_call(
         near_kernel,
         in_specs=[pl.BlockSpec(memory_space=pltpu.SMEM)]
         + [pl.BlockSpec(memory_space=pltpu.VMEM)] * 5,
-        out_specs=[pl.BlockSpec(memory_space=pltpu.VMEM)] * 6,
-        out_shape=[own(BF16), own(BF16), pltpu.VMEM(gots[0].shape, BF16), own(F32), row, row],
+        out_specs=[pl.BlockSpec(memory_space=pltpu.VMEM)] * len(shapes),
+        out_shape=shapes,
         compiler_params=pltpu.CompilerParams(vmem_limit_bytes=16 * MIB),
         name="near_levels",
     )(where, *in_vmem(*gots, state, decay))
@@ -260,7 +265,9 @@
     gots = [flipped(payload, "ctx", mask) for mask in (1, 2, 3)]
     *gots, beside = lax.optimization_barrier((*gots, beside))
     where = position.astype(jnp.int32).reshape(1)
-    *levels, payload, state, decay, before = near_levels(where, gots, state, decay)
+    low, high, payload, before, *group = near_levels(where, gots, state, decay, depth > 3)
+    levels = [low, high]
+    state, decay = group or (state, decay)
     for bit in range(2, depth):
         upper = ((position >> bit) & 1) == 1
         other, other_decay = unpacked(flipped(payload, "ctx", 1 << bit), heads)
@@ -599,7 +606,7 @@
     shape = keep.shape
     return pl.pallas_call(
         update_kernel,
-        out_shape=[jax.ShapeDtypeStruct(shape, F32), jax.ShapeDtypeStruct(shape, BF16)],
+        out_shape=[pltpu.VMEM(shape, F32), pltpu.VMEM(shape, BF16)],
         compiler_params=pltpu.CompilerParams(vmem_limit_bytes=16 * MIB),
         name="update_rows",
     )(keep, got, master, one, two)
@@ -730,8 +737,9 @@
         got = lax.optimization_barrier((got, halves[1]))[0]
         have = jnp.concatenate([have, got], axis=0)
         masks = masks + [mask | 1 << bit for mask in masks]
+    far_blocks, *halves = lax.optimization_barrier((have[1:], *halves))
     pieces = gathered(halves, [0], orders)
-    pieces += gathered(nearby(have[1:], orders), masks[1:], orders)
+    pieces += gathered(nearby(far_blocks, orders), masks[1:], orders)
     shape = (count * rows, width)
     late = [pieces[5], pieces[7]]
     early = pieces[:5] + [pieces[6]]

time: 100 us -> 98.6 us (0.986)
  starting transfers between devices: 29.2 us -> 27.7 us
  Pallas kernels: 33 us -> 32 us
    ppermute x22, starting transfers between devices: 29.2 us -> 27.7 us  [flipped(): return lax.ppermute(block, axis, [(i, i ^ mask) for i in range(count)])]
  transfers between devices with their start and end apart: 22 -> 22, of which waited for: 16 -> 16; matrix products, arithmetic and copies ran while one was open for 1% -> 1% of each run, Pallas kernels for 16% -> 17%
where the time goes in v4:
time: 98.6 us; the launch traced here: 98.3 us
  Pallas kernels  32 us (32%)
  waiting for transfers between devices  30.9 us (31%)
  starting transfers between devices  27.7 us (28%)
  blocking collectives  5.19 us (5%)
  local copies, waits for them, and re-layouts  0.99 us (1%)
    ppermute x22, waiting for transfers between devices, flipped(): return lax.ppermute(block, axis, [(i, i ^ mask) for i in range(count)])  30.9 us
    ppermute x22, starting transfers between devices, flipped(): return lax.ppermute(block, axis, [(i, i ^ mask) for i in range(count)])  27.7 us
    pallas_call x3, Pallas kernels, terms_call(): pl.pallas_call(functools.partial(terms_kernel, channels), grid_spec=pltpu...  13 us
    pallas_call x1, Pallas kernels, within_blocks(): pl.pallas_call(within_kernel, grid=(length // tile,), in_specs=[by_rows(w...  6.85 us
    all_gather x1, blocking collectives, on_device(): sums = lax.all_gather(sums[0], 'head', axis=0, tiled=False)  5.19 us
    pallas_call x1, Pallas kernels, across_levels(): pl.pallas_call(functools.partial(across_kernel, len(levels)), grid=(lengt...  4.71 us
    pallas_call x1, Pallas kernels, segment_states(): pl.pallas_call(states_kernel, grid=(length // tile,), in_specs=[pl.BlockS...  3.63 us
    pallas_call x2, Pallas kernels, placed(): pl.pallas_call(functools.partial(place_kernel, slots, rows), in_specs=[pl...  2.05 us
  transfers between devices with their start and end apart: 22, of which 16 were waited for; matrix products, arithmetic and copies ran while one was open for 1% of the time, Pallas kernels for 17%

profile of v4, /device:TPU:0, one launch (start us, length us, event | category | flops | bytes accessed | tf_op | source)
XLA Modules:
  0.0 98.3 jit_solution(2783869680716821128)
XLA Ops:
  0.6 3.6 %segment_states.1 = (bf16[8,512,128]{2,1,0:T(8,128)(2,1)S(1)}, f32[8,2048]{1,0:T(8,128)}, f32[8,2048]{1,0:T(8,128)}, f32[512,128]{1,0:T(8,128)S(1)}, f32[8,128]{1,0:T(8,128)S(1)}, /*index=5*/bf16[544,128]{1,0:T(8,128)(2,1)}) custom-call(bf16[2048,512]{1,0:T(8,128)(2,1)} %x_ref.3, bf16[2048,128]{1,0:T(8,128)(2,1)} %b_ref.3, f32[8,2048]{1,0:T(8,128)} %dt_ref.3, ...), custom_call_target="tpu_custom_call" | custom-call | tf_op jit(solution)/shard_map/segment_states/pallas_call | solution.py:131
  4.3 4.0 %collective-permute-start.2 = (bf16[544,128]{1,0:T(8,128)(2,1)}, bf16[544,128]{1,0:T(8,128)(2,1)S(1)}, u32[]{:S(2)}, u32[]{:S(2)}) collective-permute-start(bf16[544,128]{1,0:T(8,128)(2,1)} %get-tuple-element.45), channel_id=1, source_target_pairs={{0,12},{4,8},{8,4},{12,0},{16,28},{20,24},{24,20},{28,16},{1,13},{... | collective-permute-start | bytes 417800 | tf_op jit(solution)/shard_map/ppermute | solution.py:617
  8.3 0.5 collective-permute-start.1
  8.8 0.2 collective-permute-start
  8.9 6.9 %within_blocks.1 = (bf16[512,2048]{1,0:T(8,128)(2,1)S(1)}, bf16[512,2048]{1,0:T(8,128)(2,1)}) custom-call(bf16[2048,512]{1,0:T(8,128)(2,1)} %x_ref.3, bf16[2048,512]{1,0:T(8,128)(2,1)} %z_ref.1, bf16[2048,128]{1,0:T(8,128)(2,1)} %b_ref.3, bf16[2048,128]{1,0:T(8,128)(2,1)} %c_ref.3, f32[8,2048]{1,0:T(8,128)} %dt_ref.3, ...), custom_call_target="tpu_custom_call" | custom-call | tf_op jit(solution)/shard_map/within_blocks/pallas_call | solution.py:331
  15.8 0.0 collective-permute-done.2.got_three
  15.8 0.0 collective-permute-done.1.got_two
  15.8 0.0 collective-permute-done.got_one
  15.8 1.1 %near_levels.1 = (bf16[512,128]{1,0:T(8,128)(2,1)S(1)}, bf16[512,128]{1,0:T(8,128)(2,1)S(1)}, bf16[544,128]{1,0:T(8,128)(2,1)S(1)}, f32[8,128]{1,0:T(8,128)S(1)}) custom-call(s32[1]{0:T(128)} %bitcast.pos_ref, bf16[544,128]{1,0:T(8,128)(2,1)} %collective-permute-done.got_one, bf16[544,128]{1,0:T(8,128)(2,1)} %collective-permute-done.1.got_two, ...), custom_call_target="tpu_custom_call" | custom-call | tf_op jit(solution)/shard_map/near_levels/pallas_call | solution.py:252
  17.0 3.0 %collective-permute-start.3 = (bf16[544,128]{1,0:T(8,128)(2,1)S(1)}, bf16[544,128]{1,0:T(8,128)(2,1)S(1)}, u32[]{:S(2)}, u32[]{:S(2)}) collective-permute-start(bf16[544,128]{1,0:T(8,128)(2,1)S(1)} %get-tuple-element.61), channel_id=1, source_target_pairs={{0,16},{4,20},{8,24},{12,28},{16,0},{20,4},{24,8},{28,12},{1,17},{... | collective-permute-start | bytes 417800 | tf_op jit(solution)/shard_map/ppermute | solution.py:617
  19.9 5.8 %collective-permute-done.3 = bf16[544,128]{1,0:T(8,128)(2,1)S(1)} collective-permute-done((bf16[544,128]{1,0:T(8,128)(2,1)S(1)}, bf16[544,128]{1,0:T(8,128)(2,1)S(1)}, u32[]{:S(2)}, u32[]{:S(2)}) %collective-permute-start.3) | collective-permute-done | bytes 139296 | tf_op jit(solution)/shard_map/ppermute | solution.py:617
  25.8 0.0 copy-start.3
  25.8 4.7 %across_levels.1 = (bf16[2048,512]{1,0:T(8,128)(2,1)S(1)}, f32[1,2048]{1,0:T(1,128)S(1)}) custom-call(bf16[512,2048]{1,0:T(8,128)(2,1)S(1)} %get-tuple-element.50.base_ref, bf16[512,2048]{1,0:T(8,128)(2,1)} %get-tuple-element.51.z_ref, bf16[2048,128]{1,0:T(8,128)(2,1)} %c_ref.3, f32[5,8,2048]{2,1,0:T(8,128)} %bitcast.25, ...), custom_call_target="tpu_custom_call" | custom-call | tf_op jit(solution)/shard_map/across_levels/pallas_call | solution.py:390
  30.5 5.2 %all-gather = f32[4,1,2048]{2,1,0:T(1,128)S(1)} all-gather(f32[1,1,2048]{2,1,0:T(1,128)S(1)} %bitcast.23), channel_id=1, replica_groups=mesh['ctx'=8,'head'=4] {'head'}, dimensions={0}, use_global_device_ids=true | all-gather | bytes 40960 | tf_op jit(solution)/shard_map/all_gather | solution.py:687
  35.8 4.9 %far_terms_to_send.1 = (bf16[2048,512]{1,0:T(8,128)(2,1)}, bf16[2,128,512]{2,1,0:T(8,128)(2,1)S(1)}, bf16[2,128,512]{2,1,0:T(8,128)(2,1)S(1)}) custom-call(s32[1]{0:T(128)} %bitcast.pos_ref, bf16[2048,512]{1,0:T(8,128)(2,1)S(1)} %get-tuple-element.62.refs_0_, f32[4,2048]{1,0:T(4,128)S(1)} %bitcast.22, f32[1,512]{1,0:T(1,128)S(1)} %bitcast.24, ...), custom_call_target="tpu_custom_call" | custom-call | tf_op jit(solution)/shard_map/far_terms_to_send/pallas_call | solution.py:539
  40.6 1.8 %collective-permute-start.4 = (bf16[2,128,512]{2,1,0:T(8,128)(2,1)S(1)}, bf16[2,128,512]{2,1,0:T(8,128)(2,1)S(1)}, u32[]{:S(2)}, u32[]{:S(2)}) collective-permute-start(bf16[2,128,512]{2,1,0:T(8,128)(2,1)S(1)} %get-tuple-element.66), channel_id=1, source_target_pairs={{0,4},{4,0},{8,12},{12,8},{16,20},{20,16},{24,28},{28,24},{1,5},{5... | collective-permute-start | bytes 786440 | tf_op jit(solution)/shard_map/ppermute | solution.py:617
  42.5 0.6 collective-permute-start.5
  43.0 4.9 %far_terms_to_keep.1 = (f32[2,128,512]{2,1,0:T(8,128)S(1)}, f32[2,128,512]{2,1,0:T(8,128)S(1)}, bf16[2,128,512]{2,1,0:T(8,128)(2,1)S(1)}, bf16[2,128,512]{2,1,0:T(8,128)(2,1)S(1)}) custom-call(s32[1]{0:T(128)} %bitcast.pos_ref, bf16[2048,512]{1,0:T(8,128)(2,1)} %get-tuple-element.75.refs_0_, bf16[2048,2048]{1,0:T(8,128)(2,1)} %refs_4_.5, ...), custom_call_target="tpu_custom_call" | custom-call | tf_op jit(solution)/shard_map/far_terms_to_keep/pallas_call | solution.py:539
  48.0 1.3 %collective-permute-done.4 = bf16[2,128,512]{2,1,0:T(8,128)(2,1)S(1)} collective-permute-done((bf16[2,128,512]{2,1,0:T(8,128)(2,1)S(1)}, bf16[2,128,512]{2,1,0:T(8,128)(2,1)S(1)}, u32[]{:S(2)}, u32[]{:S(2)}) %collective-permute-start.4) | collective-permute-done | bytes 262176 | tf_op jit(solution)/shard_map/ppermute | solution.py:617
  49.3 0.1 convert_add_fusion.3
  49.4 1.3 %collective-permute-done.5 = bf16[2,128,512]{2,1,0:T(8,128)(2,1)S(1)} collective-permute-done((bf16[2,128,512]{2,1,0:T(8,128)(2,1)S(1)}, bf16[2,128,512]{2,1,0:T(8,128)(2,1)S(1)}, u32[]{:S(2)}, u32[]{:S(2)}) %collective-permute-start.5) | collective-permute-done | bytes 262176 | tf_op jit(solution)/shard_map/ppermute | solution.py:617
  50.7 0.1 convert_add_fusion.2
  50.9 0.6 collective-permute-start.6
  51.5 0.4 collective-permute-start.7
  51.9 1.6 %collective-permute-start.8 = (bf16[2,128,512]{2,1,0:T(8,128)(2,1)S(1)}, bf16[2,128,512]{2,1,0:T(8,128)(2,1)S(1)}, u32[]{:S(2)}, u32[]{:S(2)}) collective-permute-start(bf16[2,128,512]{2,1,0:T(8,128)(2,1)S(1)} %get-tuple-element.77), channel_id=1, source_target_pairs={{0,4},{4,0},{8,12},{12,8},{16,20},{20,16},{24,28},{28,24},{1,5},{5... | collective-permute-start | bytes 786440 | tf_op jit(solution)/shard_map/ppermute | solution.py:617
  53.5 1.4 %collective-permute-start.10 = (bf16[2,128,512]{2,1,0:T(8,128)(2,1)S(1)}, bf16[2,128,512]{2,1,0:T(8,128)(2,1)S(1)}, u32[]{:S(2)}, u32[]{:S(2)}) collective-permute-start(bf16[2,128,512]{2,1,0:T(8,128)(2,1)S(1)} %get-tuple-element.79), channel_id=1, source_target_pairs={{0,8},{4,12},{8,0},{12,4},{16,24},{20,28},{24,16},{28,20},{1,9},{5... | collective-permute-start | bytes 786440 | tf_op jit(solution)/shard_map/ppermute | solution.py:617
  55.0 2.3 %collective-permute-done.6 = bf16[1,128,512]{2,1,0:T(8,128)(2,1)S(1)} collective-permute-done((bf16[1,128,512]{2,1,0:T(8,128)(2,1)S(1)}, bf16[1,128,512]{2,1,0:T(8,128)(2,1)S(1)}, u32[]{:S(2)}, u32[]{:S(2)}) %collective-permute-start.6) | collective-permute-done | bytes 131104 | tf_op jit(solution)/shard_map/ppermute | solution.py:617
  57.3 0.6 collective-permute-done.7
  58.0 3.4 %collective-permute-start.12 = (bf16[1,256,512]{2,1,0:T(8,128)(2,1)S(1)}, bf16[1,256,512]{2,1,0:T(8,128)(2,1)S(1)}, u32[]{:S(2)}, u32[]{:S(2)}) collective-permute-start(bf16[1,256,512]{2,1,0:T(8,128)(2,1)S(1)} %pad_maximum_fusion), channel_id=1, source_target_pairs={{0,16},{4,20},{8,24},{12,28},{16,0},{20,4},{24,8},{28,12},{1,17},{... | collective-permute-start | bytes 786440 | tf_op jit(solution)/shard_map/ppermute | solution.py:617
  61.4 3.3 %near_terms_to_keep.1 = (f32[2,128,512]{2,1,0:T(8,128)S(1)}, f32[2,128,512]{2,1,0:T(8,128)S(1)}) custom-call(s32[1]{0:T(128)} %bitcast.pos_ref, bf16[2048,512]{1,0:T(8,128)(2,1)} %get-tuple-element.75.refs_0_, bf16[2048,2048]{1,0:T(8,128)(2,1)} %refs_4_.5, bf16[2048,2048]{1,0:T(8,128)(2,1)} %refs_4_.5, bf16[2048,2048]{1,0:T(8,128)(2,1)} %refs_4_.5, ...), custom_call_target="tpu_custom_call" | custom-call | tf_op jit(solution)/shard_map/near_terms_to_keep/pallas_call | solution.py:539
  64.7 0.0 collective-permute-done.8
  64.7 0.1 convert_add_fusion.1
  64.8 0.0 copy-start
  64.8 0.0 copy-start.1
  64.8 0.0 copy-start.2
  64.9 0.4 collective-permute-start.9
  65.2 1.4 %collective-permute-done.10 = bf16[2,128,512]{2,1,0:T(8,128)(2,1)S(1)} collective-permute-done((bf16[2,128,512]{2,1,0:T(8,128)(2,1)S(1)}, bf16[2,128,512]{2,1,0:T(8,128)(2,1)S(1)}, u32[]{:S(2)}, u32[]{:S(2)}) %collective-permute-start.10) | collective-permute-done | bytes 262176 | tf_op jit(solution)/shard_map/ppermute | solution.py:617
  66.6 0.1 convert_add_fusion
  66.7 0.2 collective-permute-start.11
  66.9 3.4 %collective-permute-done.9 = bf16[1,128,512]{2,1,0:T(8,128)(2,1)S(1)} collective-permute-done((bf16[1,128,512]{2,1,0:T(8,128)(2,1)S(1)}, bf16[1,128,512]{2,1,0:T(8,128)(2,1)S(1)}, u32[]{:S(2)}, u32[]{:S(2)}) %collective-permute-start.9) | collective-permute-done | bytes 131104 | tf_op jit(solution)/shard_map/ppermute | solution.py:617
  70.3 1.4 %collective-permute-done.11 = bf16[1,128,512]{2,1,0:T(8,128)(2,1)S(1)} collective-permute-done((bf16[1,128,512]{2,1,0:T(8,128)(2,1)S(1)}, bf16[1,128,512]{2,1,0:T(8,128)(2,1)S(1)}, u32[]{:S(2)}, u32[]{:S(2)}) %collective-permute-start.11) | collective-permute-done | bytes 131104 | tf_op jit(solution)/shard_map/ppermute | solution.py:617
  71.8 0.0 collective-permute-done.12
  71.8 0.5 update_rows.1
  72.4 0.4 collective-permute-start.15
  72.9 4.3 %collective-permute-start.13 = (bf16[1,256,512]{2,1,0:T(8,128)(2,1)S(1)}, bf16[1,256,512]{2,1,0:T(8,128)(2,1)S(1)}, u32[]{:S(2)}, u32[]{:S(2)}) collective-permute-start(bf16[1,256,512]{2,1,0:T(8,128)(2,1)S(1)} %bitcast.21), channel_id=1, source_target_pairs={{0,16},{4,20},{8,24},{12,28},{16,0},{20,4},{24,8},{28,12},{1,17},{... | collective-permute-start | bytes 786440 | tf_op jit(solution)/shard_map/ppermute | solution.py:617
  77.2 0.0 collective-permute-start.14
  77.2 1.4 %collective-permute-done.15 = bf16[1,128,512]{2,1,0:T(8,128)(2,1)S(1)} collective-permute-done((bf16[1,128,512]{2,1,0:T(8,128)(2,1)S(1)}, bf16[1,128,512]{2,1,0:T(8,128)(2,1)S(1)}, u32[]{:S(2)}, u32[]{:S(2)}) %collective-permute-start.15) | collective-permute-done | bytes 131104 | tf_op jit(solution)/shard_map/ppermute | solution.py:617
  78.6 4.9 %collective-permute-done.14 = bf16[1,128,512]{2,1,0:T(8,128)(2,1)S(1)} collective-permute-done((bf16[1,128,512]{2,1,0:T(8,128)(2,1)S(1)}, bf16[1,128,512]{2,1,0:T(8,128)(2,1)S(1)}, u32[]{:S(2)}, u32[]{:S(2)}) %collective-permute-start.14) | collective-permute-done | bytes 131104 | tf_op jit(solution)/shard_map/ppermute | solution.py:617
  83.5 0.9 collective-permute-done.13
  84.5 0.1 collective-permute-start.16
  84.6 0.1 collective-permute-start.18
  84.6 2.0 %collective-permute-start.20 = (bf16[2,128,512]{2,1,0:T(8,128)(2,1)S(1)}, bf16[2,128,512]{2,1,0:T(8,128)(2,1)S(1)}, u32[]{:S(2)}, u32[]{:S(2)}) collective-permute-start(bf16[2,128,512]{2,1,0:T(8,128)(2,1)S(1)} %pad_maximum_fusion.2.refs_0_), channel_id=1, source_target_pairs={{0,4},{4,0},{8,12},{12,8},{16,20},{20,16},{24,28},{28,24},{1,5},{5... | collective-permute-start | bytes 786440 | tf_op jit(solution)/shard_map/ppermute | solution.py:617
  86.6 1.9 %collective-permute-start.21 = (bf16[2,128,512]{2,1,0:T(8,128)(2,1)S(1)}, bf16[2,128,512]{2,1,0:T(8,128)(2,1)S(1)}, u32[]{:S(2)}, u32[]{:S(2)}) collective-permute-start(bf16[2,128,512]{2,1,0:T(8,128)(2,1)S(1)} %pad_maximum_fusion.1.refs_2_), channel_id=1, source_target_pairs={{0,8},{4,12},{8,0},{12,4},{16,24},{20,28},{24,16},{28,20},{1,9},{5... | collective-permute-start | bytes 786440 | tf_op jit(solution)/shard_map/ppermute | solution.py:617
  88.6 2.3 %collective-permute-done.16 = bf16[1,128,512]{2,1,0:T(8,128)(2,1)S(1)} collective-permute-done((bf16[1,128,512]{2,1,0:T(8,128)(2,1)S(1)}, bf16[1,128,512]{2,1,0:T(8,128)(2,1)S(1)}, u32[]{:S(2)}, u32[]{:S(2)}) %collective-permute-start.16) | collective-permute-done | bytes 131104 | tf_op jit(solution)/shard_map/ppermute | solution.py:617
  90.9 0.1 collective-permute-start.17
  91.0 0.0 collective-permute-done.18
  91.1 0.6 collective-permute-start.19
  91.6 0.8 copy.21
  92.4 1.0 collective-permute-done.20.refs_1_
  93.4 0.7 collective-permute-done.21.refs_3_
  94.1 1.2 %placed_early.1.refs_2_ = bf16[2048,512]{1,0:T(8,128)(2,1)} custom-call(s32[1]{0:T(128)} %bitcast.pos_ref, bf16[2,128,512]{2,1,0:T(8,128)(2,1)S(1)} %pad_maximum_fusion.2.refs_0_, bf16[2,128,512]{2,1,0:T(8,128)(2,1)S(1)} %collective-permute-done.20.refs_1_, bf16[2,128,512]{2,1,0:T(8,128)(2,1)S(1)} %pad_maximum_fusion.1.refs_2_, ...), custom_call_target="tpu_custom_call" | custom-call | tf_op jit(solution)/shard_map/placed_early/pallas_call | solution.py:578
  95.3 2.1 %collective-permute-done.17.refs_0_ = bf16[2,128,512]{2,1,0:T(8,128)(2,1)S(1)} collective-permute-done((bf16[2,128,512]{2,1,0:T(8,128)(2,1)S(1)}, bf16[2,128,512]{2,1,0:T(8,128)(2,1)S(1)}, u32[]{:S(2)}, u32[]{:S(2)}) %collective-permute-start.17) | collective-permute-done | bytes 262176 | tf_op jit(solution)/shard_map/ppermute | solution.py:617
  97.4 0.1 collective-permute-done.19.refs_1_
  97.5 0.8 placed_late.1
  (25 shorter events, 0.5 us)
Async XLA Ops:
  4.3 11.5 %collective-permute-start.2 = (bf16[544,128]{1,0:T(8,128)(2,1)}, bf16[544,128]{1,0:T(8,128)(2,1)S(1)}, u32[]{:S(2)}, u32[]{:S(2)}) collective-permute-start(bf16[544,128]{1,0:T(8,128)(2,1)} %get-tuple-element.45), channel_id=1, source_target_pairs={{0,12},{4,8},{8,4},{12,0},{16,28},{20,24},{24,20},{28,16},{1,13},{... | collective-permute-start | bytes 417800 | tf_op jit(solution)/shard_map/ppermute | solution.py:617
  8.3 7.5 %collective-permute-start.1 = (bf16[544,128]{1,0:T(8,128)(2,1)}, bf16[544,128]{1,0:T(8,128)(2,1)}, u32[]{:S(2)}, u32[]{:S(2)}) collective-permute-start(bf16[544,128]{1,0:T(8,128)(2,1)} %get-tuple-element.45), channel_id=1, source_target_pairs={{0,8},{4,12},{8,0},{12,4},{16,24},{20,28},{24,16},{28,20},{1,9},{5... | collective-permute-start | bytes 417800 | tf_op jit(solution)/shard_map/ppermute | solution.py:617
  8.8 7.1 %collective-permute-start = (bf16[544,128]{1,0:T(8,128)(2,1)}, bf16[544,128]{1,0:T(8,128)(2,1)}, u32[]{:S(2)}, u32[]{:S(2)}) collective-permute-start(bf16[544,128]{1,0:T(8,128)(2,1)} %get-tuple-element.45), channel_id=1, source_target_pairs={{0,4},{4,0},{8,12},{12,8},{16,20},{20,16},{24,28},{28,24},{1,5},{5... | collective-permute-start | bytes 417800 | tf_op jit(solution)/shard_map/ppermute | solution.py:617
  17.0 8.8 %collective-permute-start.3 = (bf16[544,128]{1,0:T(8,128)(2,1)S(1)}, bf16[544,128]{1,0:T(8,128)(2,1)S(1)}, u32[]{:S(2)}, u32[]{:S(2)}) collective-permute-start(bf16[544,128]{1,0:T(8,128)(2,1)S(1)} %get-tuple-element.61), channel_id=1, source_target_pairs={{0,16},{4,20},{8,24},{12,28},{16,0},{20,4},{24,8},{28,12},{1,17},{... | collective-permute-start | bytes 417800 | tf_op jit(solution)/shard_map/ppermute | solution.py:617
  25.8 9.9 %copy-start.3 = (f32[512]{0:T(512)S(1)}, f32[512]{0:T(512)}, u32[]{:S(2)}) copy-start(f32[512]{0:T(512)} %param.21) | copy-start | bytes 6148
  40.6 8.6 %collective-permute-start.4 = (bf16[2,128,512]{2,1,0:T(8,128)(2,1)S(1)}, bf16[2,128,512]{2,1,0:T(8,128)(2,1)S(1)}, u32[]{:S(2)}, u32[]{:S(2)}) collective-permute-start(bf16[2,128,512]{2,1,0:T(8,128)(2,1)S(1)} %get-tuple-element.66), channel_id=1, source_target_pairs={{0,4},{4,0},{8,12},{12,8},{16,20},{20,16},{24,28},{28,24},{1,5},{5... | collective-permute-start | bytes 786440 | tf_op jit(solution)/shard_map/ppermute | solution.py:617
  42.5 8.3 %collective-permute-start.5 = (bf16[2,128,512]{2,1,0:T(8,128)(2,1)S(1)}, bf16[2,128,512]{2,1,0:T(8,128)(2,1)S(1)}, u32[]{:S(2)}, u32[]{:S(2)}) collective-permute-start(bf16[2,128,512]{2,1,0:T(8,128)(2,1)S(1)} %get-tuple-element.68), channel_id=1, source_target_pairs={{0,8},{4,12},{8,0},{12,4},{16,24},{20,28},{24,16},{28,20},{1,9},{5... | collective-permute-start | bytes 786440 | tf_op jit(solution)/shard_map/ppermute | solution.py:617
  50.9 6.4 %collective-permute-start.6 = (bf16[1,128,512]{2,1,0:T(8,128)(2,1)S(1)}, bf16[1,128,512]{2,1,0:T(8,128)(2,1)S(1)}, u32[]{:S(2)}, u32[]{:S(2)}) collective-permute-start(bf16[1,128,512]{2,1,0:T(8,128)(2,1)S(1)} %slice.77), channel_id=1, source_target_pairs={{0,8},{4,12},{8,0},{12,4},{16,24},{20,28},{24,16},{28,20},{1,9},{5... | collective-permute-start | bytes 393224 | tf_op jit(solution)/shard_map/ppermute | solution.py:617
  51.5 6.4 %collective-permute-start.7 = (bf16[1,128,512]{2,1,0:T(8,128)(2,1)S(1)}, bf16[1,128,512]{2,1,0:T(8,128)(2,1)S(1)}, u32[]{:S(2)}, u32[]{:S(2)}) collective-permute-start(bf16[1,128,512]{2,1,0:T(8,128)(2,1)S(1)} %slice.76), channel_id=1, source_target_pairs={{0,4},{4,0},{8,12},{12,8},{16,20},{20,16},{24,28},{28,24},{1,5},{5... | collective-permute-start | bytes 393224 | tf_op jit(solution)/shard_map/ppermute | solution.py:617
  51.9 12.8 %collective-permute-start.8 = (bf16[2,128,512]{2,1,0:T(8,128)(2,1)S(1)}, bf16[2,128,512]{2,1,0:T(8,128)(2,1)S(1)}, u32[]{:S(2)}, u32[]{:S(2)}) collective-permute-start(bf16[2,128,512]{2,1,0:T(8,128)(2,1)S(1)} %get-tuple-element.77), channel_id=1, source_target_pairs={{0,4},{4,0},{8,12},{12,8},{16,20},{20,16},{24,28},{28,24},{1,5},{5... | collective-permute-start | bytes 786440 | tf_op jit(solution)/shard_map/ppermute | solution.py:617
  53.5 13.0 %collective-permute-start.10 = (bf16[2,128,512]{2,1,0:T(8,128)(2,1)S(1)}, bf16[2,128,512]{2,1,0:T(8,128)(2,1)S(1)}, u32[]{:S(2)}, u32[]{:S(2)}) collective-permute-start(bf16[2,128,512]{2,1,0:T(8,128)(2,1)S(1)} %get-tuple-element.79), channel_id=1, source_target_pairs={{0,8},{4,12},{8,0},{12,4},{16,24},{20,28},{24,16},{28,20},{1,9},{5... | collective-permute-start | bytes 786440 | tf_op jit(solution)/shard_map/ppermute | solution.py:617
  58.0 13.8 %collective-permute-start.12 = (bf16[1,256,512]{2,1,0:T(8,128)(2,1)S(1)}, bf16[1,256,512]{2,1,0:T(8,128)(2,1)S(1)}, u32[]{:S(2)}, u32[]{:S(2)}) collective-permute-start(bf16[1,256,512]{2,1,0:T(8,128)(2,1)S(1)} %pad_maximum_fusion), channel_id=1, source_target_pairs={{0,16},{4,20},{8,24},{12,28},{16,0},{20,4},{24,8},{28,12},{1,17},{... | collective-permute-start | bytes 786440 | tf_op jit(solution)/shard_map/ppermute | solution.py:617
  64.8 7.0 %copy-start = (f32[256,512]{1,0:T(8,128)S(1)}, f32[256,512]{1,0:T(8,128)}, u32[]{:S(2)}) copy-start(f32[256,512]{1,0:T(8,128)} %master_ref.1) | copy-start | bytes 1572868
  64.8 7.0 %copy-start.1 = (f32[256,512]{1,0:T(8,128)S(1)}, f32[256,512]{1,0:T(8,128)}, u32[]{:S(2)}) copy-start(f32[256,512]{1,0:T(8,128)} %one_ref.1) | copy-start | bytes 1572868
  64.8 7.0 %copy-start.2 = (f32[256,512]{1,0:T(8,128)S(1)}, f32[256,512]{1,0:T(8,128)}, u32[]{:S(2)}) copy-start(f32[256,512]{1,0:T(8,128)} %two_ref.1) | copy-start | bytes 1572868
  64.9 5.4 %collective-permute-start.9 = (bf16[1,128,512]{2,1,0:T(8,128)(2,1)S(1)}, bf16[1,128,512]{2,1,0:T(8,128)(2,1)S(1)}, u32[]{:S(2)}, u32[]{:S(2)}) collective-permute-start(bf16[1,128,512]{2,1,0:T(8,128)(2,1)S(1)} %slice.75), channel_id=1, source_target_pairs={{0,8},{4,12},{8,0},{12,4},{16,24},{20,28},{24,16},{28,20},{1,9},{5... | collective-permute-start | bytes 393224 | tf_op jit(solution)/shard_map/ppermute | solution.py:617
  66.7 5.0 %collective-permute-start.11 = (bf16[1,128,512]{2,1,0:T(8,128)(2,1)S(1)}, bf16[1,128,512]{2,1,0:T(8,128)(2,1)S(1)}, u32[]{:S(2)}, u32[]{:S(2)}) collective-permute-start(bf16[1,128,512]{2,1,0:T(8,128)(2,1)S(1)} %slice.74), channel_id=1, source_target_pairs={{0,4},{4,0},{8,12},{12,8},{16,20},{20,16},{24,28},{28,24},{1,5},{5... | collective-permute-start | bytes 393224 | tf_op jit(solution)/shard_map/ppermute | solution.py:617
  72.4 6.2 %collective-permute-start.15 = (bf16[1,128,512]{2,1,0:T(8,128)(2,1)S(1)}, bf16[1,128,512]{2,1,0:T(8,128)(2,1)S(1)}, u32[]{:S(2)}, u32[]{:S(2)}) collective-permute-start(bf16[1,128,512]{2,1,0:T(8,128)(2,1)S(1)} %get-tuple-element.89), channel_id=1, source_target_pairs={{0,8},{4,12},{8,0},{12,4},{16,24},{20,28},{24,16},{28,20},{1,9},{5... | collective-permute-start | bytes 393224 | tf_op jit(solution)/shard_map/ppermute | solution.py:617
  72.9 11.6 %collective-permute-start.13 = (bf16[1,256,512]{2,1,0:T(8,128)(2,1)S(1)}, bf16[1,256,512]{2,1,0:T(8,128)(2,1)S(1)}, u32[]{:S(2)}, u32[]{:S(2)}) collective-permute-start(bf16[1,256,512]{2,1,0:T(8,128)(2,1)S(1)} %bitcast.21), channel_id=1, source_target_pairs={{0,16},{4,20},{8,24},{12,28},{16,0},{20,4},{24,8},{28,12},{1,17},{... | collective-permute-start | bytes 786440 | tf_op jit(solution)/shard_map/ppermute | solution.py:617
  77.2 6.3 %collective-permute-start.14 = (bf16[1,128,512]{2,1,0:T(8,128)(2,1)S(1)}, bf16[1,128,512]{2,1,0:T(8,128)(2,1)S(1)}, u32[]{:S(2)}, u32[]{:S(2)}) collective-permute-start(bf16[1,128,512]{2,1,0:T(8,128)(2,1)S(1)} %get-tuple-element.90), channel_id=1, source_target_pairs={{0,4},{4,0},{8,12},{12,8},{16,20},{20,16},{24,28},{28,24},{1,5},{5... | collective-permute-start | bytes 393224 | tf_op jit(solution)/shard_map/ppermute | solution.py:617
  84.5 6.4 %collective-permute-start.16 = (bf16[1,128,512]{2,1,0:T(8,128)(2,1)S(1)}, bf16[1,128,512]{2,1,0:T(8,128)(2,1)S(1)}, u32[]{:S(2)}, u32[]{:S(2)}) collective-permute-start(bf16[1,128,512]{2,1,0:T(8,128)(2,1)S(1)} %get-tuple-element.88), channel_id=1, source_target_pairs={{0,8},{4,12},{8,0},{12,4},{16,24},{20,28},{24,16},{28,20},{1,9},{5... | collective-permute-start | bytes 393224 | tf_op jit(solution)/shard_map/ppermute | solution.py:617
  84.6 6.5 %collective-permute-start.18 = (bf16[1,128,512]{2,1,0:T(8,128)(2,1)S(1)}, bf16[1,128,512]{2,1,0:T(8,128)(2,1)S(1)}, u32[]{:S(2)}, u32[]{:S(2)}) collective-permute-start(bf16[1,128,512]{2,1,0:T(8,128)(2,1)S(1)} %get-tuple-element.87), channel_id=1, source_target_pairs={{0,4},{4,0},{8,12},{12,8},{16,20},{20,16},{24,28},{28,24},{1,5},{5... | collective-permute-start | bytes 393224 | tf_op jit(solution)/shard_map/ppermute | solution.py:617
  84.6 8.8 %collective-permute-start.20 = (bf16[2,128,512]{2,1,0:T(8,128)(2,1)S(1)}, bf16[2,128,512]{2,1,0:T(8,128)(2,1)S(1)}, u32[]{:S(2)}, u32[]{:S(2)}) collective-permute-start(bf16[2,128,512]{2,1,0:T(8,128)(2,1)S(1)} %pad_maximum_fusion.2.refs_0_), channel_id=1, source_target_pairs={{0,4},{4,0},{8,12},{12,8},{16,20},{20,16},{24,28},{28,24},{1,5},{5... | collective-permute-start | bytes 786440 | tf_op jit(solution)/shard_map/ppermute | solution.py:617
  86.6 7.4 %collective-permute-start.21 = (bf16[2,128,512]{2,1,0:T(8,128)(2,1)S(1)}, bf16[2,128,512]{2,1,0:T(8,128)(2,1)S(1)}, u32[]{:S(2)}, u32[]{:S(2)}) collective-permute-start(bf16[2,128,512]{2,1,0:T(8,128)(2,1)S(1)} %pad_maximum_fusion.1.refs_2_), channel_id=1, source_target_pairs={{0,8},{4,12},{8,0},{12,4},{16,24},{20,28},{24,16},{28,20},{1,9},{5... | collective-permute-start | bytes 786440 | tf_op jit(solution)/shard_map/ppermute | solution.py:617
  90.9 6.4 %collective-permute-start.17 = (bf16[2,128,512]{2,1,0:T(8,128)(2,1)S(1)}, bf16[2,128,512]{2,1,0:T(8,128)(2,1)S(1)}, u32[]{:S(2)}, u32[]{:S(2)}) collective-permute-start(bf16[2,128,512]{2,1,0:T(8,128)(2,1)S(1)} %pad_maximum_fusion.3.refs_4_), channel_id=1, source_target_pairs={{0,4},{4,0},{8,12},{12,8},{16,20},{20,16},{24,28},{28,24},{1,5},{5... | collective-permute-start | bytes 786440 | tf_op jit(solution)/shard_map/ppermute | solution.py:617
  91.1 6.4 %collective-permute-start.19 = (bf16[2,128,512]{2,1,0:T(8,128)(2,1)S(1)}, bf16[2,128,512]{2,1,0:T(8,128)(2,1)S(1)}, u32[]{:S(2)}, u32[]{:S(2)}) collective-permute-start(bf16[2,128,512]{2,1,0:T(8,128)(2,1)S(1)} %pad_maximum_fusion.4.refs_5_), channel_id=1, source_target_pairs={{0,8},{4,12},{8,0},{12,4},{16,24},{20,28},{24,16},{28,20},{1,9},{5... | collective-permute-start | bytes 786440 | tf_op jit(solution)/shard_map/ppermute | solution.py:617

commit v5 on v4

--- a/solution.py
+++ b/solution.py
@@ -309,8 +309,8 @@
             lows.append(rest)
         weighted, rest = jnp.concatenate(highs, axis=0), jnp.concatenate(lows, axis=0)
         total = mm(
-            jnp.concatenate([weighted, weighted, rest], axis=1),
-            jnp.concatenate([high, low, high], axis=0),
+            jnp.concatenate([weighted, rest], axis=1),
+            jnp.concatenate([high, high], axis=0),
         ) + mm(state_ref[block], readout, TRANSPOSED_RHS)
         z_turned = z_ref[part].T
         gating_ref[:, part] = z_turned

time: 98.6 us -> 98.6 us (level)
  transfers between devices with their start and end apart: 22 -> 22, of which waited for: 16 -> 16; matrix products, arithmetic and copies ran while one was open for 1% -> 1% of each run, Pallas kernels for 17% -> 16%
where the time goes in v5:
time: 98.6 us; the launch traced here: 98.3 us
  Pallas kernels  31.6 us (32%)
  waiting for transfers between devices  30.9 us (31%)
  starting transfers between devices  28 us (28%)
  blocking collectives  5.19 us (5%)
  local copies, waits for them, and re-layouts  0.99 us (1%)
    ppermute x22, waiting for transfers between devices, flipped(): return lax.ppermute(block, axis, [(i, i ^ mask) for i in range(count)])  30.9 us
    ppermute x22, starting transfers between devices, flipped(): return lax.ppermute(block, axis, [(i, i ^ mask) for i in range(count)])  28 us
    pallas_call x3, Pallas kernels, terms_call(): pl.pallas_call(functools.partial(terms_kernel, channels), grid_spec=pltpu...  13 us
    pallas_call x1, Pallas kernels, within_blocks(): pl.pallas_call(within_kernel, grid=(length // tile,), in_specs=[by_rows(w...  6.49 us
    all_gather x1, blocking collectives, on_device(): sums = lax.all_gather(sums[0], 'head', axis=0, tiled=False)  5.19 us
    pallas_call x1, Pallas kernels, across_levels(): pl.pallas_call(functools.partial(across_kernel, len(levels)), grid=(lengt...  4.71 us
    pallas_call x1, Pallas kernels, segment_states(): pl.pallas_call(states_kernel, grid=(length // tile,), in_specs=[pl.BlockS...  3.63 us
    pallas_call x2, Pallas kernels, placed(): pl.pallas_call(functools.partial(place_kernel, slots, rows), in_specs=[pl...  2.05 us
  transfers between devices with their start and end apart: 22, of which 16 were waited for; matrix products, arithmetic and copies ran while one was open for 1% of the time, Pallas kernels for 16%

profile of v5, /device:TPU:0, one launch (start us, length us, event | category | flops | bytes accessed | tf_op | source)
XLA Modules:
  0.0 98.3 jit_solution(926481012699273890)
XLA Ops:
  0.6 3.6 %segment_states.1 = (bf16[8,512,128]{2,1,0:T(8,128)(2,1)S(1)}, f32[8,2048]{1,0:T(8,128)}, f32[8,2048]{1,0:T(8,128)}, f32[512,128]{1,0:T(8,128)S(1)}, f32[8,128]{1,0:T(8,128)S(1)}, /*index=5*/bf16[544,128]{1,0:T(8,128)(2,1)}) custom-call(bf16[2048,512]{1,0:T(8,128)(2,1)} %x_ref.3, bf16[2048,128]{1,0:T(8,128)(2,1)} %b_ref.3, f32[8,2048]{1,0:T(8,128)} %dt_ref.3, ...), custom_call_target="tpu_custom_call" | custom-call | tf_op jit(solution)/shard_map/segment_states/pallas_call | solution.py:131
  4.3 4.0 %collective-permute-start.2 = (bf16[544,128]{1,0:T(8,128)(2,1)}, bf16[544,128]{1,0:T(8,128)(2,1)S(1)}, u32[]{:S(2)}, u32[]{:S(2)}) collective-permute-start(bf16[544,128]{1,0:T(8,128)(2,1)} %get-tuple-element.45), channel_id=1, source_target_pairs={{0,12},{4,8},{8,4},{12,0},{16,28},{20,24},{24,20},{28,16},{1,13},{... | collective-permute-start | bytes 417800 | tf_op jit(solution)/shard_map/ppermute | solution.py:617
  8.3 0.5 collective-permute-start.1
  8.8 0.2 collective-permute-start
  8.9 6.5 %within_blocks.1 = (bf16[512,2048]{1,0:T(8,128)(2,1)S(1)}, bf16[512,2048]{1,0:T(8,128)(2,1)}) custom-call(bf16[2048,512]{1,0:T(8,128)(2,1)} %x_ref.3, bf16[2048,512]{1,0:T(8,128)(2,1)} %z_ref.1, bf16[2048,128]{1,0:T(8,128)(2,1)} %b_ref.3, bf16[2048,128]{1,0:T(8,128)(2,1)} %c_ref.3, f32[8,2048]{1,0:T(8,128)} %dt_ref.3, ...), custom_call_target="tpu_custom_call" | custom-call | tf_op jit(solution)/shard_map/within_blocks/pallas_call | solution.py:331
  15.4 0.0 collective-permute-done.2.got_three
  15.4 0.0 collective-permute-done.1.got_two
  15.5 0.0 collective-permute-done.got_one
  15.5 1.1 %near_levels.1 = (bf16[512,128]{1,0:T(8,128)(2,1)S(1)}, bf16[512,128]{1,0:T(8,128)(2,1)S(1)}, bf16[544,128]{1,0:T(8,128)(2,1)S(1)}, f32[8,128]{1,0:T(8,128)S(1)}) custom-call(s32[1]{0:T(128)} %bitcast.pos_ref, bf16[544,128]{1,0:T(8,128)(2,1)} %collective-permute-done.got_one, bf16[544,128]{1,0:T(8,128)(2,1)} %collective-permute-done.1.got_two, ...), custom_call_target="tpu_custom_call" | custom-call | tf_op jit(solution)/shard_map/near_levels/pallas_call | solution.py:252
  16.6 3.0 %collective-permute-start.3 = (bf16[544,128]{1,0:T(8,128)(2,1)S(1)}, bf16[544,128]{1,0:T(8,128)(2,1)S(1)}, u32[]{:S(2)}, u32[]{:S(2)}) collective-permute-start(bf16[544,128]{1,0:T(8,128)(2,1)S(1)} %get-tuple-element.61), channel_id=1, source_target_pairs={{0,16},{4,20},{8,24},{12,28},{16,0},{20,4},{24,8},{28,12},{1,17},{... | collective-permute-start | bytes 417800 | tf_op jit(solution)/shard_map/ppermute | solution.py:617
  19.6 5.8 %collective-permute-done.3 = bf16[544,128]{1,0:T(8,128)(2,1)S(1)} collective-permute-done((bf16[544,128]{1,0:T(8,128)(2,1)S(1)}, bf16[544,128]{1,0:T(8,128)(2,1)S(1)}, u32[]{:S(2)}, u32[]{:S(2)}) %collective-permute-start.3) | collective-permute-done | bytes 139296 | tf_op jit(solution)/shard_map/ppermute | solution.py:617
  25.5 0.0 copy-start.3
  25.5 4.7 %across_levels.1 = (bf16[2048,512]{1,0:T(8,128)(2,1)S(1)}, f32[1,2048]{1,0:T(1,128)S(1)}) custom-call(bf16[512,2048]{1,0:T(8,128)(2,1)S(1)} %get-tuple-element.50.base_ref, bf16[512,2048]{1,0:T(8,128)(2,1)} %get-tuple-element.51.z_ref, bf16[2048,128]{1,0:T(8,128)(2,1)} %c_ref.3, f32[5,8,2048]{2,1,0:T(8,128)} %bitcast.25, ...), custom_call_target="tpu_custom_call" | custom-call | tf_op jit(solution)/shard_map/across_levels/pallas_call | solution.py:390
  30.2 5.2 %all-gather = f32[4,1,2048]{2,1,0:T(1,128)S(1)} all-gather(f32[1,1,2048]{2,1,0:T(1,128)S(1)} %bitcast.23), channel_id=1, replica_groups=mesh['ctx'=8,'head'=4] {'head'}, dimensions={0}, use_global_device_ids=true | all-gather | bytes 40960 | tf_op jit(solution)/shard_map/all_gather | solution.py:687
  35.4 4.9 %far_terms_to_send.1 = (bf16[2048,512]{1,0:T(8,128)(2,1)}, bf16[2,128,512]{2,1,0:T(8,128)(2,1)S(1)}, bf16[2,128,512]{2,1,0:T(8,128)(2,1)S(1)}) custom-call(s32[1]{0:T(128)} %bitcast.pos_ref, bf16[2048,512]{1,0:T(8,128)(2,1)S(1)} %get-tuple-element.62.refs_0_, f32[4,2048]{1,0:T(4,128)S(1)} %bitcast.22, f32[1,512]{1,0:T(1,128)S(1)} %bitcast.24, ...), custom_call_target="tpu_custom_call" | custom-call | tf_op jit(solution)/shard_map/far_terms_to_send/pallas_call | solution.py:539
  40.3 2.1 %collective-permute-start.4 = (bf16[2,128,512]{2,1,0:T(8,128)(2,1)S(1)}, bf16[2,128,512]{2,1,0:T(8,128)(2,1)S(1)}, u32[]{:S(2)}, u32[]{:S(2)}) collective-permute-start(bf16[2,128,512]{2,1,0:T(8,128)(2,1)S(1)} %get-tuple-element.66), channel_id=1, source_target_pairs={{0,4},{4,0},{8,12},{12,8},{16,20},{20,16},{24,28},{28,24},{1,5},{5... | collective-permute-start | bytes 786440 | tf_op jit(solution)/shard_map/ppermute | solution.py:617
  42.5 0.6 collective-permute-start.5
  43.0 4.9 %far_terms_to_keep.1 = (f32[2,128,512]{2,1,0:T(8,128)S(1)}, f32[2,128,512]{2,1,0:T(8,128)S(1)}, bf16[2,128,512]{2,1,0:T(8,128)(2,1)S(1)}, bf16[2,128,512]{2,1,0:T(8,128)(2,1)S(1)}) custom-call(s32[1]{0:T(128)} %bitcast.pos_ref, bf16[2048,512]{1,0:T(8,128)(2,1)} %get-tuple-element.75.refs_0_, bf16[2048,2048]{1,0:T(8,128)(2,1)} %refs_4_.5, ...), custom_call_target="tpu_custom_call" | custom-call | tf_op jit(solution)/shard_map/far_terms_to_keep/pallas_call | solution.py:539
  48.0 1.3 %collective-permute-done.4 = bf16[2,128,512]{2,1,0:T(8,128)(2,1)S(1)} collective-permute-done((bf16[2,128,512]{2,1,0:T(8,128)(2,1)S(1)}, bf16[2,128,512]{2,1,0:T(8,128)(2,1)S(1)}, u32[]{:S(2)}, u32[]{:S(2)}) %collective-permute-start.4) | collective-permute-done | bytes 262176 | tf_op jit(solution)/shard_map/ppermute | solution.py:617
  49.3 0.1 convert_add_fusion.3
  49.4 1.3 %collective-permute-done.5 = bf16[2,128,512]{2,1,0:T(8,128)(2,1)S(1)} collective-permute-done((bf16[2,128,512]{2,1,0:T(8,128)(2,1)S(1)}, bf16[2,128,512]{2,1,0:T(8,128)(2,1)S(1)}, u32[]{:S(2)}, u32[]{:S(2)}) %collective-permute-start.5) | collective-permute-done | bytes 262176 | tf_op jit(solution)/shard_map/ppermute | solution.py:617
  50.7 0.1 convert_add_fusion.2
  50.9 0.6 collective-permute-start.6
  51.5 0.4 collective-permute-start.7
  51.9 1.6 %collective-permute-start.8 = (bf16[2,128,512]{2,1,0:T(8,128)(2,1)S(1)}, bf16[2,128,512]{2,1,0:T(8,128)(2,1)S(1)}, u32[]{:S(2)}, u32[]{:S(2)}) collective-permute-start(bf16[2,128,512]{2,1,0:T(8,128)(2,1)S(1)} %get-tuple-element.77), channel_id=1, source_target_pairs={{0,4},{4,0},{8,12},{12,8},{16,20},{20,16},{24,28},{28,24},{1,5},{5... | collective-permute-start | bytes 786440 | tf_op jit(solution)/shard_map/ppermute | solution.py:617
  53.5 1.4 %collective-permute-start.10 = (bf16[2,128,512]{2,1,0:T(8,128)(2,1)S(1)}, bf16[2,128,512]{2,1,0:T(8,128)(2,1)S(1)}, u32[]{:S(2)}, u32[]{:S(2)}) collective-permute-start(bf16[2,128,512]{2,1,0:T(8,128)(2,1)S(1)} %get-tuple-element.79), channel_id=1, source_target_pairs={{0,8},{4,12},{8,0},{12,4},{16,24},{20,28},{24,16},{28,20},{1,9},{5... | collective-permute-start | bytes 786440 | tf_op jit(solution)/shard_map/ppermute | solution.py:617
  55.0 2.3 %collective-permute-done.6 = bf16[1,128,512]{2,1,0:T(8,128)(2,1)S(1)} collective-permute-done((bf16[1,128,512]{2,1,0:T(8,128)(2,1)S(1)}, bf16[1,128,512]{2,1,0:T(8,128)(2,1)S(1)}, u32[]{:S(2)}, u32[]{:S(2)}) %collective-permute-start.6) | collective-permute-done | bytes 131104 | tf_op jit(solution)/shard_map/ppermute | solution.py:617
  57.3 0.6 collective-permute-done.7
  58.0 3.4 %collective-permute-start.12 = (bf16[1,256,512]{2,1,0:T(8,128)(2,1)S(1)}, bf16[1,256,512]{2,1,0:T(8,128)(2,1)S(1)}, u32[]{:S(2)}, u32[]{:S(2)}) collective-permute-start(bf16[1,256,512]{2,1,0:T(8,128)(2,1)S(1)} %pad_maximum_fusion), channel_id=1, source_target_pairs={{0,16},{4,20},{8,24},{12,28},{16,0},{20,4},{24,8},{28,12},{1,17},{... | collective-permute-start | bytes 786440 | tf_op jit(solution)/shard_map/ppermute | solution.py:617
  61.4 3.3 %near_terms_to_keep.1 = (f32[2,128,512]{2,1,0:T(8,128)S(1)}, f32[2,128,512]{2,1,0:T(8,128)S(1)}) custom-call(s32[1]{0:T(128)} %bitcast.pos_ref, bf16[2048,512]{1,0:T(8,128)(2,1)} %get-tuple-element.75.refs_0_, bf16[2048,2048]{1,0:T(8,128)(2,1)} %refs_4_.5, bf16[2048,2048]{1,0:T(8,128)(2,1)} %refs_4_.5, bf16[2048,2048]{1,0:T(8,128)(2,1)} %refs_4_.5, ...), custom_call_target="tpu_custom_call" | custom-call | tf_op jit(solution)/shard_map/near_terms_to_keep/pallas_call | solution.py:539
  64.7 0.0 collective-permute-done.8
  64.7 0.1 convert_add_fusion.1
  64.8 0.0 copy-start
  64.8 0.0 copy-start.1
  64.8 0.0 copy-start.2
  64.9 0.4 collective-permute-start.9
  65.2 1.4 %collective-permute-done.10 = bf16[2,128,512]{2,1,0:T(8,128)(2,1)S(1)} collective-permute-done((bf16[2,128,512]{2,1,0:T(8,128)(2,1)S(1)}, bf16[2,128,512]{2,1,0:T(8,128)(2,1)S(1)}, u32[]{:S(2)}, u32[]{:S(2)}) %collective-permute-start.10) | collective-permute-done | bytes 262176 | tf_op jit(solution)/shard_map/ppermute | solution.py:617
  66.6 0.1 convert_add_fusion
  66.7 0.2 collective-permute-start.11
  66.9 3.4 %collective-permute-done.9 = bf16[1,128,512]{2,1,0:T(8,128)(2,1)S(1)} collective-permute-done((bf16[1,128,512]{2,1,0:T(8,128)(2,1)S(1)}, bf16[1,128,512]{2,1,0:T(8,128)(2,1)S(1)}, u32[]{:S(2)}, u32[]{:S(2)}) %collective-permute-start.9) | collective-permute-done | bytes 131104 | tf_op jit(solution)/shard_map/ppermute | solution.py:617
  70.3 1.4 %collective-permute-done.11 = bf16[1,128,512]{2,1,0:T(8,128)(2,1)S(1)} collective-permute-done((bf16[1,128,512]{2,1,0:T(8,128)(2,1)S(1)}, bf16[1,128,512]{2,1,0:T(8,128)(2,1)S(1)}, u32[]{:S(2)}, u32[]{:S(2)}) %collective-permute-start.11) | collective-permute-done | bytes 131104 | tf_op jit(solution)/shard_map/ppermute | solution.py:617
  71.8 0.0 collective-permute-done.12
  71.8 0.5 update_rows.1
  72.4 0.4 collective-permute-start.15
  72.9 4.3 %collective-permute-start.13 = (bf16[1,256,512]{2,1,0:T(8,128)(2,1)S(1)}, bf16[1,256,512]{2,1,0:T(8,128)(2,1)S(1)}, u32[]{:S(2)}, u32[]{:S(2)}) collective-permute-start(bf16[1,256,512]{2,1,0:T(8,128)(2,1)S(1)} %bitcast.21), channel_id=1, source_target_pairs={{0,16},{4,20},{8,24},{12,28},{16,0},{20,4},{24,8},{28,12},{1,17},{... | collective-permute-start | bytes 786440 | tf_op jit(solution)/shard_map/ppermute | solution.py:617
  77.2 0.0 collective-permute-start.14
  77.2 1.4 %collective-permute-done.15 = bf16[1,128,512]{2,1,0:T(8,128)(2,1)S(1)} collective-permute-done((bf16[1,128,512]{2,1,0:T(8,128)(2,1)S(1)}, bf16[1,128,512]{2,1,0:T(8,128)(2,1)S(1)}, u32[]{:S(2)}, u32[]{:S(2)}) %collective-permute-start.15) | collective-permute-done | bytes 131104 | tf_op jit(solution)/shard_map/ppermute | solution.py:617
  78.6 4.9 %collective-permute-done.14 = bf16[1,128,512]{2,1,0:T(8,128)(2,1)S(1)} collective-permute-done((bf16[1,128,512]{2,1,0:T(8,128)(2,1)S(1)}, bf16[1,128,512]{2,1,0:T(8,128)(2,1)S(1)}, u32[]{:S(2)}, u32[]{:S(2)}) %collective-permute-start.14) | collective-permute-done | bytes 131104 | tf_op jit(solution)/shard_map/ppermute | solution.py:617
  83.5 0.9 collective-permute-done.13
  84.5 0.1 collective-permute-start.16
  84.6 0.1 collective-permute-start.18
  84.6 2.0 %collective-permute-start.20 = (bf16[2,128,512]{2,1,0:T(8,128)(2,1)S(1)}, bf16[2,128,512]{2,1,0:T(8,128)(2,1)S(1)}, u32[]{:S(2)}, u32[]{:S(2)}) collective-permute-start(bf16[2,128,512]{2,1,0:T(8,128)(2,1)S(1)} %pad_maximum_fusion.2.refs_0_), channel_id=1, source_target_pairs={{0,4},{4,0},{8,12},{12,8},{16,20},{20,16},{24,28},{28,24},{1,5},{5... | collective-permute-start | bytes 786440 | tf_op jit(solution)/shard_map/ppermute | solution.py:617
  86.6 1.9 %collective-permute-start.21 = (bf16[2,128,512]{2,1,0:T(8,128)(2,1)S(1)}, bf16[2,128,512]{2,1,0:T(8,128)(2,1)S(1)}, u32[]{:S(2)}, u32[]{:S(2)}) collective-permute-start(bf16[2,128,512]{2,1,0:T(8,128)(2,1)S(1)} %pad_maximum_fusion.1.refs_2_), channel_id=1, source_target_pairs={{0,8},{4,12},{8,0},{12,4},{16,24},{20,28},{24,16},{28,20},{1,9},{5... | collective-permute-start | bytes 786440 | tf_op jit(solution)/shard_map/ppermute | solution.py:617
  88.6 2.3 %collective-permute-done.16 = bf16[1,128,512]{2,1,0:T(8,128)(2,1)S(1)} collective-permute-done((bf16[1,128,512]{2,1,0:T(8,128)(2,1)S(1)}, bf16[1,128,512]{2,1,0:T(8,128)(2,1)S(1)}, u32[]{:S(2)}, u32[]{:S(2)}) %collective-permute-start.16) | collective-permute-done | bytes 131104 | tf_op jit(solution)/shard_map/ppermute | solution.py:617
  90.9 0.1 collective-permute-start.17
  91.0 0.0 collective-permute-done.18
  91.1 0.6 collective-permute-start.19
  91.6 0.8 copy.21
  92.4 1.0 collective-permute-done.20.refs_1_
  93.4 0.8 collective-permute-done.21.refs_3_
  94.2 1.2 %placed_early.1.refs_2_ = bf16[2048,512]{1,0:T(8,128)(2,1)} custom-call(s32[1]{0:T(128)} %bitcast.pos_ref, bf16[2,128,512]{2,1,0:T(8,128)(2,1)S(1)} %pad_maximum_fusion.2.refs_0_, bf16[2,128,512]{2,1,0:T(8,128)(2,1)S(1)} %collective-permute-done.20.refs_1_, bf16[2,128,512]{2,1,0:T(8,128)(2,1)S(1)} %pad_maximum_fusion.1.refs_2_, ...), custom_call_target="tpu_custom_call" | custom-call | tf_op jit(solution)/shard_map/placed_early/pallas_call | solution.py:578
  95.4 1.9 %collective-permute-done.17.refs_0_ = bf16[2,128,512]{2,1,0:T(8,128)(2,1)S(1)} collective-permute-done((bf16[2,128,512]{2,1,0:T(8,128)(2,1)S(1)}, bf16[2,128,512]{2,1,0:T(8,128)(2,1)S(1)}, u32[]{:S(2)}, u32[]{:S(2)}) %collective-permute-start.17) | collective-permute-done | bytes 262176 | tf_op jit(solution)/shard_map/ppermute | solution.py:617
  97.4 0.1 collective-permute-done.19.refs_1_
  97.5 0.8 placed_late.1
  (25 shorter events, 0.5 us)
Async XLA Ops:
  4.3 11.2 %collective-permute-start.2 = (bf16[544,128]{1,0:T(8,128)(2,1)}, bf16[544,128]{1,0:T(8,128)(2,1)S(1)}, u32[]{:S(2)}, u32[]{:S(2)}) collective-permute-start(bf16[544,128]{1,0:T(8,128)(2,1)} %get-tuple-element.45), channel_id=1, source_target_pairs={{0,12},{4,8},{8,4},{12,0},{16,28},{20,24},{24,20},{28,16},{1,13},{... | collective-permute-start | bytes 417800 | tf_op jit(solution)/shard_map/ppermute | solution.py:617
  8.3 7.1 %collective-permute-start.1 = (bf16[544,128]{1,0:T(8,128)(2,1)}, bf16[544,128]{1,0:T(8,128)(2,1)}, u32[]{:S(2)}, u32[]{:S(2)}) collective-permute-start(bf16[544,128]{1,0:T(8,128)(2,1)} %get-tuple-element.45), channel_id=1, source_target_pairs={{0,8},{4,12},{8,0},{12,4},{16,24},{20,28},{24,16},{28,20},{1,9},{5... | collective-permute-start | bytes 417800 | tf_op jit(solution)/shard_map/ppermute | solution.py:617
  8.8 6.7 %collective-permute-start = (bf16[544,128]{1,0:T(8,128)(2,1)}, bf16[544,128]{1,0:T(8,128)(2,1)}, u32[]{:S(2)}, u32[]{:S(2)}) collective-permute-start(bf16[544,128]{1,0:T(8,128)(2,1)} %get-tuple-element.45), channel_id=1, source_target_pairs={{0,4},{4,0},{8,12},{12,8},{16,20},{20,16},{24,28},{28,24},{1,5},{5... | collective-permute-start | bytes 417800 | tf_op jit(solution)/shard_map/ppermute | solution.py:617
  16.6 8.8 %collective-permute-start.3 = (bf16[544,128]{1,0:T(8,128)(2,1)S(1)}, bf16[544,128]{1,0:T(8,128)(2,1)S(1)}, u32[]{:S(2)}, u32[]{:S(2)}) collective-permute-start(bf16[544,128]{1,0:T(8,128)(2,1)S(1)} %get-tuple-element.61), channel_id=1, source_target_pairs={{0,16},{4,20},{8,24},{12,28},{16,0},{20,4},{24,8},{28,12},{1,17},{... | collective-permute-start | bytes 417800 | tf_op jit(solution)/shard_map/ppermute | solution.py:617
  25.5 9.9 %copy-start.3 = (f32[512]{0:T(512)S(1)}, f32[512]{0:T(512)}, u32[]{:S(2)}) copy-start(f32[512]{0:T(512)} %param.21) | copy-start | bytes 6148
  40.3 8.9 %collective-permute-start.4 = (bf16[2,128,512]{2,1,0:T(8,128)(2,1)S(1)}, bf16[2,128,512]{2,1,0:T(8,128)(2,1)S(1)}, u32[]{:S(2)}, u32[]{:S(2)}) collective-permute-start(bf16[2,128,512]{2,1,0:T(8,128)(2,1)S(1)} %get-tuple-element.66), channel_id=1, source_target_pairs={{0,4},{4,0},{8,12},{12,8},{16,20},{20,16},{24,28},{28,24},{1,5},{5... | collective-permute-start | bytes 786440 | tf_op jit(solution)/shard_map/ppermute | solution.py:617
  42.5 8.3 %collective-permute-start.5 = (bf16[2,128,512]{2,1,0:T(8,128)(2,1)S(1)}, bf16[2,128,512]{2,1,0:T(8,128)(2,1)S(1)}, u32[]{:S(2)}, u32[]{:S(2)}) collective-permute-start(bf16[2,128,512]{2,1,0:T(8,128)(2,1)S(1)} %get-tuple-element.68), channel_id=1, source_target_pairs={{0,8},{4,12},{8,0},{12,4},{16,24},{20,28},{24,16},{28,20},{1,9},{5... | collective-permute-start | bytes 786440 | tf_op jit(solution)/shard_map/ppermute | solution.py:617
  50.9 6.4 %collective-permute-start.6 = (bf16[1,128,512]{2,1,0:T(8,128)(2,1)S(1)}, bf16[1,128,512]{2,1,0:T(8,128)(2,1)S(1)}, u32[]{:S(2)}, u32[]{:S(2)}) collective-permute-start(bf16[1,128,512]{2,1,0:T(8,128)(2,1)S(1)} %slice.77), channel_id=1, source_target_pairs={{0,8},{4,12},{8,0},{12,4},{16,24},{20,28},{24,16},{28,20},{1,9},{5... | collective-permute-start | bytes 393224 | tf_op jit(solution)/shard_map/ppermute | solution.py:617
  51.5 6.4 %collective-permute-start.7 = (bf16[1,128,512]{2,1,0:T(8,128)(2,1)S(1)}, bf16[1,128,512]{2,1,0:T(8,128)(2,1)S(1)}, u32[]{:S(2)}, u32[]{:S(2)}) collective-permute-start(bf16[1,128,512]{2,1,0:T(8,128)(2,1)S(1)} %slice.76), channel_id=1, source_target_pairs={{0,4},{4,0},{8,12},{12,8},{16,20},{20,16},{24,28},{28,24},{1,5},{5... | collective-permute-start | bytes 393224 | tf_op jit(solution)/shard_map/ppermute | solution.py:617
  51.9 12.8 %collective-permute-start.8 = (bf16[2,128,512]{2,1,0:T(8,128)(2,1)S(1)}, bf16[2,128,512]{2,1,0:T(8,128)(2,1)S(1)}, u32[]{:S(2)}, u32[]{:S(2)}) collective-permute-start(bf16[2,128,512]{2,1,0:T(8,128)(2,1)S(1)} %get-tuple-element.77), channel_id=1, source_target_pairs={{0,4},{4,0},{8,12},{12,8},{16,20},{20,16},{24,28},{28,24},{1,5},{5... | collective-permute-start | bytes 786440 | tf_op jit(solution)/shard_map/ppermute | solution.py:617
  53.5 13.0 %collective-permute-start.10 = (bf16[2,128,512]{2,1,0:T(8,128)(2,1)S(1)}, bf16[2,128,512]{2,1,0:T(8,128)(2,1)S(1)}, u32[]{:S(2)}, u32[]{:S(2)}) collective-permute-start(bf16[2,128,512]{2,1,0:T(8,128)(2,1)S(1)} %get-tuple-element.79), channel_id=1, source_target_pairs={{0,8},{4,12},{8,0},{12,4},{16,24},{20,28},{24,16},{28,20},{1,9},{5... | collective-permute-start | bytes 786440 | tf_op jit(solution)/shard_map/ppermute | solution.py:617
  58.0 13.8 %collective-permute-start.12 = (bf16[1,256,512]{2,1,0:T(8,128)(2,1)S(1)}, bf16[1,256,512]{2,1,0:T(8,128)(2,1)S(1)}, u32[]{:S(2)}, u32[]{:S(2)}) collective-permute-start(bf16[1,256,512]{2,1,0:T(8,128)(2,1)S(1)} %pad_maximum_fusion), channel_id=1, source_target_pairs={{0,16},{4,20},{8,24},{12,28},{16,0},{20,4},{24,8},{28,12},{1,17},{... | collective-permute-start | bytes 786440 | tf_op jit(solution)/shard_map/ppermute | solution.py:617
  64.8 7.0 %copy-start = (f32[256,512]{1,0:T(8,128)S(1)}, f32[256,512]{1,0:T(8,128)}, u32[]{:S(2)}) copy-start(f32[256,512]{1,0:T(8,128)} %master_ref.1) | copy-start | bytes 1572868
  64.8 7.0 %copy-start.1 = (f32[256,512]{1,0:T(8,128)S(1)}, f32[256,512]{1,0:T(8,128)}, u32[]{:S(2)}) copy-start(f32[256,512]{1,0:T(8,128)} %one_ref.1) | copy-start | bytes 1572868
  64.8 7.0 %copy-start.2 = (f32[256,512]{1,0:T(8,128)S(1)}, f32[256,512]{1,0:T(8,128)}, u32[]{:S(2)}) copy-start(f32[256,512]{1,0:T(8,128)} %two_ref.1) | copy-start | bytes 1572868
  64.9 5.4 %collective-permute-start.9 = (bf16[1,128,512]{2,1,0:T(8,128)(2,1)S(1)}, bf16[1,128,512]{2,1,0:T(8,128)(2,1)S(1)}, u32[]{:S(2)}, u32[]{:S(2)}) collective-permute-start(bf16[1,128,512]{2,1,0:T(8,128)(2,1)S(1)} %slice.75), channel_id=1, source_target_pairs={{0,8},{4,12},{8,0},{12,4},{16,24},{20,28},{24,16},{28,20},{1,9},{5... | collective-permute-start | bytes 393224 | tf_op jit(solution)/shard_map/ppermute | solution.py:617
  66.7 5.0 %collective-permute-start.11 = (bf16[1,128,512]{2,1,0:T(8,128)(2,1)S(1)}, bf16[1,128,512]{2,1,0:T(8,128)(2,1)S(1)}, u32[]{:S(2)}, u32[]{:S(2)}) collective-permute-start(bf16[1,128,512]{2,1,0:T(8,128)(2,1)S(1)} %slice.74), channel_id=1, source_target_pairs={{0,4},{4,0},{8,12},{12,8},{16,20},{20,16},{24,28},{28,24},{1,5},{5... | collective-permute-start | bytes 393224 | tf_op jit(solution)/shard_map/ppermute | solution.py:617
  72.4 6.2 %collective-permute-start.15 = (bf16[1,128,512]{2,1,0:T(8,128)(2,1)S(1)}, bf16[1,128,512]{2,1,0:T(8,128)(2,1)S(1)}, u32[]{:S(2)}, u32[]{:S(2)}) collective-permute-start(bf16[1,128,512]{2,1,0:T(8,128)(2,1)S(1)} %get-tuple-element.89), channel_id=1, source_target_pairs={{0,8},{4,12},{8,0},{12,4},{16,24},{20,28},{24,16},{28,20},{1,9},{5... | collective-permute-start | bytes 393224 | tf_op jit(solution)/shard_map/ppermute | solution.py:617
  72.9 11.6 %collective-permute-start.13 = (bf16[1,256,512]{2,1,0:T(8,128)(2,1)S(1)}, bf16[1,256,512]{2,1,0:T(8,128)(2,1)S(1)}, u32[]{:S(2)}, u32[]{:S(2)}) collective-permute-start(bf16[1,256,512]{2,1,0:T(8,128)(2,1)S(1)} %bitcast.21), channel_id=1, source_target_pairs={{0,16},{4,20},{8,24},{12,28},{16,0},{20,4},{24,8},{28,12},{1,17},{... | collective-permute-start | bytes 786440 | tf_op jit(solution)/shard_map/ppermute | solution.py:617
  77.2 6.3 %collective-permute-start.14 = (bf16[1,128,512]{2,1,0:T(8,128)(2,1)S(1)}, bf16[1,128,512]{2,1,0:T(8,128)(2,1)S(1)}, u32[]{:S(2)}, u32[]{:S(2)}) collective-permute-start(bf16[1,128,512]{2,1,0:T(8,128)(2,1)S(1)} %get-tuple-element.90), channel_id=1, source_target_pairs={{0,4},{4,0},{8,12},{12,8},{16,20},{20,16},{24,28},{28,24},{1,5},{5... | collective-permute-start | bytes 393224 | tf_op jit(solution)/shard_map/ppermute | solution.py:617
  84.5 6.4 %collective-permute-start.16 = (bf16[1,128,512]{2,1,0:T(8,128)(2,1)S(1)}, bf16[1,128,512]{2,1,0:T(8,128)(2,1)S(1)}, u32[]{:S(2)}, u32[]{:S(2)}) collective-permute-start(bf16[1,128,512]{2,1,0:T(8,128)(2,1)S(1)} %get-tuple-element.88), channel_id=1, source_target_pairs={{0,8},{4,12},{8,0},{12,4},{16,24},{20,28},{24,16},{28,20},{1,9},{5... | collective-permute-start | bytes 393224 | tf_op jit(solution)/shard_map/ppermute | solution.py:617
  84.6 6.5 %collective-permute-start.18 = (bf16[1,128,512]{2,1,0:T(8,128)(2,1)S(1)}, bf16[1,128,512]{2,1,0:T(8,128)(2,1)S(1)}, u32[]{:S(2)}, u32[]{:S(2)}) collective-permute-start(bf16[1,128,512]{2,1,0:T(8,128)(2,1)S(1)} %get-tuple-element.87), channel_id=1, source_target_pairs={{0,4},{4,0},{8,12},{12,8},{16,20},{20,16},{24,28},{28,24},{1,5},{5... | collective-permute-start | bytes 393224 | tf_op jit(solution)/shard_map/ppermute | solution.py:617
  84.6 8.8 %collective-permute-start.20 = (bf16[2,128,512]{2,1,0:T(8,128)(2,1)S(1)}, bf16[2,128,512]{2,1,0:T(8,128)(2,1)S(1)}, u32[]{:S(2)}, u32[]{:S(2)}) collective-permute-start(bf16[2,128,512]{2,1,0:T(8,128)(2,1)S(1)} %pad_maximum_fusion.2.refs_0_), channel_id=1, source_target_pairs={{0,4},{4,0},{8,12},{12,8},{16,20},{20,16},{24,28},{28,24},{1,5},{5... | collective-permute-start | bytes 786440 | tf_op jit(solution)/shard_map/ppermute | solution.py:617
  86.6 7.6 %collective-permute-start.21 = (bf16[2,128,512]{2,1,0:T(8,128)(2,1)S(1)}, bf16[2,128,512]{2,1,0:T(8,128)(2,1)S(1)}, u32[]{:S(2)}, u32[]{:S(2)}) collective-permute-start(bf16[2,128,512]{2,1,0:T(8,128)(2,1)S(1)} %pad_maximum_fusion.1.refs_2_), channel_id=1, source_target_pairs={{0,8},{4,12},{8,0},{12,4},{16,24},{20,28},{24,16},{28,20},{1,9},{5... | collective-permute-start | bytes 786440 | tf_op jit(solution)/shard_map/ppermute | solution.py:617
  90.9 6.4 %collective-permute-start.17 = (bf16[2,128,512]{2,1,0:T(8,128)(2,1)S(1)}, bf16[2,128,512]{2,1,0:T(8,128)(2,1)S(1)}, u32[]{:S(2)}, u32[]{:S(2)}) collective-permute-start(bf16[2,128,512]{2,1,0:T(8,128)(2,1)S(1)} %pad_maximum_fusion.3.refs_4_), channel_id=1, source_target_pairs={{0,4},{4,0},{8,12},{12,8},{16,20},{20,16},{24,28},{28,24},{1,5},{5... | collective-permute-start | bytes 786440 | tf_op jit(solution)/shard_map/ppermute | solution.py:617
  91.1 6.4 %collective-permute-start.19 = (bf16[2,128,512]{2,1,0:T(8,128)(2,1)S(1)}, bf16[2,128,512]{2,1,0:T(8,128)(2,1)S(1)}, u32[]{:S(2)}, u32[]{:S(2)}) collective-permute-start(bf16[2,128,512]{2,1,0:T(8,128)(2,1)S(1)} %pad_maximum_fusion.4.refs_5_), channel_id=1, source_target_pairs={{0,8},{4,12},{8,0},{12,4},{16,24},{20,28},{24,16},{28,20},{1,9},{5... | collective-permute-start | bytes 786440 | tf_op jit(solution)/shard_map/ppermute | solution.py:617
